TPU v7x, 32 devices: a whole 2x2x4 slice. The times are simulated.
32 devices in a mesh: seq: 4 (over y, core), dp: 8 (over z, x).
Axes of the slice: x: 2, y: 2, z: 4, core: 2. Of those that a mesh axis runs over, the one named last changes fastest.
Arguments:
- tokens: bfloat16 [8, 768, 2048], P('dp', 'seq'), may hold values from -6 to 6
- doc_lengths: int32 [8, 4], P('dp'), may hold values from 1 to 696, as said below
- w_in: bfloat16 [2048, 2048], P(('seq', 'dp')), may hold values from -0.125 to 0.125
- w_forget: bfloat16 [2048, 2048], P(('seq', 'dp')), may hold values from -0.125 to 0.125
- w_gate_out: bfloat16 [2048, 2048], P(('seq', 'dp')), may hold values from -0.125 to 0.125
- w_out: bfloat16 [2048, 2048], P(('seq', 'dp')), may hold values from -0.125 to 0.125
- w_gate: bfloat16 [2048, 5632], P(('seq', 'dp')), may hold values from -0.125 to 0.125
- w_up: bfloat16 [2048, 5632], P(('seq', 'dp')), may hold values from -0.125 to 0.125
- w_down: bfloat16 [2048, 5632], P(('seq', 'dp')), may hold values from -0.078125 to 0.078125
- g_mix: bfloat16 [2048], P(('seq', 'dp')), may hold values from 0.5 to 1.5
- g_out: bfloat16 [2048], P(('seq', 'dp')), may hold values from 0.5 to 1.5
- g_ffn: bfloat16 [2048], P(('seq', 'dp')), may hold values from 0.5 to 1.5
- floor_logit: bfloat16 [2048], P(('seq', 'dp')), may hold values from -2 to 9
- cotangent: bfloat16 [8, 768, 2048], P('dp', 'seq'), may hold values from -6 to 6
Outputs:
- output: bfloat16 [8, 768, 2048], P('dp', 'seq')
- grad_tokens: bfloat16 [8, 768, 2048], P('dp', 'seq')
- grad_w_in: float32 [2048, 2048], P(('seq', 'dp'))
- grad_w_forget: float32 [2048, 2048], P(('seq', 'dp'))
- grad_w_gate_out: float32 [2048, 2048], P(('seq', 'dp'))
- grad_w_out: float32 [2048, 2048], P(('seq', 'dp'))
- grad_w_gate: float32 [2048, 5632], P(('seq', 'dp'))
- grad_w_up: float32 [2048, 5632], P(('seq', 'dp'))
- grad_w_down: float32 [2048, 5632], P(('seq', 'dp'))
- grad_g_mix: float32 [2048], P(('seq', 'dp'))
- grad_g_out: float32 [2048], P(('seq', 'dp'))
- grad_g_ffn: float32 [2048], P(('seq', 'dp'))
- grad_floor_logit: float32 [2048], P(('seq', 'dp'))
Inputs may be any that keep to these rules, and one draw needn't show every extreme that they name: `doc_lengths`: in each bucket the 4 lengths sum to at most 768; one document, at a place drawn from the seed, starts in the rows of the bucket's first device and ends in those of its last; rows past the sum are padding.
All inputs are finite; a program needn't handle non-finite values.
Results may differ from a plain program's by a relative error of at most 0.01.
Values may be sent and summed in bfloat16 or wider, within the bound.
No kernel may reach another device: no remote copies, remote signals or barrier semaphores. Data moves between devices by JAX's collectives and lax.ppermute only.
A program may use at most 448 MiB of HBM per device.

v0:
```python
import jax
import jax.numpy as jnp
from jax import lax
from jax.sharding import PartitionSpec as P

EPSILON = 1e-06


def product(left_op, right_op):
    return jnp.dot(left_op, right_op, preferred_element_type=jnp.float32)


def product_nt(left_op, right_op):
    return lax.dot_general(
        left_op, right_op, (((1,), (1,)), ((), ())), preferred_element_type=jnp.float32
    )


def product_tn(left_op, right_op):
    return lax.dot_general(
        left_op, right_op, (((0,), (0,)), ((), ())), preferred_element_type=jnp.float32
    )


def linear_combine(first_op, second_op):
    return (first_op[0] * second_op[0], second_op[0] * first_op[1] + second_op[1])


def row_flags(lengths, row_count):
    doc_ends = jnp.cumsum(lengths)
    positions = jnp.arange(row_count, dtype=jnp.int32)
    starts_hit = jnp.any(positions[:, None] == doc_ends[None, :-1], axis=1)
    resets = jnp.logical_or(positions == 0, starts_hit)
    live_rows = positions < doc_ends[-1]
    return (resets.astype(jnp.float32)[:, None], live_rows.astype(jnp.float32)[:, None])


def norm_forward(values):
    inverse = lax.rsqrt(jnp.mean(values * values, axis=-1, keepdims=True) + EPSILON)
    return (values * inverse, inverse)


def norm_backward(grad_in, normed, inverse, gains):
    grad_gain = jnp.sum(grad_in * normed, axis=0)
    grad_normed = grad_in * gains
    grad_values = inverse * (
        grad_normed - normed * jnp.mean(grad_normed * normed, axis=-1, keepdims=True)
    )
    return (grad_values, grad_gain)


def silu_slope(values):
    sig_values = jax.nn.sigmoid(values)
    return sig_values * (1.0 + values * (1.0 - sig_values))


def gates_from(input_low, forget_low, floors, resets, live_rows):
    forget_pre = forget_low.astype(jnp.float32)
    sig_forget = jax.nn.sigmoid(forget_pre)
    forget = (floors + (1.0 - floors) * sig_forget) * (1.0 - resets)
    drive = jax.nn.silu(input_low.astype(jnp.float32)) * live_rows
    return (forget, drive, sig_forget)


def recurrence_tail(
    grad_state,
    decay_prod,
    state_part,
    incoming,
    forget,
    drive,
    state_prev,
    sig_forget,
    input_low,
    floors,
    resets,
    live_rows,
):
    carried = state_part + decay_prod * incoming
    carried_next = jnp.concatenate([carried[1:], incoming[None, :]], axis=0)
    grad_total = grad_state + carried_next
    grad_forget = grad_total * (state_prev - drive) * (1.0 - resets)
    grad_drive = grad_total * (1.0 - forget) * live_rows
    grad_forget_pre = grad_forget * (1.0 - floors) * sig_forget * (1.0 - sig_forget)
    grad_floor = jnp.sum(grad_forget * (1.0 - sig_forget), axis=0)
    grad_input_pre = grad_drive * silu_slope(input_low.astype(jnp.float32))
    return (grad_input_pre, grad_forget_pre, grad_floor)


def on_device(
    tokens,
    doc_lengths,
    w_in,
    w_forget,
    w_gate_out,
    w_out,
    w_gate,
    w_up,
    w_down,
    g_mix,
    g_out,
    g_ffn,
    floor_logit,
    cotangent,
):
    full_in, full_forget, full_gate_out, full_out, gain_mix, gain_out, floor_raw = (
        lax.all_gather(w_in, ("seq", "dp"), axis=0, tiled=True),
        lax.all_gather(w_forget, ("seq", "dp"), axis=0, tiled=True),
        lax.all_gather(w_gate_out, ("seq", "dp"), axis=0, tiled=True),
        lax.all_gather(w_out, ("seq", "dp"), axis=0, tiled=True),
        lax.all_gather(g_mix, ("seq", "dp"), axis=0, tiled=True),
        lax.all_gather(g_out, ("seq", "dp"), axis=0, tiled=True),
        lax.all_gather(floor_logit, ("seq", "dp"), axis=0, tiled=True),
    )
    gain_mix = gain_mix.astype(jnp.float32)
    gain_out = gain_out.astype(jnp.float32)
    floors = jax.nn.sigmoid(floor_raw.astype(jnp.float32))
    row_count = tokens.shape[1]
    model_width = tokens.shape[2]
    seq_parts = lax.axis_size("seq")
    seq_place = lax.axis_index("seq")
    lengths = doc_lengths[0]
    inputs = tokens[0].astype(jnp.float32)
    normed_in, inverse_in = norm_forward(inputs)
    mixed_in = (normed_in * gain_mix).astype(jnp.bfloat16)
    input_low = product(mixed_in, full_in).astype(jnp.bfloat16)
    forget_low = product(mixed_in, full_forget).astype(jnp.bfloat16)
    gate_out_pre = product(mixed_in, full_gate_out)
    slab_width = model_width // seq_parts
    input_cols, forget_cols = (
        lax.all_to_all(input_low, "seq", split_axis=1, concat_axis=0, tiled=True),
        lax.all_to_all(forget_low, "seq", split_axis=1, concat_axis=0, tiled=True),
    )
    floor_cols = lax.dynamic_slice_in_dim(floors, seq_place * slab_width, slab_width)
    resets, live_rows = row_flags(lengths, row_count * seq_parts)
    forget, drive, sig_forget = gates_from(input_cols, forget_cols, floor_cols, resets, live_rows)
    _, hidden_states = lax.associative_scan(
        linear_combine, (forget, (1.0 - forget) * drive), axis=0
    )
    state_prev = jnp.concatenate([jnp.zeros_like(hidden_states[:1]), hidden_states[:-1]], axis=0)
    states = lax.all_to_all(
        hidden_states.astype(jnp.bfloat16), "seq", split_axis=0, concat_axis=1, tiled=True
    )
    normed_h, inverse_h = norm_forward(states.astype(jnp.float32))
    silu_gate_out = jax.nn.silu(gate_out_pre)
    scaled_h = normed_h * gain_out
    branch_in = (scaled_h * silu_gate_out).astype(jnp.bfloat16)
    residual = inputs + product(branch_in, full_out)
    full_gate, full_up, full_down, gain_ffn = (
        lax.all_gather(w_gate, ("seq", "dp"), axis=0, tiled=True),
        lax.all_gather(w_up, ("seq", "dp"), axis=0, tiled=True),
        lax.all_gather(w_down, ("seq", "dp"), axis=0, tiled=True),
        lax.all_gather(g_ffn, ("seq", "dp"), axis=0, tiled=True),
    )
    gain_ffn = gain_ffn.astype(jnp.float32)
    normed_z, inverse_z = norm_forward(residual)
    ffn_in = (normed_z * gain_ffn).astype(jnp.bfloat16)
    gate_pre = product(ffn_in, full_gate)
    up_pre = product(ffn_in, full_up)
    silu_gate = jax.nn.silu(gate_pre)
    middle = (silu_gate * up_pre).astype(jnp.bfloat16)
    output = residual + product_nt(middle, full_down)
    grad_out = cotangent[0]
    grad_middle = product(grad_out, full_down)
    grad_gate_low = (grad_middle * up_pre * silu_slope(gate_pre)).astype(jnp.bfloat16)
    grad_up_low = (grad_middle * silu_gate).astype(jnp.bfloat16)
    grad_ffn_in = product_nt(grad_gate_low, full_gate) + product_nt(grad_up_low, full_up)
    grad_z_norm, grad_g_ffn = norm_backward(grad_ffn_in, normed_z, inverse_z, gain_ffn)
    grad_residual = grad_out.astype(jnp.float32) + grad_z_norm
    grad_w_down = product_tn(grad_out, middle)
    grad_w_gate = product_tn(ffn_in, grad_gate_low)
    grad_w_up = product_tn(ffn_in, grad_up_low)
    mlp_shares = (
        lax.psum_scatter(grad_w_gate, ("seq", "dp"), scatter_dimension=0, tiled=True),
        lax.psum_scatter(grad_w_up, ("seq", "dp"), scatter_dimension=0, tiled=True),
        lax.psum_scatter(grad_w_down, ("seq", "dp"), scatter_dimension=0, tiled=True),
        lax.psum_scatter(grad_g_ffn, ("seq", "dp"), scatter_dimension=0, tiled=True),
    )
    grad_branch_low = grad_residual.astype(jnp.bfloat16)
    grad_w_out = product_tn(branch_in, grad_branch_low)
    grad_branch_in = product_nt(grad_branch_low, full_out)
    grad_gate_out_low = (grad_branch_in * scaled_h * silu_slope(gate_out_pre)).astype(jnp.bfloat16)
    grad_h_norm, grad_g_out = norm_backward(
        grad_branch_in * silu_gate_out, normed_h, inverse_h, gain_out
    )
    grad_hidden = grad_h_norm.astype(jnp.bfloat16)
    grad_state = lax.all_to_all(grad_hidden, "seq", split_axis=1, concat_axis=0, tiled=True).astype(
        jnp.float32
    )
    decay_back, state_back = lax.associative_scan(
        linear_combine, (forget, forget * grad_state), reverse=True, axis=0
    )
    incoming = jnp.zeros((slab_width,), jnp.float32)
    grad_input_pre, grad_forget_pre, floor_part = recurrence_tail(
        grad_state,
        decay_back,
        state_back,
        incoming,
        forget,
        drive,
        state_prev,
        sig_forget,
        input_cols,
        floor_cols,
        resets,
        live_rows,
    )
    grad_input_low, grad_forget_low = (
        lax.all_to_all(
            grad_input_pre.astype(jnp.bfloat16), "seq", split_axis=0, concat_axis=1, tiled=True
        ),
        lax.all_to_all(
            grad_forget_pre.astype(jnp.bfloat16), "seq", split_axis=0, concat_axis=1, tiled=True
        ),
    )
    grad_floor = lax.dynamic_update_slice_in_dim(
        jnp.zeros((model_width,), jnp.float32), floor_part, seq_place * slab_width, 0
    )
    grad_floor_logit = grad_floor * floors * (1.0 - floors)
    grad_mixed_in = (
        product_nt(grad_input_low, full_in)
        + product_nt(grad_forget_low, full_forget)
        + product_nt(grad_gate_out_low, full_gate_out)
    )
    grad_x_norm, grad_g_mix = norm_backward(grad_mixed_in, normed_in, inverse_in, gain_mix)
    grad_tokens = grad_residual + grad_x_norm
    grad_w_in = product_tn(mixed_in, grad_input_low)
    grad_w_forget = product_tn(mixed_in, grad_forget_low)
    grad_w_gate_out = product_tn(mixed_in, grad_gate_out_low)
    mixer_shares = (
        lax.psum_scatter(grad_w_in, ("seq", "dp"), scatter_dimension=0, tiled=True),
        lax.psum_scatter(grad_w_forget, ("seq", "dp"), scatter_dimension=0, tiled=True),
        lax.psum_scatter(grad_w_gate_out, ("seq", "dp"), scatter_dimension=0, tiled=True),
        lax.psum_scatter(grad_w_out, ("seq", "dp"), scatter_dimension=0, tiled=True),
        lax.psum_scatter(grad_g_mix, ("seq", "dp"), scatter_dimension=0, tiled=True),
        lax.psum_scatter(grad_g_out, ("seq", "dp"), scatter_dimension=0, tiled=True),
        lax.psum_scatter(grad_floor_logit, ("seq", "dp"), scatter_dimension=0, tiled=True),
    )
    return (
        output[None].astype(jnp.bfloat16),
        grad_tokens[None].astype(jnp.bfloat16),
        mixer_shares[0],
        mixer_shares[1],
        mixer_shares[2],
        mixer_shares[3],
        mlp_shares[0],
        mlp_shares[1],
        mlp_shares[2],
        mixer_shares[4],
        mixer_shares[5],
        mlp_shares[3],
        mixer_shares[6],
    )


def solution(mesh):
    return jax.shard_map(
        on_device,
        mesh=mesh,
        in_specs=(
            P("dp", "seq", None),
            P("dp", None),
            P(("seq", "dp"), None),
            P(("seq", "dp"), None),
            P(("seq", "dp"), None),
            P(("seq", "dp"), None),
            P(("seq", "dp"), None),
            P(("seq", "dp"), None),
            P(("seq", "dp"), None),
            P(("seq", "dp")),
            P(("seq", "dp")),
            P(("seq", "dp")),
            P(("seq", "dp")),
            P("dp", "seq", None),
        ),
        out_specs=(
            P("dp", "seq", None),
            P("dp", "seq", None),
            P(("seq", "dp"), None),
            P(("seq", "dp"), None),
            P(("seq", "dp"), None),
            P(("seq", "dp"), None),
            P(("seq", "dp"), None),
            P(("seq", "dp"), None),
            P(("seq", "dp"), None),
            P(("seq", "dp")),
            P(("seq", "dp")),
            P(("seq", "dp")),
            P(("seq", "dp")),
        ),
        check_vma=False,
    )
```

profile of v0, /device:TPU:16, one launch (start us, length us, event | category | flops | bytes accessed | tf_op | source)
XLA Modules:
  0.0 5177.8 jit_solution(12178746995672434585)
XLA Ops:
  13.7 40.8 all-reduce.65
  55.5 33.6 all-gather.8.cloned.1.call-done
  89.1 5.2 convolution_convert_fusion.1
  98.8 70.9 %all-gather.10.cloned.1.call-done = bf16[2048,2048]{1,0:T(8,128)(2,1)} async-done(((bf16[64,2048]{1,0:T(8,128)(2,1)}), bf16[2048,2048]{1,0:T(8,128)(2,1)}) %all-gather.10.cloned.1.call-update) | async-done | bytes 8388624 | tf_op jit(solution)/shard_map/all_gather | solution.py:107
  169.7 5.2 convolution_convert_fusion
  181.2 11.8 all-to-all-done.1
  200.9 4.9 slice.579
  251.9 5.2 pad.184
  269.0 11.5 all-to-all-done.2
  282.4 7.0 multiply_convert_fusion.6
  289.4 39.7 all-gather.14.cloned.1.call-done
  329.1 5.3 multiply_reduce_fusion.5
  335.8 138.9 %all-gather.18.cloned.1.call-done = bf16[2048,5632]{1,0:T(8,128)(2,1)} async-done(((bf16[64,5632]{1,0:T(8,128)(2,1)}), bf16[2048,5632]{1,0:T(8,128)(2,1)}) %all-gather.18.cloned.1.call-update) | async-done | bytes 23068688 | tf_op jit(solution)/shard_map/all_gather | solution.py:151
  474.7 12.2 fusion.96
  486.9 133.3 %all-gather.16.cloned.1.call-done = bf16[2048,5632]{1,0:T(8,128)(2,1)} async-done(((bf16[64,5632]{1,0:T(8,128)(2,1)}), bf16[2048,5632]{1,0:T(8,128)(2,1)}) %all-gather.16.cloned.1.call-update) | async-done | bytes 23068688 | tf_op jit(solution)/shard_map/all_gather | solution.py:150
  620.3 12.0 fusion.95
  632.2 133.8 %all-gather.20.cloned.1.call-done = bf16[2048,5632]{1,0:T(8,128)(2,1)} async-done(((bf16[64,5632]{1,0:T(8,128)(2,1)}), bf16[2048,5632]{1,0:T(8,128)(2,1)}) %all-gather.20.cloned.1.call-update) | async-done | bytes 23068688 | tf_op jit(solution)/shard_map/all_gather | solution.py:152
  766.0 14.7 multiply_convert_fusion
  780.7 14.0 fusion.97
  794.7 15.4 multiply_reduce_fusion.1
  813.7 8.2 fusion.42
  821.9 8.7 multiply_reduce_fusion.2
  832.7 8.2 fusion.72
  846.4 7.0 slice.589
  877.6 4.9 slice.584
  882.5 6.8 slice.585
  977.8 5.1 pad.201
  983.9 5.2 pad.219
  995.7 12.8 rev.9
  1015.1 12.8 rev.8
  1034.9 14.8 all_to_all.90
  1049.7 8.3 fusion.47
  1058.1 14.1 all_to_all.91
  1072.2 8.3 fusion.49
  1081.6 19.7 convolution_bitcast_fusion
  1101.3 42.5 copy.49
  1144.9 19.7 fusion.100
  1164.7 19.9 fusion.99
  1184.6 14.0 fusion.2
  1198.9 6.4 fusion.98
  1205.4 6.5 convolution_add_fusion.1
  1216.2 49.7 all-reduce.64
  1271.0 269.1 %reduce-scatter.14.cloned.1.call-done = f32[64,2048]{1,0:T(8,128)} async-done(((f32[2048,2048]{1,0:T(8,128)}), f32[64,2048]{1,0:T(8,128)}) %reduce-scatter.14.cloned.1.call-update) | async-done | bytes 524304 | tf_op jit(solution)/shard_map/reduce_scatter | solution.py:233
  1540.1 360.1 %reduce-scatter.12.cloned.1.call-done = f32[64,2048]{1,0:T(8,128)} async-done(((f32[2048,2048]{1,0:T(8,128)}), f32[64,2048]{1,0:T(8,128)}) %reduce-scatter.12.cloned.1.call-update) | async-done | bytes 524304 | tf_op jit(solution)/shard_map/reduce_scatter | solution.py:232
  1900.1 360.2 %reduce-scatter.10.cloned.1.call-done = f32[64,2048]{1,0:T(8,128)} async-done(((f32[2048,2048]{1,0:T(8,128)}), f32[64,2048]{1,0:T(8,128)}) %reduce-scatter.10.cloned.1.call-update) | async-done | bytes 524304 | tf_op jit(solution)/shard_map/reduce_scatter | solution.py:231
  2260.4 970.1 %reduce-scatter.22.cloned.1.call-done = f32[64,5632]{1,0:T(8,128)} async-done(((f32[2048,5632]{1,0:T(8,128)}), f32[64,5632]{1,0:T(8,128)}) %reduce-scatter.22.cloned.1.call-update) | async-done | bytes 1441808
  3230.5 970.2 %reduce-scatter.20.cloned.1.call-done = f32[64,5632]{1,0:T(8,128)} async-done(((f32[2048,5632]{1,0:T(8,128)}), f32[64,5632]{1,0:T(8,128)}) %reduce-scatter.20.cloned.1.call-update) | async-done | bytes 1441808 | tf_op jit(solution)/shard_map/reduce_scatter | solution.py:175
  4200.7 970.1 %reduce-scatter.18.cloned.1.call-done = f32[64,5632]{1,0:T(8,128)} async-done(((f32[2048,5632]{1,0:T(8,128)}), f32[64,5632]{1,0:T(8,128)}) %reduce-scatter.18.cloned.1.call-update) | async-done | bytes 1441808 | tf_op jit(solution)/shard_map/reduce_scatter | solution.py:174
  (488 shorter events, 243.2 us)
Async XLA Ops:
  7.2 5.5 copy-start.66
  7.2 5.8 copy-start.67
  7.2 6.0 copy-start.68
  7.2 6.2 copy-start.69
  7.2 81.8 %all-gather.8.cloned.1.call-start = ((), (), s32[]{:S(2)}) async-start(), calls=%async_computation.13 | async-start | bytes 8650752 | tf_op jit(solution)/shard_map/all_gather | solution.py:108
  8.0 47.3 copy-start
  8.0 161.7 %all-gather.10.cloned.1.call-start = ((), (), s32[]{:S(2)}) async-start(), calls=%async_computation.14 | async-start | bytes 8650752 | tf_op jit(solution)/shard_map/all_gather | solution.py:107
  8.7 273.6 %all-gather.12.cloned.1.call-start = ((), (), s32[]{:S(2)}) async-start(), calls=%async_computation.15 | async-start | bytes 8650752 | tf_op jit(solution)/shard_map/all_gather | solution.py:109
  9.5 319.7 %all-gather.14.cloned.1.call-start = ((), (), s32[]{:S(2)}) async-start(), calls=%async_computation.16 | async-start | bytes 8650752 | tf_op jit(solution)/shard_map/all_gather | solution.py:110
  10.0 464.7 %all-gather.18.cloned.1.call-start = ((), (), s32[]{:S(2)}) async-start(), calls=%async_computation.18 | async-start | bytes 23789568 | tf_op jit(solution)/shard_map/all_gather | solution.py:151
  10.6 609.7 %all-gather.16.cloned.1.call-start = ((), (), s32[]{:S(2)}) async-start(), calls=%async_computation.17 | async-start | bytes 23789568 | tf_op jit(solution)/shard_map/all_gather | solution.py:150
  11.2 754.8 %all-gather.20.cloned.1.call-start = ((), (), s32[]{:S(2)}) async-start(), calls=%async_computation.19 | async-start | bytes 23789568 | tf_op jit(solution)/shard_map/all_gather | solution.py:152
  54.5 39.8 copy-start.51
  55.1 137.9 %copy-start.47 = (f32[768]{0:T(1024)}, f32[768]{0:T(1024)S(1)}, u32[]{:S(2)}) copy-start(f32[768]{0:T(1024)S(1)} %fusion.71) | copy-start | bytes 9220
  95.3 80.6 %all-to-all-start = ((bf16[192,4,512]{2,0,1:T(8,128)(2,1)}), bf16[192,4,512]{2,0,1:T(8,128)(2,1)S(1)}, u32[]{:S(2)}, u32[]{:S(2)}) async-start(bf16[192,4,512]{2,0,1:T(8,128)(2,1)} %bitcast.179), calls=%async_computation | async-start | bytes 1572864 | tf_op jit(solution)/shard_map/all_to_all | solution.py:132
  175.8 17.1 all-to-all-start.1
  179.6 16.9 copy-start.49
  179.6 16.9 copy-start.45
  197.3 18.2 copy-start.9
  218.6 8.6 copy-start.19
  265.3 15.3 all-to-all-start.2
  268.9 1002.0 %reduce-scatter.16.cloned.1.call-start = ((), (), s32[]{:S(2)}) async-start(), calls=%async_computation.23 | async-start | bytes 17301504 | tf_op jit(solution)/shard_map/reduce_scatter | solution.py:234
  289.4 45.0 copy-start.37
  335.8 284.5 %copy-start.5 = (bf16[192,2048]{1,0:T(8,128)(2,1)}, bf16[192,2048]{1,0:T(8,128)(2,1)S(1)}, u32[]{:S(2)}) copy-start(bf16[192,2048]{1,0:T(8,128)(2,1)S(1)} %multiply_convert_fusion.5) | copy-start | bytes 2359300
  780.7 14.0 copy-start.30
  794.7 15.4 copy-start.22
  821.9 718.2 %reduce-scatter.14.cloned.1.call-start = ((), (), s32[]{:S(2)}) async-start(), calls=%async_computation.22 | async-start | bytes 17301504 | tf_op jit(solution)/shard_map/reduce_scatter | solution.py:233
  821.9 8.7 copy-start.17
  821.9 8.7 copy-start.34
  842.0 11.4 copy-start.10
  842.0 23.6 all-to-all-start.3
  846.3 1053.8 %reduce-scatter.12.cloned.1.call-start = ((), (), s32[]{:S(2)}) async-start(), calls=%async_computation.21 | async-start | bytes 17301504 | tf_op jit(solution)/shard_map/reduce_scatter | solution.py:232
  919.3 16.5 copy-start.27
  935.8 8.9 copy-start.44
  963.6 5.7 copy-start.35
  977.8 5.1 copy-start.26
  983.9 5.2 copy-start.29
  995.7 12.8 copy-start.28
  1058.0 1202.4 %reduce-scatter.10.cloned.1.call-start = ((), (), s32[]{:S(2)}) async-start(), calls=%async_computation.20 | async-start | bytes 17301504 | tf_op jit(solution)/shard_map/reduce_scatter | solution.py:231
  1080.5 2150.0 %reduce-scatter.22.cloned.1.call-start = ((), (), s32[]{:S(2)}) async-start(), calls=%async_computation.26 | async-start | bytes 47579136
  1143.8 3056.9 %reduce-scatter.20.cloned.1.call-start = ((), (), s32[]{:S(2)}) async-start(), calls=%async_computation.25 | async-start | bytes 47579136 | tf_op jit(solution)/shard_map/reduce_scatter | solution.py:175
  1164.6 4006.2 %reduce-scatter.18.cloned.1.call-start = ((), (), s32[]{:S(2)}) async-start(), calls=%async_computation.24 | async-start | bytes 47579136 | tf_op jit(solution)/shard_map/reduce_scatter | solution.py:174
  1184.6 14.1 copy-start.57
  1184.6 14.3 copy-start.52
  1198.9 13.0 slice-start
  1205.4 6.5 slice-start.1
  1205.4 6.5 copy-start.12
  1211.9 56.3 %copy-start.3 = (f32[192,2048]{1,0:T(8,128)S(1)}, f32[192,2048]{1,0:T(8,128)}, u32[]{:S(2)}) copy-start(f32[192,2048]{1,0:T(8,128)} %copy-done.2) | copy-start | bytes 4718596
  (42 other events, 110.8 us)
Sparse Core Ops, SparseCore 0:
  11.0 77.9 all-gather.7
  92.1 77.5 all-gather.9
  172.6 77.5 all-gather.11
  253.0 76.0 all-gather.13
  331.9 142.7 all-gather.17
  477.5 142.7 all-gather.15
  623.2 142.7 all-gather.19
  822.0 356.3 reduce-scatter.15
  1181.3 358.7 reduce-scatter.13
  1542.8 357.3 reduce-scatter.11
  1903.0 357.3 reduce-scatter.9
  2263.1 967.3 reduce-scatter.21
  3233.4 967.3 reduce-scatter.19
  4203.5 967.3 reduce-scatter.17
where the time goes:
time: 5190 us; the launch traced here: 5180 us
  waiting for transfers between devices  4480 us (86%)
  local copies, waits for them, and re-layouts  248 us (5%)
  matrix products  223 us (4%)
  blocking collectives  119 us (2%)
  other arithmetic  77.9 us (2%)
    unnamed x15, waiting for transfers between devices  975 us
    reduce_scatter x1, waiting for transfers between devices, on_device(): lax.psum_scatter(grad_w_up, ('seq', 'dp'), scatter_dimension=0, tiled=True)  970 us
    reduce_scatter x1, waiting for transfers between devices, on_device(): lax.psum_scatter(grad_w_gate, ('seq', 'dp'), scatter_dimension=0, tiled=T...  970 us
    reduce_scatter x1, waiting for transfers between devices, on_device(): lax.psum_scatter(grad_w_in, ('seq', 'dp'), scatter_dimension=0, tiled=True)  360 us
    reduce_scatter x1, waiting for transfers between devices, on_device(): lax.psum_scatter(grad_w_forget, ('seq', 'dp'), scatter_dimension=0, tiled...  360 us
    reduce_scatter x1, waiting for transfers between devices, on_device(): lax.psum_scatter(grad_w_gate_out, ('seq', 'dp'), scatter_dimension=0, til...  269 us
    all_gather x1, waiting for transfers between devices, on_device(): lax.all_gather(w_up, ('seq', 'dp'), axis=0, tiled=True)  139 us
    all_gather x1, waiting for transfers between devices, on_device(): lax.all_gather(w_down, ('seq', 'dp'), axis=0, tiled=True)  134 us
  transfers between devices with their start and end apart: 18, of which 14 were waited for; matrix products, arithmetic and copies ran while one was open for 9% of the time, Pallas kernels for 0%

commit v1 on v0

v1 whole, which is shorter than its diff:
```python
import functools

import jax
import jax.numpy as jnp
from jax import lax
from jax.experimental import pallas as pl
from jax.experimental.pallas import tpu as pltpu
from jax.sharding import Mesh
from jax.sharding import PartitionSpec as P

EPSILON = 1e-06
F32 = jnp.float32
LOW = jnp.bfloat16
TENSOR_PARTS = 8
SWAP = [(0, 1), (1, 0)]
ROWS = 16


def product(left_op, right_op, kind=F32):
    return jnp.dot(left_op, right_op, preferred_element_type=F32).astype(kind)


def product_nt(left_op, right_op, kind=F32):
    return lax.dot_general(
        left_op, right_op, (((1,), (1,)), ((), ())), preferred_element_type=F32
    ).astype(kind)


def product_tn(left_op, right_op, kind=F32):
    return lax.dot_general(
        left_op, right_op, (((0,), (0,)), ((), ())), preferred_element_type=F32
    ).astype(kind)


def norm_forward(values):
    inverse = lax.rsqrt(jnp.mean(values * values, axis=-1, keepdims=True) + EPSILON)
    return (values * inverse, inverse)


def norm_backward(grad_in, normed, inverse, gains):
    grad_gain = jnp.sum(grad_in * normed, axis=0)
    grad_normed = grad_in * gains
    grad_values = inverse * (
        grad_normed - normed * jnp.mean(grad_normed * normed, axis=-1, keepdims=True)
    )
    return (grad_values, grad_gain)


def silu_slope(values):
    sig_values = jax.nn.sigmoid(values)
    return sig_values * (1.0 + values * (1.0 - sig_values))


def row_marks(ends, bucket, first, shape):
    rows = first + lax.broadcasted_iota(jnp.int32, shape, 0)
    docs = ends.shape[1]
    hit = rows == 0
    for doc in range(docs - 1):
        hit = jnp.logical_or(hit, rows == ends[bucket, doc])
    keep = jnp.where(hit, 0.0, 1.0)
    live = jnp.where(rows < ends[bucket, docs - 1], 1.0, 0.0)
    return (keep, live)


def prefix(decay, term, forward):
    rows = lax.broadcasted_iota(jnp.int32, decay.shape, 0)
    for step in (1, 2, 4):
        shift = step if forward else 8 - step
        inside = rows >= step if forward else rows < 8 - step
        moved_term = jnp.where(inside, pltpu.roll(term, shift, 0), 0.0)
        moved_decay = jnp.where(inside, pltpu.roll(decay, shift, 0), 1.0)
        term = term + decay * moved_term
        decay = decay * moved_decay
    return (decay, term)


def forward_kernel(
    buckets,
    segments,
    slots,
    ends,
    pre,
    floors,
    gains,
    forget_out,
    floor_out,
    slope_forget_out,
    slope_input_out,
    states_out,
    scaled_out,
    squares_out,
):
    width = floors.shape[1]
    seg_rows = pre.shape[0] // (buckets * segments)
    floor = floors[...]
    gain = gains[...]
    first_row = lax.broadcasted_iota(jnp.int32, (8, width), 0) == 0

    def one(bucket, segment, block, carry):
        base = pl.multiple_of(slots[bucket * segments + segment] * seg_rows + block * ROWS, ROWS)
        at = pl.ds(base, ROWS)
        keep, live = row_marks(ends, bucket, segment * seg_rows + block * ROWS, (ROWS, width))
        input_pre = pre[at, :width].astype(LOW).astype(F32)
        forget_pre = pre[at, width : 2 * width].astype(LOW).astype(F32)
        gate_pre = pre[at, 2 * width :]
        sig_forget = jax.nn.sigmoid(forget_pre)
        forget = (floor + (1.0 - floor) * sig_forget) * keep
        sig_input = jax.nn.sigmoid(input_pre)
        drive = input_pre * sig_input * live
        term = (1.0 - forget) * drive
        hidden, previous = [], []
        for low in range(0, ROWS, 8):
            decay_part, term_part = prefix(forget[low : low + 8], term[low : low + 8], True)
            here = term_part + decay_part * carry
            previous.append(jnp.where(first_row, carry, pltpu.roll(here, 1, 0)))
            hidden.append(here)
            carry = here[7:8]
        hidden = jnp.concatenate(hidden, axis=0)
        previous = jnp.concatenate(previous, axis=0)
        forget_out[at, :] = forget
        floor_term = (previous - drive) * keep * (1.0 - sig_forget)
        floor_out[at, :] = floor_term
        slope_forget_out[at, :] = floor_term * (1.0 - floor) * sig_forget
        slope_input_out[at, :] = (
            (1.0 - forget) * live * (sig_input * (1.0 + input_pre * (1.0 - sig_input)))
        )
        states = hidden.astype(LOW)
        states_out[at, :] = states
        states = states.astype(F32)
        scaled_out[at, :] = (states * gain * (gate_pre * jax.nn.sigmoid(gate_pre))).astype(LOW)
        squares_out[at, :] = jnp.sum(states * states, axis=1, keepdims=True)
        return carry

    def over_segments(segment, carries):
        def over_blocks(block, carries):
            return tuple(one(b, segment, block, carries[b]) for b in range(buckets))

        return lax.fori_loop(0, seg_rows // ROWS, over_blocks, carries)

    lax.fori_loop(
        0, segments, over_segments, tuple(jnp.zeros((1, width), F32) for _ in range(buckets))
    )


def backward_kernel(
    buckets,
    segments,
    slots,
    grad_branch,
    pre,
    states_in,
    factors,
    gains,
    forget_in,
    floor_in,
    slope_forget_in,
    slope_input_in,
    grads_out,
    branch_out,
    sums_out,
):
    width = gains.shape[1]
    seg_rows = pre.shape[0] // (buckets * segments)
    gain = gains[...]
    last_row = lax.broadcasted_iota(jnp.int32, (8, width), 0) == 7

    def one(bucket, segment, block, carry, floor_sum, gain_sum):
        base = pl.multiple_of(slots[bucket * segments + segment] * seg_rows + block * ROWS, ROWS)
        at = pl.ds(base, ROWS)
        grad_in = grad_branch[at, :]
        gate_pre = pre[at, 2 * width :]
        inverse = factors[at, 0:1]
        mean = factors[at, 1:2]
        normed = states_in[at, :].astype(F32) * inverse
        sig_gate = jax.nn.sigmoid(gate_pre)
        silu_gate = gate_pre * sig_gate
        scaled = normed * gain
        branch_out[at, :] = (scaled * silu_gate).astype(LOW)
        grads_out[at, 2 * width :] = (
            grad_in * scaled * (sig_gate * (1.0 + gate_pre * (1.0 - sig_gate)))
        ).astype(LOW)
        grad_scaled = grad_in * silu_gate
        gain_sum = gain_sum + grad_scaled * normed
        grad_hidden = (inverse * (grad_scaled * gain - normed * mean)).astype(LOW).astype(F32)
        forget = forget_in[at, :]
        term = forget * grad_hidden
        later = []
        for low in reversed(range(0, ROWS, 8)):
            decay_part, term_part = prefix(forget[low : low + 8], term[low : low + 8], False)
            here = term_part + decay_part * carry
            later.insert(0, jnp.where(last_row, carry, pltpu.roll(here, 7, 0)))
            carry = here[0:1]
        grad_total = grad_hidden + jnp.concatenate(later, axis=0)
        grads_out[at, :width] = (grad_total * slope_input_in[at, :]).astype(LOW)
        grads_out[at, width : 2 * width] = (grad_total * slope_forget_in[at, :]).astype(LOW)
        floor_sum = floor_sum + grad_total * floor_in[at, :]
        return (carry, floor_sum, gain_sum)

    def over_segments(step, state):
        segment = segments - 1 - step

        def over_blocks(block_step, state):
            block = seg_rows // ROWS - 1 - block_step
            carries, floor_sum, gain_sum = state
            fresh = []
            for b in range(buckets):
                carry, floor_sum, gain_sum = one(
                    b, segment, block, carries[b], floor_sum, gain_sum
                )
                fresh.append(carry)
            return (tuple(fresh), floor_sum, gain_sum)

        return lax.fori_loop(0, seg_rows // ROWS, over_blocks, state)

    zeros = jnp.zeros((ROWS, width), F32)
    carries = tuple(jnp.zeros((1, width), F32) for _ in range(buckets))
    _, floor_sum, gain_sum = lax.fori_loop(0, segments, over_segments, (carries, zeros, zeros))
    sums_out[0:1, :] = jnp.sum(floor_sum, axis=0, keepdims=True)
    sums_out[1:2, :] = jnp.sum(gain_sum, axis=0, keepdims=True)


VMEM_SPEC = pl.BlockSpec(memory_space=pltpu.VMEM)
SMEM_SPEC = pl.BlockSpec(memory_space=pltpu.SMEM)


def recurrence_forward(buckets, segments, slots, ends, pre, floors, gains):
    rows, width = pre.shape[0], floors.shape[1]
    shape = jax.ShapeDtypeStruct
    return pl.pallas_call(
        functools.partial(forward_kernel, buckets, segments),
        out_shape=tuple(shape((rows, width), F32) for _ in range(4))
        + tuple(shape((rows, width), LOW) for _ in range(2))
        + (shape((rows, 1), F32),),
        in_specs=[SMEM_SPEC] * 2 + [VMEM_SPEC] * 3,
        out_specs=tuple([VMEM_SPEC] * 7),
        compiler_params=pltpu.CompilerParams(vmem_limit_bytes=40 * 1024 * 1024),
        cost_estimate=pl.CostEstimate(
            flops=60 * rows * width, bytes_accessed=36 * rows * width, transcendentals=6 * rows * width
        ),
        name="recurrence_forward",
    )(slots, ends, pre, floors, gains)


def recurrence_backward(buckets, segments, slots, *operands):
    rows, width = operands[0].shape
    shape = jax.ShapeDtypeStruct
    return pl.pallas_call(
        functools.partial(backward_kernel, buckets, segments),
        out_shape=(
            shape((rows, 3 * width), LOW),
            shape((rows, width), LOW),
            shape((2, width), F32),
        ),
        in_specs=[SMEM_SPEC] + [VMEM_SPEC] * len(operands),
        out_specs=tuple([VMEM_SPEC] * 3),
        compiler_params=pltpu.CompilerParams(vmem_limit_bytes=40 * 1024 * 1024),
        cost_estimate=pl.CostEstimate(
            flops=60 * rows * width, bytes_accessed=44 * rows * width, transcendentals=2 * rows * width
        ),
        name="recurrence_backward",
    )(slots, *operands)


class Links:
    def __init__(self, sizes):
        self.sizes = sizes
        self.pairs = sizes["y"] == sizes["core"] == sizes["x"] == 2
        self.plane = ("x", "y", "core")
        self.owners = ("y", "core", "x")

    def place(self, axis):
        return lax.axis_index(axis)

    def slots(self):
        sizes = self.sizes
        x, y, core = jnp.meshgrid(
            jnp.arange(sizes["x"]), jnp.arange(sizes["y"]), jnp.arange(sizes["core"]), indexing="ij"
        )
        if self.pairs:
            x, y, core = x ^ self.place("x"), y ^ self.place("y"), core ^ self.place("core")
            slot = (core * 2 + x) * 2 + y
        else:
            slot = (x * sizes["y"] + y) * sizes["core"] + core
        return slot.reshape(-1).astype(jnp.int32)

    def swap(self, axis, value):
        return lax.ppermute(value, axis, SWAP)

    def rows(self, value):
        if not self.pairs:
            return lax.all_gather(value, self.plane, axis=0, tiled=True)
        half = value.shape[0] // 2
        top, end = value[:half], value[half:]
        x_top, y_end = self.swap("x", top), self.swap("y", end)
        x_end, y_top = self.swap("x", end), self.swap("y", top)
        both_top, both_end = self.swap("y", x_top), self.swap("x", y_end)
        own = jnp.concatenate([top, end, y_top, y_end, x_top, x_end, both_top, both_end], axis=0)
        return jnp.concatenate([own, self.swap("core", own)], axis=0)

    def rows_small(self, value):
        if not self.pairs:
            return lax.all_gather(value, self.plane, axis=0, tiled=True)
        for axis in ("y", "x", "core"):
            value = jnp.concatenate([value, self.swap(axis, value)], axis=0)
        return value

    def sum_rows(self, parts):
        if not self.pairs:
            return lax.psum_scatter(parts, self.plane, scatter_dimension=0, tiled=True).astype(F32)
        rows = parts.shape[0] // 8
        half = rows // 2
        kind = parts.dtype
        parts = parts.reshape(2, 4, rows, -1)
        other = self.swap("core", parts[1])
        chip = (parts[0].astype(F32) + other.astype(F32)).astype(kind).reshape(2, 2, rows, -1)
        top_in, end_in = self.swap("x", chip[1, :, :half]), self.swap("y", chip[:, 1, half:])
        top = chip[0, :, :half].astype(F32) + top_in.astype(F32)
        end = chip[:, 0, half:].astype(F32) + end_in.astype(F32)
        top_in, end_in = self.swap("y", top[1].astype(kind)), self.swap("x", end[1].astype(kind))
        return jnp.concatenate([top[0] + top_in.astype(F32), end[0] + end_in.astype(F32)], axis=0)

    def sum_rows_small(self, parts):
        if not self.pairs:
            return lax.psum_scatter(parts, self.plane, scatter_dimension=0, tiled=True)
        for axis in ("core", "x", "y"):
            half = parts.shape[0] // 2
            parts = parts[:half] + self.swap(axis, parts[half:])
        return parts

    def sum_all_small(self, value):
        planes = self.sizes["z"]
        if not (self.pairs and planes & (planes - 1) == 0):
            return lax.psum(value, ("z",) + self.plane)
        for axis in ("core", "x", "y"):
            value = value + self.swap(axis, value)
        step = 1
        while step < planes:
            value = value + lax.ppermute(value, "z", [(i, i ^ step) for i in range(planes)])
            step *= 2
        return value

    def exchange(self, value):
        return lax.all_to_all(value, self.owners, split_axis=0, concat_axis=0, tiled=True)

    def planes(self, value):
        return lax.all_gather(value, "z", axis=0, tiled=True)

    def sum_planes(self, value):
        return lax.psum_scatter(value, "z", scatter_dimension=0, tiled=True)

    def both_x(self, value):
        if self.sizes["x"] == 1:
            return value
        if self.sizes["x"] != 2:
            return lax.all_gather(value, "x", axis=0, tiled=True)
        other = self.swap("x", value)
        return jnp.where(
            self.place("x") == 0,
            jnp.concatenate([value, other], axis=0),
            jnp.concatenate([other, value], axis=0),
        )


def on_device(
    sizes,
    tokens,
    doc_lengths,
    w_in,
    w_forget,
    w_gate_out,
    w_out,
    w_gate,
    w_up,
    w_down,
    g_mix,
    g_out,
    g_ffn,
    floor_logit,
    cotangent,
):
    links = Links(sizes)
    seq, planes, buckets = sizes["y"] * sizes["core"], sizes["z"], sizes["x"]
    parts = seq * buckets
    width = tokens.shape[2]
    block = w_in.shape[0]
    hidden = w_gate.shape[1]
    slab = width // parts
    seq_place = links.place("y") * sizes["core"] + links.place("core")
    x_place, z_place = links.place("x"), links.place("z")
    owner = (seq_place * planes + z_place) * buckets + x_place

    def to_planes(values):
        lead = values.shape[:-1]
        return jnp.swapaxes(values.reshape(lead + (seq, planes, -1)), -3, -2).reshape(
            lead + (width,)
        )

    def from_planes(values):
        lead = values.shape[:-1]
        return jnp.swapaxes(values.reshape(lead + (planes, seq, -1)), -3, -2).reshape(
            lead + (width,)
        )

    def to_channels(weight):
        return (
            weight.reshape(block, seq, planes, buckets, block)
            .transpose(1, 3, 0, 2, 4)
            .reshape(parts, block, slab)
        )

    def from_channels(grads):
        return (
            grads.reshape(seq, buckets, block, planes, block)
            .transpose(2, 0, 3, 1, 4)
            .reshape(block, width)
        )

    def to_hidden(weight):
        return weight.reshape(block, parts, -1).transpose(1, 0, 2)

    def from_hidden(grads):
        return grads.transpose(1, 0, 2).reshape(block, hidden)

    def own_channels(vector):
        return lax.dynamic_index_in_dim(
            lax.dynamic_index_in_dim(
                vector.reshape(-1, seq, planes, buckets, block), seq_place, 1, keepdims=False
            ),
            x_place,
            2,
            keepdims=False,
        ).reshape(-1, slab)

    def put_channels(vector):
        vector = vector.reshape(-1, 1, planes, 1, block)
        zeros = jnp.zeros((vector.shape[0], seq, planes, buckets, block), F32)
        return lax.dynamic_update_slice(zeros, vector, (0, seq_place, 0, x_place, 0)).reshape(
            -1, width
        )

    mixer = jnp.concatenate([to_channels(w) for w in (w_in, w_forget, w_gate_out)], axis=2)
    full_mixer = links.planes(links.exchange(mixer).reshape(parts * block, 3 * slab))
    full_out = links.planes(to_planes(w_out))
    full_gate, full_up, full_down = (
        links.planes(links.exchange(to_hidden(w)).reshape(parts * block, -1))
        for w in (w_gate, w_up, w_down)
    )
    vectors = jnp.stack([g_mix, g_ffn, g_out, floor_logit]).astype(F32)
    vectors = links.sum_all_small(
        lax.dynamic_update_slice(jnp.zeros((4, width), F32), vectors, (0, owner * block))
    )
    gain_mix, gain_ffn = to_planes(vectors[0]), to_planes(vectors[1])
    own_vectors = own_channels(vectors[2:])
    gain_out = own_vectors[0:1]
    floors = jax.nn.sigmoid(own_vectors[1:2])
    slots = links.slots()
    ends = links.both_x(jnp.cumsum(doc_lengths, axis=1).astype(jnp.int32))

    inputs = to_planes(tokens[0]).astype(F32)
    grad_out = to_planes(cotangent[0])
    normed_in, inverse_in = norm_forward(inputs)
    all_mixed = links.rows((normed_in * gain_mix).astype(LOW))
    all_grad_out = links.rows(grad_out)
    pre = product(all_mixed, full_mixer)
    forget, floor_term, slope_forget, slope_input, states, scaled, squares = recurrence_forward(
        buckets, seq, slots, ends, pre, floors, gain_out
    )
    branch = links.sum_rows(product(scaled, full_out, LOW))
    square_sum = links.sum_rows_small(squares.reshape(parts, -1))
    inverse_h = lax.rsqrt(square_sum.reshape(-1, 1) * (1.0 / width) + EPSILON)
    branch = branch * inverse_h
    residual = inputs + branch

    normed_z, inverse_z = norm_forward(residual)
    all_ffn = links.rows((normed_z * gain_ffn).astype(LOW))
    gate_pre = product(all_ffn, full_gate)
    up_pre = product(all_ffn, full_up)
    silu_gate = jax.nn.silu(gate_pre)
    middle = (silu_gate * up_pre).astype(LOW)
    grad_middle = product(all_grad_out, full_down)
    grad_gate_low = (grad_middle * up_pre * silu_slope(gate_pre)).astype(LOW)
    grad_up_low = (grad_middle * silu_gate).astype(LOW)
    grad_ffn_in = links.sum_rows(
        (product_nt(grad_gate_low, full_gate) + product_nt(grad_up_low, full_up)).astype(LOW)
    )
    output = residual + links.sum_rows(product_nt(middle, full_down, LOW))
    grad_gate_w, grad_up_w, grad_down_w = (
        from_hidden(
            links.exchange(links.sum_planes(product_tn(*ops, LOW)).reshape(parts, block, -1))
        ).astype(F32)
        for ops in (
            (all_ffn, grad_gate_low),
            (all_ffn, grad_up_low),
            (all_grad_out, middle),
        )
    )
    grad_z_norm, grad_g_ffn = norm_backward(grad_ffn_in, normed_z, inverse_z, gain_ffn)
    grad_residual = grad_out.astype(F32) + grad_z_norm

    grad_branch_low = grad_residual.astype(LOW)
    mean_h = jnp.sum(grad_branch_low.astype(F32) * branch, axis=-1, keepdims=True) * (1.0 / width)
    factors = links.rows_small(jnp.concatenate([inverse_h, mean_h], axis=1).T[None])
    factors = jnp.swapaxes(factors, 1, 2).reshape(-1, 2)
    all_grad_branch = links.rows(grad_branch_low)
    grad_branch_in = product_nt(all_grad_branch, full_out)
    grads, branch_in, sums = recurrence_backward(
        buckets,
        seq,
        slots,
        grad_branch_in,
        pre,
        states,
        factors,
        gain_out,
        forget,
        floor_term,
        slope_forget,
        slope_input,
    )
    grad_mixed_in = links.sum_rows(product_nt(grads, full_mixer, LOW))
    grad_mixer = links.exchange(
        links.sum_planes(product_tn(all_mixed, grads, LOW)).reshape(parts, block, 3 * slab)
    )
    grad_in_w, grad_forget_w, grad_gate_out_w = (
        from_channels(grad_mixer[:, :, i * slab : (i + 1) * slab]).astype(F32) for i in range(3)
    )
    grad_out_w = from_planes(
        links.sum_planes(product_tn(branch_in, all_grad_branch, LOW))
    ).astype(F32)
    grad_x_norm, grad_g_mix = norm_backward(grad_mixed_in, normed_in, inverse_in, gain_mix)
    grad_tokens = grad_residual + grad_x_norm
    sums = jnp.concatenate([sums[0:1] * floors * (1.0 - floors), sums[1:2]], axis=0)
    vector_grads = jnp.concatenate(
        [from_planes(grad_g_mix)[None], from_planes(grad_g_ffn)[None], put_channels(sums)], axis=0
    )
    vector_grads = lax.dynamic_slice(
        links.sum_all_small(vector_grads), (0, owner * block), (4, block)
    )
    return (
        from_planes(output.astype(LOW))[None],
        from_planes(grad_tokens.astype(LOW))[None],
        grad_in_w,
        grad_forget_w,
        grad_gate_out_w,
        grad_out_w,
        grad_gate_w,
        grad_up_w,
        grad_down_w,
        vector_grads[0],
        vector_grads[3],
        vector_grads[1],
        vector_grads[2],
    )


def solution(mesh):
    seq, dp = mesh.shape["seq"], mesh.shape["dp"]
    core = 2 if seq % 2 == 0 else 1
    x = max(1, TENSOR_PARTS // seq)
    if dp % x:
        x = 1
    sizes = {"y": seq // core, "core": core, "z": dp // x, "x": x}
    split = Mesh(mesh.devices.reshape(tuple(sizes.values())), tuple(sizes))
    rows = P(("z", "x"), ("y", "core"), None)
    lengths = P(("z", "x"), None)
    matrix = P(("y", "core", "z", "x"), None)
    vector = P(("y", "core", "z", "x"))
    return jax.shard_map(
        functools.partial(on_device, sizes),
        mesh=split,
        in_specs=(rows, lengths) + (matrix,) * 7 + (vector,) * 4 + (rows,),
        out_specs=(rows, rows) + (matrix,) * 7 + (vector,) * 4,
        check_vma=False,
    )
```

time: 5190 us -> 776 us (0.15)
  waiting for transfers between devices: 4480 us -> 221 us
  matrix products: 223 us -> 123 us
  blocking collectives: 119 us -> 30.9 us
  starting transfers between devices: 15.7 us -> 94.3 us
  local copies, waits for them, and re-layouts: 248 us -> 194 us
    reduce_scatter x6 -> x5, waiting for transfers between devices: 2930 us -> 0.03 us  [sum_planes(): return lax.psum_scatter(value, 'z', scatter_dimension=0, tiled=True)]
    unnamed x15 -> x10, waiting for transfers between devices: 975 us -> 0.17 us
    all_gather x7 -> x5, waiting for transfers between devices: 550 us -> 59.4 us  [planes(): return lax.all_gather(value, 'z', axis=0, tiled=True)]
    ppermute x0 -> x65, waiting for transfers between devices: none -> 148 us  [the longest x61 142 us: swap(): return lax.ppermute(value, axis, SWAP)]
    slice x125 -> x21, local copies, waits for them, and re-layouts: 119 us -> 21.6 us  [the longest x4 14 us: sum_rows(): other = self.swap('core', parts[1])]
    unnamed x2 -> x0, blocking collectives: 90.4 us -> none
    ppermute x0 -> x65, starting transfers between devices: none -> 66.7 us  [the longest x61 61.6 us: swap(): return lax.ppermute(value, axis, SWAP)]
  transfers between devices with their start and end apart: 18 -> 81, of which waited for: 14 -> 36; matrix products, arithmetic and copies ran while one was open for 9% -> 44% of each run, Pallas kernels for 0% -> 2%
where the time goes in v1:
time: 776 us; the launch traced here: 765 us
  waiting for transfers between devices  221 us (28%)
  local copies, waits for them, and re-layouts  194 us (25%)
  matrix products  123 us (16%)
  starting transfers between devices  94.3 us (12%)
  other arithmetic  70.2 us (9%)
  blocking collectives  30.9 us (4%)
  between operations  16 us (2%)
  Pallas kernels  15.4 us (2%)
    ppermute x61, waiting for transfers between devices, swap(): return lax.ppermute(value, axis, SWAP)  142 us
    ppermute x61, starting transfers between devices, swap(): return lax.ppermute(value, axis, SWAP)  61.6 us
    all_gather x5, waiting for transfers between devices, planes(): return lax.all_gather(value, 'z', axis=0, tiled=True)  59.4 us
    dot_general x5, matrix products, product(): return jnp.dot(left_op, right_op, preferred_element_type=F32).astype(kind)  44.8 us
    unnamed x147, local copies, waits for them, and re-layouts  44.7 us
    dot_general x5, matrix products, product_tn(): lax.dot_general(left_op, right_op, (((0,), (0,)), ((), ())), preferred_el...  43.9 us
    dot_general x5, matrix products, product_nt(): lax.dot_general(left_op, right_op, (((1,), (1,)), ((), ())), preferred_el...  34.6 us
    all_to_all x2, blocking collectives, exchange(): lax.all_to_all(value, self.owners, split_axis=0, concat_axis=0, tiled=True)  30.9 us
  transfers between devices with their start and end apart: 81, of which 36 were waited for; matrix products, arithmetic and copies ran while one was open for 44% of the time, Pallas kernels for 2%

profile of v1, /device:TPU:16, one launch (start us, length us, event | category | flops | bytes accessed | tf_op | source)
XLA Modules:
  0.0 764.8 jit_solution(16483081813709617845)
XLA Ops:
  19.5 4.2 all-to-all-start
  41.7 7.9 %collective-permute-done.8 = bf16[96,2048]{1,0:T(8,128)(2,1)S(1)} collective-permute-done((bf16[96,2048]{1,0:T(8,128)(2,1)S(1)}, bf16[96,2048]{1,0:T(8,128)(2,1)S(1)}, u32[]{:S(2)}, u32[]{:S(2)}) %collective-permute-start.8) | collective-permute-done | bytes 393248 | tf_op jit(solution)/shard_map/ppermute | solution.py:287
  53.0 6.9 collective-permute-done.6
  79.9 20.3 %all-gather.6.cloned.1.call-done = bf16[2048,768]{1,0:T(8,128)(2,1)} async-done(((bf16[512,768]{1,0:T(8,128)(2,1)}), bf16[2048,768]{1,0:T(8,128)(2,1)}) %all-gather.6.cloned.1.call-update) | async-done | bytes 3145744 | tf_op jit(solution)/shard_map/all_gather | solution.py:346
  100.2 8.1 %fusion.44.pre = f32[1536,768]{1,0:T(8,128)S(1)} fusion(bf16[1536,2048]{1,0:T(8,128)(2,1)} %constant_dynamic-update-slice_fusion.7, bf16[2048,768]{1,0:T(8,128)(2,1)} %all-gather.6.cloned.1.call-done), kind=kOutput, calls=%fused_computation.230 | convolution fusion | flops 4831838208 | bytes 14155776 | tf_op jit(solution)/shard_map/dot_general | solution.py:20
  108.3 7.1 recurrence_forward.1
  122.0 7.8 %all-gather.8.cloned.1.call-done = bf16[256,2048]{1,0:T(8,128)(2,1)} async-done(((bf16[64,2048]{1,0:T(8,128)(2,1)}), bf16[256,2048]{1,0:T(8,128)(2,1)}) %all-gather.8.cloned.1.call-update) | async-done | bytes 1048592 | tf_op jit(solution)/shard_map/all_gather | solution.py:346
  138.0 15.7 %all_to_all.40 = bf16[8,64,704]{2,1,0:T(8,128)(2,1)} all-to-all(bf16[8,64,704]{2,1,0:T(8,128)(2,1)S(1)} %bitcast.297), channel_id=1, replica_groups=mesh['y'=2,'core'=2,'z'=4,'x'=2] {'y','core','x'}, dimensions={0} | all-to-all | bytes 1441792 | tf_op jit(solution)/shard_map/all_to_all | solution.py:343
  169.3 4.3 all-to-all-start.2
  190.2 4.2 fusion.3
  203.7 13.9 %collective-permute-done.20 = f32[1,192]{1,0:T(1,128)S(1)} collective-permute-done((f32[1,192]{1,0:T(1,128)S(1)}, f32[1,192]{1,0:T(1,128)S(1)}, u32[]{:S(2)}, u32[]{:S(2)}) %collective-permute-start.20) | collective-permute-done | bytes 800 | tf_op jit(solution)/shard_map/ppermute | solution.py:287
  221.7 8.2 %collective-permute-done.15 = bf16[96,2048]{1,0:T(8,128)(2,1)S(1)} collective-permute-done((bf16[96,2048]{1,0:T(8,128)(2,1)S(1)}, bf16[96,2048]{1,0:T(8,128)(2,1)S(1)}, u32[]{:S(2)}, u32[]{:S(2)}) %collective-permute-start.15) | collective-permute-done | bytes 393248 | tf_op jit(solution)/shard_map/ppermute | solution.py:287
  240.0 5.1 multiply_reduce_fusion.5
  259.6 7.4 collective-permute-done.22
  277.8 15.2 %all_to_all.41 = bf16[8,64,704]{2,1,0:T(8,128)(2,1)} all-to-all(bf16[8,64,704]{2,1,0:T(8,128)(2,1)S(1)} %bitcast.298), channel_id=1, replica_groups=mesh['y'=2,'core'=2,'z'=4,'x'=2] {'y','core','x'}, dimensions={0} | all-to-all | bytes 1441792 | tf_op jit(solution)/shard_map/all_to_all | solution.py:343
  297.5 4.3 constant_dynamic-update-slice_fusion.22
  301.7 10.5 %fusion.45 = f32[1536,704]{0,1:T(8,128)} fusion(bf16[1536,2048]{1,0:T(8,128)(2,1)} %constant_dynamic-update-slice_fusion.22, bf16[2048,704]{1,0:T(8,128)(2,1)} %all-gather.10.cloned.1.call-done), kind=kOutput, calls=%fused_computation.231 | convolution fusion | flops 4429185024 | bytes 13500416 | tf_op jit(solution)/shard_map/dot_general | solution.py:20
  312.3 10.5 %fusion.46 = f32[1536,704]{0,1:T(8,128)} fusion(bf16[1536,2048]{1,0:T(8,128)(2,1)} %constant_dynamic-update-slice_fusion.22, bf16[2048,704]{1,0:T(8,128)(2,1)} %all-gather.12.cloned.1.call-done), kind=kOutput, calls=%fused_computation.232 | convolution fusion | flops 4429185024 | bytes 13500416 | tf_op jit(solution)/shard_map/dot_general | solution.py:20
  322.7 31.3 %all-gather.14.cloned.1.call-done = bf16[2048,704]{1,0:T(8,128)(2,1)} async-done(((bf16[512,704]{1,0:T(8,128)(2,1)}), bf16[2048,704]{1,0:T(8,128)(2,1)}) %all-gather.14.cloned.1.call-update) | async-done | bytes 2883600 | tf_op jit(solution)/shard_map/all_gather | solution.py:346
  354.0 12.7 %multiply_convert_fusion = (bf16[1536,704]{0,1:T(8,128)(2,1)}, bf16[1536,704]{0,1:T(8,128)(2,1)}, bf16[1536,704]{0,1:T(8,128)(2,1)S(1)}) fusion(f32[1536,704]{0,1:T(8,128)} %fusion.45, f32[1536,704]{0,1:T(8,128)} %fusion.46, bf16[1536,2048]{1,0:T(8,128)(2,1)} %constant_dynamic-update-slice_fusion.38, bf16[2048,704]{1,0:T(8,128)(2,1)} %all-gather.14.cloned.1.call-done), kind=kOutput, calls=%fused_computation.12 | convolution fusion | flops 4445405184 | bytes 24313856 | tf_op jit(solution)/shard_map/dot_general | solution.py:20
  368.1 9.0 %convolution_convert_fusion.4 = bf16[2048,704]{0,1:T(8,128)(2,1)} fusion(bf16[1536,704]{0,1:T(8,128)(2,1)S(1)} %get-tuple-element.51, bf16[1536,2048]{1,0:T(8,128)(2,1)} %constant_dynamic-update-slice_fusion.38), kind=kOutput, calls=%fused_computation.18 | convolution fusion | flops 4430626816 | bytes 11337728 | tf_op jit(solution)/shard_map/dot_general | solution.py:30
  377.2 9.7 %convolution_convert_fusion.6 = bf16[2048,704]{0,1:T(8,128)(2,1)} fusion(bf16[1536,704]{0,1:T(8,128)(2,1)} %get-tuple-element.50, bf16[1536,2048]{1,0:T(8,128)(2,1)} %constant_dynamic-update-slice_fusion.22), kind=kOutput, calls=%fused_computation.20 | convolution fusion | flops 4430626816 | bytes 11337728 | tf_op jit(solution)/shard_map/dot_general | solution.py:30
  386.9 10.5 %fusion.47 = f32[1536,2048]{1,0:T(8,128)} fusion(bf16[1536,704]{0,1:T(8,128)(2,1)} %get-tuple-element.50, bf16[2048,704]{1,0:T(8,128)(2,1)} %all-gather.10.cloned.1.call-done), kind=kOutput, calls=%fused_computation.233 | convolution fusion | flops 4429185024 | bytes 17629184 | tf_op jit(solution)/shard_map/dot_general | solution.py:24
  397.4 8.5 %add_convert_fusion = bf16[1536,2048]{1,0:T(8,128)(2,1)S(1)} fusion(f32[1536,2048]{1,0:T(8,128)} %fusion.47, bf16[1536,704]{0,1:T(8,128)(2,1)S(1)} %copy-done.57, bf16[2048,704]{1,0:T(8,128)(2,1)S(1)} %copy-done.54), kind=kOutput, calls=%fused_computation | convolution fusion | flops 4435476480 | bytes 23920640 | tf_op jit(solution)/shard_map/dot_general | solution.py:24
  410.7 5.5 convolution_convert_fusion.2
  424.2 9.7 %convolution_convert_fusion.5 = bf16[2048,704]{0,1:T(8,128)(2,1)} fusion(bf16[1536,704]{0,1:T(8,128)(2,1)} %get-tuple-element.49, bf16[1536,2048]{1,0:T(8,128)(2,1)} %constant_dynamic-update-slice_fusion.22), kind=kOutput, calls=%fused_computation.19 | convolution fusion | flops 4430626816 | bytes 11337728 | tf_op jit(solution)/shard_map/dot_general | solution.py:30
  434.4 4.2 fusion.1
  449.0 10.1 %collective-permute-done.41 = bf16[2,96,2048]{2,1,0:T(8,128)(2,1)S(1)} collective-permute-done((bf16[2,96,2048]{2,1,0:T(8,128)(2,1)S(1)}, bf16[2,96,2048]{2,1,0:T(8,128)(2,1)S(1)}, u32[]{:S(2)}, u32[]{:S(2)}) %collective-permute-start.41) | collective-permute-done | bytes 786464 | tf_op jit(solution)/shard_map/ppermute | solution.py:287
  464.0 19.8 %collective-permute-done.44 = bf16[96,2048]{1,0:T(8,128)(2,1)S(1)} collective-permute-done((bf16[96,2048]{1,0:T(8,128)(2,1)S(1)}, bf16[96,2048]{1,0:T(8,128)(2,1)S(1)}, u32[]{:S(2)}, u32[]{:S(2)}) %collective-permute-start.44) | collective-permute-done | bytes 393248 | tf_op jit(solution)/shard_map/ppermute | solution.py:287
  508.8 6.5 collective-permute-done.47
  515.8 6.4 collective-permute-done.46
  535.1 8.5 %collective-permute-done.30 = bf16[96,2048]{1,0:T(8,128)(2,1)S(1)} collective-permute-done((bf16[96,2048]{1,0:T(8,128)(2,1)S(1)}, bf16[96,2048]{1,0:T(8,128)(2,1)S(1)}, u32[]{:S(2)}, u32[]{:S(2)}) %collective-permute-start.30) | collective-permute-done | bytes 393248 | tf_op jit(solution)/shard_map/ppermute | solution.py:287
  555.5 6.6 multiply_reduce_fusion.3
  575.0 4.8 fusion.48.grad_branch
  579.8 8.3 %recurrence_backward.1 = (bf16[1536,768]{1,0:T(8,128)(2,1)S(1)}, bf16[1536,256]{1,0:T(8,128)(2,1)S(1)}, f32[2,256]{1,0:T(2,128)S(1)}) custom-call(s32[8]{0:T(128)S(1)} %add.235.slots, f32[1536,256]{1,0:T(8,128)S(1)} %fusion.48.grad_branch, f32[1536,768]{1,0:T(8,128)} %copy-done, bf16[1536,256]{1,0:T(8,128)(2,1)S(1)} %get-tuple-element.25.states_in, ...), custom_call_target="tpu_custom_call" | custom-call | flops 23592960 | bytes 17301504 | tf_op jit(solution)/shard_map/recurrence_backward/pallas_call | solution.py:247
  588.1 5.3 convolution_convert_fusion
  597.5 5.7 convolution_convert_fusion.7
  603.3 9.9 %convolution_convert_fusion.3 = bf16[2048,768]{1,0:T(8,128)(2,1)} fusion(bf16[1536,2048]{1,0:T(8,128)(2,1)} %constant_dynamic-update-slice_fusion.7, bf16[1536,768]{1,0:T(8,128)(2,1)S(1)} %copy-done.10), kind=kOutput, calls=%fused_computation.17 | convolution fusion | flops 4833411072 | bytes 11796480 | tf_op jit(solution)/shard_map/dot_general | solution.py:30
  613.2 4.2 fusion
  626.2 4.2 all-to-all-start.7
  635.2 4.8 collective-permute-done.56
  646.0 10.4 %collective-permute-done.59 = bf16[96,2048]{1,0:T(8,128)(2,1)S(1)} collective-permute-done((bf16[96,2048]{1,0:T(8,128)(2,1)S(1)}, bf16[96,2048]{1,0:T(8,128)(2,1)S(1)}, u32[]{:S(2)}, u32[]{:S(2)}) %collective-permute-start.59) | collective-permute-done | bytes 393248 | tf_op jit(solution)/shard_map/ppermute | solution.py:287
  663.0 4.2 all-to-all-start.5
  672.3 7.1 all-to-all-done.5
  679.4 4.5 all-to-all-start.6
  688.4 7.7 %collective-permute-done.61 = f32[4,2048]{1,0:T(4,128)S(1)} collective-permute-done((f32[4,2048]{1,0:T(4,128)S(1)}, f32[4,2048]{1,0:T(4,128)S(1)}, u32[]{:S(2)}, u32[]{:S(2)}) %collective-permute-start.61) | collective-permute-done | bytes 32800 | tf_op jit(solution)/shard_map/ppermute | solution.py:287
  730.5 4.5 all-to-all-start.4
  740.8 6.2 all-to-all-done.4
  (473 shorter events, 336.4 us)
Async XLA Ops:
  19.5 16.7 %all-to-all-start = ((bf16[8,64,768]{2,1,0:T(8,128)(2,1)}), bf16[8,64,768]{2,1,0:T(8,128)(2,1)}, u32[]{:S(2)}, u32[]{:S(2)}) async-start(bf16[8,64,768]{2,1,0:T(8,128)(2,1)} %pad_maximum_fusion), calls=%async_computation | async-start | bytes 1572864 | tf_op jit(solution)/shard_map/all_to_all | solution.py:343
  23.7 76.5 %all-gather.6.cloned.1.call-start = ((), (), s32[]{:S(2)}) async-start(), calls=%async_computation.13 | async-start | bytes 3932160 | tf_op jit(solution)/shard_map/all_gather | solution.py:346
  36.3 93.5 %all-gather.8.cloned.1.call-start = ((), (), s32[]{:S(2)}) async-start(), calls=%async_computation.14 | async-start | bytes 1310720 | tf_op jit(solution)/shard_map/all_gather | solution.py:346
  40.9 19.0 %collective-permute-start.6 = (bf16[96,2048]{1,0:T(8,128)(2,1)S(1)}, bf16[96,2048]{1,0:T(8,128)(2,1)S(1)}, u32[]{:S(2)}, u32[]{:S(2)}) collective-permute-start(bf16[96,2048]{1,0:T(8,128)(2,1)S(1)} %get-tuple-element.79), channel_id=1, source_target_pairs={{0,16},{16,0},{1,17},{17,1},{2,18},{18,2},{3,19},{19,3},{4,20},{20... | collective-permute-start | bytes 1179656 | tf_op jit(solution)/shard_map/ppermute | solution.py:287
  41.5 20.9 %collective-permute-start.9 = (bf16[96,2048]{1,0:T(8,128)(2,1)S(1)}, bf16[96,2048]{1,0:T(8,128)(2,1)S(1)}, u32[]{:S(2)}, u32[]{:S(2)}) collective-permute-start(bf16[96,2048]{1,0:T(8,128)(2,1)S(1)} %get-tuple-element.78), channel_id=1, source_target_pairs={{0,1},{1,0},{2,3},{3,2},{4,5},{5,4},{6,7},{7,6},{8,9},{9,8},{10,11... | collective-permute-start | bytes 1179656 | tf_op jit(solution)/shard_map/ppermute | solution.py:287
  72.2 229.6 %all-gather.10.cloned.1.call-start = ((), (), s32[]{:S(2)}) async-start(), calls=%async_computation.15 | async-start | bytes 3932160 | tf_op jit(solution)/shard_map/all_gather | solution.py:346
  136.0 54.2 %collective-permute-start.13 = (bf16[4,192,2048]{2,1,0:T(8,128)(2,1)}, bf16[4,192,2048]{2,1,0:T(8,128)(2,1)}, u32[]{:S(2)}, u32[]{:S(2)}) collective-permute-start(bf16[4,192,2048]{2,1,0:T(8,128)(2,1)} %bitcast.14), channel_id=1, source_target_pairs={{0,8},{8,0},{1,9},{9,1},{2,10},{10,2},{3,11},{11,3},{4,12},{12,4},... | collective-permute-start | bytes 9437192 | tf_op jit(solution)/shard_map/ppermute | solution.py:287
  158.3 23.2 %collective-permute-start.33 = (bf16[96,2048]{1,0:T(8,128)(2,1)}, bf16[96,2048]{1,0:T(8,128)(2,1)}, u32[]{:S(2)}, u32[]{:S(2)}) collective-permute-start(bf16[96,2048]{1,0:T(8,128)(2,1)} %slice.281), channel_id=1, source_target_pairs={{0,16},{16,0},{1,17},{17,1},{2,18},{18,2},{3,19},{19,3},{4,20},{20... | collective-permute-start | bytes 1179656 | tf_op jit(solution)/shard_map/ppermute | solution.py:287
  158.9 19.2 %collective-permute-start.35 = (bf16[96,2048]{1,0:T(8,128)(2,1)}, bf16[96,2048]{1,0:T(8,128)(2,1)}, u32[]{:S(2)}, u32[]{:S(2)}) collective-permute-start(bf16[96,2048]{1,0:T(8,128)(2,1)} %slice.281), channel_id=1, source_target_pairs={{0,1},{1,0},{2,3},{3,2},{4,5},{5,4},{6,7},{7,6},{8,9},{9,8},{10,11... | collective-permute-start | bytes 1179656 | tf_op jit(solution)/shard_map/ppermute | solution.py:287
  162.2 17.8 %collective-permute-start.34 = (bf16[96,2048]{1,0:T(8,128)(2,1)}, bf16[96,2048]{1,0:T(8,128)(2,1)}, u32[]{:S(2)}, u32[]{:S(2)}) collective-permute-start(bf16[96,2048]{1,0:T(8,128)(2,1)} %slice.283), channel_id=1, source_target_pairs={{0,16},{16,0},{1,17},{17,1},{2,18},{18,2},{3,19},{19,3},{4,20},{20... | collective-permute-start | bytes 1179656 | tf_op jit(solution)/shard_map/ppermute | solution.py:287
  163.7 34.2 %collective-permute-start.36 = (bf16[96,2048]{1,0:T(8,128)(2,1)}, bf16[96,2048]{1,0:T(8,128)(2,1)}, u32[]{:S(2)}, u32[]{:S(2)}) collective-permute-start(bf16[96,2048]{1,0:T(8,128)(2,1)} %slice.283), channel_id=1, source_target_pairs={{0,1},{1,0},{2,3},{3,2},{4,5},{5,4},{6,7},{7,6},{8,9},{9,8},{10,11... | collective-permute-start | bytes 1179656 | tf_op jit(solution)/shard_map/ppermute | solution.py:287
  169.3 31.2 %all-to-all-start.2 = ((bf16[8,64,704]{2,1,0:T(8,128)(2,1)}), bf16[8,64,704]{2,1,0:T(8,128)(2,1)}, u32[]{:S(2)}, u32[]{:S(2)}) async-start(bf16[8,64,704]{2,1,0:T(8,128)(2,1)} %bitcast.294), calls=%async_computation.2 | async-start | bytes 1572864 | tf_op jit(solution)/shard_map/all_to_all | solution.py:343
  173.6 138.6 %all-gather.12.cloned.1.call-start = ((), (), s32[]{:S(2)}) async-start(), calls=%async_computation.16 | async-start | bytes 3932160 | tf_op jit(solution)/shard_map/all_gather | solution.py:346
  178.2 24.5 %collective-permute-start.37 = (bf16[96,2048]{1,0:T(8,128)(2,1)}, bf16[96,2048]{1,0:T(8,128)(2,1)S(1)}, u32[]{:S(2)}, u32[]{:S(2)}) collective-permute-start(bf16[96,2048]{1,0:T(8,128)(2,1)} %collective-permute-done.35), channel_id=1, source_target_pairs={{0,16},{16,0},{1,17},{17,1},{2,18},{18,2},{3,19},{19,3},{4,20},{20... | collective-permute-start | bytes 1179656 | tf_op jit(solution)/shard_map/ppermute | solution.py:287
  180.0 70.0 %collective-permute-start.38 = (bf16[96,2048]{1,0:T(8,128)(2,1)}, bf16[96,2048]{1,0:T(8,128)(2,1)}, u32[]{:S(2)}, u32[]{:S(2)}) collective-permute-start(bf16[96,2048]{1,0:T(8,128)(2,1)} %collective-permute-done.34), channel_id=1, source_target_pairs={{0,1},{1,0},{2,3},{3,2},{4,5},{5,4},{6,7},{7,6},{8,9},{9,8},{10,11... | collective-permute-start | bytes 1179656 | tf_op jit(solution)/shard_map/ppermute | solution.py:287
  195.4 22.1 %collective-permute-start.14 = (bf16[2,96,2048]{2,1,0:T(8,128)(2,1)}, bf16[2,96,2048]{2,1,0:T(8,128)(2,1)S(1)}, u32[]{:S(2)}, u32[]{:S(2)}) collective-permute-start(bf16[2,96,2048]{2,1,0:T(8,128)(2,1)} %slice_bitcast_fusion.22), channel_id=1, source_target_pairs={{0,1},{1,0},{2,3},{3,2},{4,5},{5,4},{6,7},{7,6},{8,9},{9,8},{10,11... | collective-permute-start | bytes 2359304 | tf_op jit(solution)/shard_map/ppermute | solution.py:287
  197.9 19.7 %collective-permute-start.16 = (bf16[2,96,2048]{2,1,0:T(8,128)(2,1)}, bf16[2,96,2048]{2,1,0:T(8,128)(2,1)}, u32[]{:S(2)}, u32[]{:S(2)}) collective-permute-start(bf16[2,96,2048]{2,1,0:T(8,128)(2,1)} %slice_bitcast_fusion.19), channel_id=1, source_target_pairs={{0,16},{16,0},{1,17},{17,1},{2,18},{18,2},{3,19},{19,3},{4,20},{20... | collective-permute-start | bytes 2359304 | tf_op jit(solution)/shard_map/ppermute | solution.py:287
  200.5 153.5 %all-gather.14.cloned.1.call-start = ((), (), s32[]{:S(2)}) async-start(), calls=%async_computation.17 | async-start | bytes 3932160 | tf_op jit(solution)/shard_map/all_gather | solution.py:346
  201.2 16.3 %collective-permute-start.20 = (f32[1,192]{1,0:T(1,128)S(1)}, f32[1,192]{1,0:T(1,128)S(1)}, u32[]{:S(2)}, u32[]{:S(2)}) collective-permute-start(f32[1,192]{1,0:T(1,128)S(1)} %slice.332), channel_id=1, source_target_pairs={{0,16},{16,0},{1,17},{17,1},{2,18},{18,2},{3,19},{19,3},{4,20},{20... | collective-permute-start | bytes 2312 | tf_op jit(solution)/shard_map/ppermute | solution.py:287
  246.5 22.0 %collective-permute-start.21 = (bf16[96,2048]{1,0:T(8,128)(2,1)S(1)}, bf16[96,2048]{1,0:T(8,128)(2,1)S(1)}, u32[]{:S(2)}, u32[]{:S(2)}) collective-permute-start(bf16[96,2048]{1,0:T(8,128)(2,1)S(1)} %get-tuple-element.77), channel_id=1, source_target_pairs={{0,16},{16,0},{1,17},{17,1},{2,18},{18,2},{3,19},{19,3},{4,20},{20... | collective-permute-start | bytes 1179656 | tf_op jit(solution)/shard_map/ppermute | solution.py:287
  248.6 18.4 %collective-permute-start.22 = (bf16[96,2048]{1,0:T(8,128)(2,1)S(1)}, bf16[96,2048]{1,0:T(8,128)(2,1)S(1)}, u32[]{:S(2)}, u32[]{:S(2)}) collective-permute-start(bf16[96,2048]{1,0:T(8,128)(2,1)S(1)} %get-tuple-element.76), channel_id=1, source_target_pairs={{0,16},{16,0},{1,17},{17,1},{2,18},{18,2},{3,19},{19,3},{4,20},{20... | collective-permute-start | bytes 1179656 | tf_op jit(solution)/shard_map/ppermute | solution.py:287
  252.1 41.4 %collective-permute-start.39 = (bf16[768,2048]{1,0:T(8,128)(2,1)}, bf16[768,2048]{1,0:T(8,128)(2,1)}, u32[]{:S(2)}, u32[]{:S(2)}) collective-permute-start(bf16[768,2048]{1,0:T(8,128)(2,1)} %get-tuple-element.92), channel_id=1, source_target_pairs={{0,8},{8,0},{1,9},{9,1},{2,10},{10,2},{3,11},{11,3},{4,12},{12,4},... | collective-permute-start | bytes 9437192 | tf_op jit(solution)/shard_map/ppermute | solution.py:287
  252.1 19.5 %collective-permute-start.24 = (bf16[96,2048]{1,0:T(8,128)(2,1)S(1)}, bf16[96,2048]{1,0:T(8,128)(2,1)S(1)}, u32[]{:S(2)}, u32[]{:S(2)}) collective-permute-start(bf16[96,2048]{1,0:T(8,128)(2,1)S(1)} %get-tuple-element.76), channel_id=1, source_target_pairs={{0,1},{1,0},{2,3},{3,2},{4,5},{5,4},{6,7},{7,6},{8,9},{9,8},{10,11... | collective-permute-start | bytes 1179656 | tf_op jit(solution)/shard_map/ppermute | solution.py:287
  275.8 21.7 %collective-permute-start.27 = (bf16[768,2048]{1,0:T(8,128)(2,1)}, bf16[768,2048]{1,0:T(8,128)(2,1)}, u32[]{:S(2)}, u32[]{:S(2)}) collective-permute-start(bf16[768,2048]{1,0:T(8,128)(2,1)} %get-tuple-element.108), channel_id=1, source_target_pairs={{0,8},{8,0},{1,9},{9,1},{2,10},{10,2},{3,11},{11,3},{4,12},{12,4},... | collective-permute-start | bytes 9437192 | tf_op jit(solution)/shard_map/ppermute | solution.py:287
  293.0 330.9 %reduce-scatter.14.cloned.1.call-start = ((), (), s32[]{:S(2)}) async-start(), calls=%async_computation.22 | async-start | bytes 3604480 | tf_op jit(solution)/shard_map/reduce_scatter | solution.py:349
  377.1 253.3 %reduce-scatter.10.cloned.1.call-start = ((), (), s32[]{:S(2)}) async-start(), calls=%async_computation.20 | async-start | bytes 3604480 | tf_op jit(solution)/shard_map/reduce_scatter | solution.py:349
  386.8 245.9 %reduce-scatter.12.cloned.1.call-start = ((), (), s32[]{:S(2)}) async-start(), calls=%async_computation.21 | async-start | bytes 3604480 | tf_op jit(solution)/shard_map/reduce_scatter | solution.py:349
  409.7 24.7 %collective-permute-start.40 = (bf16[4,192,2048]{2,1,0:T(8,128)(2,1)}, bf16[4,192,2048]{2,1,0:T(8,128)(2,1)}, u32[]{:S(2)}, u32[]{:S(2)}) collective-permute-start(bf16[4,192,2048]{2,1,0:T(8,128)(2,1)} %bitcast.48), channel_id=1, source_target_pairs={{0,8},{8,0},{1,9},{9,1},{2,10},{10,2},{3,11},{11,3},{4,12},{12,4},... | collective-permute-start | bytes 9437192 | tf_op jit(solution)/shard_map/ppermute | solution.py:287
  419.5 22.3 %collective-permute-start.28 = (bf16[4,192,2048]{2,1,0:T(8,128)(2,1)}, bf16[4,192,2048]{2,1,0:T(8,128)(2,1)}, u32[]{:S(2)}, u32[]{:S(2)}) collective-permute-start(bf16[4,192,2048]{2,1,0:T(8,128)(2,1)} %bitcast.35), channel_id=1, source_target_pairs={{0,8},{8,0},{1,9},{9,1},{2,10},{10,2},{3,11},{11,3},{4,12},{12,4},... | collective-permute-start | bytes 9437192 | tf_op jit(solution)/shard_map/ppermute | solution.py:287
  433.9 283.8 %reduce-scatter.8.cloned.1.call-start = ((), (), s32[]{:S(2)}) async-start(), calls=%async_computation.19 | async-start | bytes 1310720 | tf_op jit(solution)/shard_map/reduce_scatter | solution.py:349
  438.6 20.4 %collective-permute-start.41 = (bf16[2,96,2048]{2,1,0:T(8,128)(2,1)S(1)}, bf16[2,96,2048]{2,1,0:T(8,128)(2,1)S(1)}, u32[]{:S(2)}, u32[]{:S(2)}) collective-permute-start(bf16[2,96,2048]{2,1,0:T(8,128)(2,1)S(1)} %slice_bitcast_fusion.10), channel_id=1, source_target_pairs={{0,1},{1,0},{2,3},{3,2},{4,5},{5,4},{6,7},{7,6},{8,9},{9,8},{10,11... | collective-permute-start | bytes 2359304 | tf_op jit(solution)/shard_map/ppermute | solution.py:287
  440.2 20.4 %collective-permute-start.43 = (bf16[2,96,2048]{2,1,0:T(8,128)(2,1)S(1)}, bf16[2,96,2048]{2,1,0:T(8,128)(2,1)S(1)}, u32[]{:S(2)}, u32[]{:S(2)}) collective-permute-start(bf16[2,96,2048]{2,1,0:T(8,128)(2,1)S(1)} %slice_bitcast_fusion.7), channel_id=1, source_target_pairs={{0,16},{16,0},{1,17},{17,1},{2,18},{18,2},{3,19},{19,3},{4,20},{20... | collective-permute-start | bytes 2359304 | tf_op jit(solution)/shard_map/ppermute | solution.py:287
  446.2 59.0 %collective-permute-start.29 = (bf16[2,96,2048]{2,1,0:T(8,128)(2,1)}, bf16[2,96,2048]{2,1,0:T(8,128)(2,1)}, u32[]{:S(2)}, u32[]{:S(2)}) collective-permute-start(bf16[2,96,2048]{2,1,0:T(8,128)(2,1)} %slice_bitcast_fusion.16), channel_id=1, source_target_pairs={{0,1},{1,0},{2,3},{3,2},{4,5},{5,4},{6,7},{7,6},{8,9},{9,8},{10,11... | collective-permute-start | bytes 2359304 | tf_op jit(solution)/shard_map/ppermute | solution.py:287
  448.1 57.1 %collective-permute-start.31 = (bf16[2,96,2048]{2,1,0:T(8,128)(2,1)}, bf16[2,96,2048]{2,1,0:T(8,128)(2,1)}, u32[]{:S(2)}, u32[]{:S(2)}) collective-permute-start(bf16[2,96,2048]{2,1,0:T(8,128)(2,1)} %slice_bitcast_fusion.13), channel_id=1, source_target_pairs={{0,16},{16,0},{1,17},{17,1},{2,18},{18,2},{3,19},{19,3},{4,20},{20... | collective-permute-start | bytes 2359304 | tf_op jit(solution)/shard_map/ppermute | solution.py:287
  461.4 22.5 %collective-permute-start.44 = (bf16[96,2048]{1,0:T(8,128)(2,1)S(1)}, bf16[96,2048]{1,0:T(8,128)(2,1)S(1)}, u32[]{:S(2)}, u32[]{:S(2)}) collective-permute-start(bf16[96,2048]{1,0:T(8,128)(2,1)S(1)} %fusion.28), channel_id=1, source_target_pairs={{0,1},{1,0},{2,3},{3,2},{4,5},{5,4},{6,7},{7,6},{8,9},{9,8},{10,11... | collective-permute-start | bytes 1179656 | tf_op jit(solution)/shard_map/ppermute | solution.py:287
  462.5 25.0 %collective-permute-start.42 = (bf16[96,2048]{1,0:T(8,128)(2,1)S(1)}, bf16[96,2048]{1,0:T(8,128)(2,1)}, u32[]{:S(2)}, u32[]{:S(2)}) collective-permute-start(bf16[96,2048]{1,0:T(8,128)(2,1)S(1)} %fusion.27), channel_id=1, source_target_pairs={{0,16},{16,0},{1,17},{17,1},{2,18},{18,2},{3,19},{19,3},{4,20},{20... | collective-permute-start | bytes 1179656 | tf_op jit(solution)/shard_map/ppermute | solution.py:287
  501.7 22.0 %collective-permute-start.45 = (bf16[96,2048]{1,0:T(8,128)(2,1)S(1)}, bf16[96,2048]{1,0:T(8,128)(2,1)S(1)}, u32[]{:S(2)}, u32[]{:S(2)}) collective-permute-start(bf16[96,2048]{1,0:T(8,128)(2,1)S(1)} %get-tuple-element.73), channel_id=1, source_target_pairs={{0,16},{16,0},{1,17},{17,1},{2,18},{18,2},{3,19},{19,3},{4,20},{20... | collective-permute-start | bytes 1179656 | tf_op jit(solution)/shard_map/ppermute | solution.py:287
  504.7 17.5 %collective-permute-start.46 = (bf16[96,2048]{1,0:T(8,128)(2,1)S(1)}, bf16[96,2048]{1,0:T(8,128)(2,1)S(1)}, u32[]{:S(2)}, u32[]{:S(2)}) collective-permute-start(bf16[96,2048]{1,0:T(8,128)(2,1)S(1)} %get-tuple-element.72), channel_id=1, source_target_pairs={{0,16},{16,0},{1,17},{17,1},{2,18},{18,2},{3,19},{19,3},{4,20},{20... | collective-permute-start | bytes 1179656 | tf_op jit(solution)/shard_map/ppermute | solution.py:287
  507.2 19.4 %collective-permute-start.48 = (bf16[96,2048]{1,0:T(8,128)(2,1)S(1)}, bf16[96,2048]{1,0:T(8,128)(2,1)S(1)}, u32[]{:S(2)}, u32[]{:S(2)}) collective-permute-start(bf16[96,2048]{1,0:T(8,128)(2,1)S(1)} %get-tuple-element.72), channel_id=1, source_target_pairs={{0,1},{1,0},{2,3},{3,2},{4,5},{5,4},{6,7},{7,6},{8,9},{9,8},{10,11... | collective-permute-start | bytes 1179656 | tf_op jit(solution)/shard_map/ppermute | solution.py:287
  532.0 38.9 %collective-permute-start.51 = (bf16[768,2048]{1,0:T(8,128)(2,1)}, bf16[768,2048]{1,0:T(8,128)(2,1)}, u32[]{:S(2)}, u32[]{:S(2)}) collective-permute-start(bf16[768,2048]{1,0:T(8,128)(2,1)} %get-tuple-element.80), channel_id=1, source_target_pairs={{0,8},{8,0},{1,9},{9,1},{2,10},{10,2},{3,11},{11,3},{4,12},{12,4},... | collective-permute-start | bytes 9437192 | tf_op jit(solution)/shard_map/ppermute | solution.py:287
  603.2 127.3 %reduce-scatter.6.cloned.1.call-start = ((), (), s32[]{:S(2)}) async-start(), calls=%async_computation.18 | async-start | bytes 3932160 | tf_op jit(solution)/shard_map/reduce_scatter | solution.py:349
  619.4 20.6 %collective-permute-start.56 = (bf16[2,96,2048]{2,1,0:T(8,128)(2,1)}, bf16[2,96,2048]{2,1,0:T(8,128)(2,1)S(1)}, u32[]{:S(2)}, u32[]{:S(2)}) collective-permute-start(bf16[2,96,2048]{2,1,0:T(8,128)(2,1)} %slice_bitcast_fusion.4), channel_id=1, source_target_pairs={{0,1},{1,0},{2,3},{3,2},{4,5},{5,4},{6,7},{7,6},{8,9},{9,8},{10,11... | collective-permute-start | bytes 2359304 | tf_op jit(solution)/shard_map/ppermute | solution.py:287
  621.0 20.4 %collective-permute-start.58 = (bf16[2,96,2048]{2,1,0:T(8,128)(2,1)S(1)}, bf16[2,96,2048]{2,1,0:T(8,128)(2,1)S(1)}, u32[]{:S(2)}, u32[]{:S(2)}) collective-permute-start(bf16[2,96,2048]{2,1,0:T(8,128)(2,1)S(1)} %slice_bitcast_fusion.1), channel_id=1, source_target_pairs={{0,16},{16,0},{1,17},{17,1},{2,18},{18,2},{3,19},{19,3},{4,20},{20... | collective-permute-start | bytes 2359304 | tf_op jit(solution)/shard_map/ppermute | solution.py:287
  626.2 36.8 %all-to-all-start.7 = ((bf16[8,64,704]{2,1,0:T(8,128)(2,1)}), bf16[8,64,704]{2,1,0:T(8,128)(2,1)}, u32[]{:S(2)}, u32[]{:S(2)}) async-start(bf16[8,64,704]{2,1,0:T(8,128)(2,1)} %bitcast.88), calls=%async_computation.12 | async-start | bytes 1572864 | tf_op jit(solution)/shard_map/all_to_all | solution.py:343
  663.0 16.4 %all-to-all-start.5 = ((bf16[8,64,704]{2,1,0:T(8,128)(2,1)}), bf16[8,64,704]{2,1,0:T(8,128)(2,1)}, u32[]{:S(2)}, u32[]{:S(2)}) async-start(bf16[8,64,704]{2,1,0:T(8,128)(2,1)} %bitcast.295), calls=%async_computation.8 | async-start | bytes 1572864 | tf_op jit(solution)/shard_map/all_to_all | solution.py:343
  679.4 18.3 %all-to-all-start.6 = ((bf16[8,64,704]{2,1,0:T(8,128)(2,1)}), bf16[8,64,704]{2,1,0:T(8,128)(2,1)}, u32[]{:S(2)}, u32[]{:S(2)}) async-start(bf16[8,64,704]{2,1,0:T(8,128)(2,1)} %bitcast.293), calls=%async_computation.10 | async-start | bytes 1572864 | tf_op jit(solution)/shard_map/all_to_all | solution.py:343
  696.1 27.8 %collective-permute-start.62 = (f32[4,2048]{1,0:T(4,128)S(1)}, f32[4,2048]{1,0:T(4,128)S(1)}, u32[]{:S(2)}, u32[]{:S(2)}) collective-permute-start(f32[4,2048]{1,0:T(4,128)S(1)} %add.284), channel_id=1, source_target_pairs={{0,16},{16,0},{1,17},{17,1},{2,18},{18,2},{3,19},{19,3},{4,20},{20... | collective-permute-start | bytes 98312 | tf_op jit(solution)/shard_map/ppermute | solution.py:287
  730.5 16.6 %all-to-all-start.4 = ((bf16[8,64,768]{2,1,0:T(8,128)(2,1)}), bf16[8,64,768]{2,1,0:T(8,128)(2,1)}, u32[]{:S(2)}, u32[]{:S(2)}) async-start(bf16[8,64,768]{2,1,0:T(8,128)(2,1)} %bitcast.304), calls=%async_computation.5 | async-start | bytes 1572864 | tf_op jit(solution)/shard_map/all_to_all | solution.py:343
  (93 other events, 697.9 us)
Sparse Core Ops, SparseCore 0:
  36.4 63.7 all-gather.5
  102.3 27.4 all-gather.7
  153.9 60.8 all-gather.9
  216.2 62.1 all-gather.11
  293.1 60.8 all-gather.13
  377.2 56.0 reduce-scatter.13
  435.6 56.0 reduce-scatter.9
  494.0 56.0 reduce-scatter.11
  603.3 25.8 reduce-scatter.7
  631.5 60.2 reduce-scatter.5

commit v2 on v1

v2 whole, which is shorter than its diff:
```python
import functools
import math

import jax
import jax.numpy as jnp
from jax import lax
from jax.experimental import pallas as pl
from jax.experimental.pallas import tpu as pltpu
from jax.sharding import Mesh
from jax.sharding import PartitionSpec as P

EPSILON = 1e-06
F32 = jnp.float32
LOW = jnp.bfloat16
TENSOR_PARTS = 8
SWAP = [(0, 1), (1, 0)]
ROWS = 16
TILE = 512
SLOTS = 2
COST = 1
VMEM_BYTES = 58 * 1024 * 1024
SPARE_BYTES = 12 * 1024 * 1024
VMEM_SPEC = pl.BlockSpec(memory_space=pltpu.VMEM)
SMEM_SPEC = pl.BlockSpec(memory_space=pltpu.SMEM)
ANY_SPEC = pl.BlockSpec(memory_space=pl.ANY)


def product(left_op, right_op):
    return jnp.dot(left_op, right_op, preferred_element_type=F32)


def product_nt(left_op, right_op):
    return lax.dot_general(
        left_op, right_op, (((1,), (1,)), ((), ())), preferred_element_type=F32
    )


def product_tn(left_op, right_op):
    return lax.dot_general(
        left_op, right_op, (((0,), (0,)), ((), ())), preferred_element_type=F32
    )


def call(
    kernel,
    name,
    outs,
    operands,
    scratch=(),
    smem=0,
    any_from=None,
    any_outs=(),
    cost=(0, 0),
    after=(),
):
    any_from = len(operands) if any_from is None else any_from
    if after:
        inner, count, extra = kernel, len(operands), len(after)

        def kernel(*refs):
            inner(*refs[:count], *refs[count + extra :])

        operands = list(operands) + list(after)
        any_from = min(any_from, count)
    held = list(operands[smem:any_from]) + [
        jax.ShapeDtypeStruct(*out) for i, out in enumerate(outs) if i not in any_outs
    ]
    held = sum(math.prod(array.shape) * array.dtype.itemsize for array in held)
    specs = [
        SMEM_SPEC if i < smem else (ANY_SPEC if i >= any_from else VMEM_SPEC)
        for i in range(len(operands))
    ]
    return pl.pallas_call(
        kernel,
        out_shape=tuple(jax.ShapeDtypeStruct(*out) for out in outs),
        in_specs=specs,
        out_specs=tuple(ANY_SPEC if i in any_outs else VMEM_SPEC for i in range(len(outs))),
        scratch_shapes=list(scratch),
        compiler_params=pltpu.CompilerParams(
            vmem_limit_bytes=VMEM_BYTES if scratch else held + SPARE_BYTES
        ),
        cost_estimate=pl.CostEstimate(
            flops=int(cost[0] * COST), bytes_accessed=int(cost[1] * COST), transcendentals=0
        ),
        name=name,
    )(*operands)


def await_copies(view, sem):
    pltpu.make_async_copy(view, view, sem).wait()


def send(source, target, sem):
    pltpu.make_async_copy(source, target, sem).start()


class Layout:
    def __init__(self, sizes, slot_rows, block, hidden):
        self.seq = sizes["y"] * sizes["core"]
        self.planes = sizes["z"]
        self.buckets = sizes["x"]
        self.parts = self.seq * self.buckets
        self.slot_rows = slot_rows
        self.block = block
        share = hidden // self.parts
        self.split = -(-share // 256) * 128
        self.rest = share - self.split
        self.pieces = sizes["y"] == sizes["core"] == sizes["x"] == 2
        self.strip = self.buckets * block
        half = slot_rows // 2
        self.row_pieces = (
            [(c + s, r) for c in (0, 4) for s, r in ((0, 0), (1, 0), (2, 0), (3, 0), (3, half))]
            if self.pieces
            else [(0, 0)]
        )
        self.row_count = len(self.row_pieces)
        self.plane_count = self.planes if self.pieces else 1
        self.step_rows = SLOTS * slot_rows
        self.steps = self.parts // SLOTS

    def step(self, index):
        return pl.ds(pl.multiple_of(index * self.step_rows, self.step_rows), self.step_rows)

    def await_step(self, target, sems, index):
        for i in range(SLOTS):
            slot = index * SLOTS + i
            first = pl.multiple_of(slot * self.slot_rows, self.slot_rows)
            await_copies(target.at[pl.ds(first, self.slot_rows)], sems.at[slot])

    def fill_rows(self, pieces, target, sems):
        if not self.pieces:
            for slot in range(self.parts):
                at = pl.ds(slot * self.slot_rows, self.slot_rows)
                send(pieces[0].at[at], target.at[at], sems.at[slot])
            return
        for piece, (slot, first) in zip(pieces, self.row_pieces):
            at = pl.ds(slot * self.slot_rows + first, piece.shape[0])
            send(piece, target.at[at], sems.at[slot])

    def fill_weights(self, place, pieces, target, sem, columns=None):
        columns = target.shape[1] if columns is None else columns
        lanes = pl.ds(0, columns)
        if not self.pieces:
            send(pieces[0].at[:, lanes], target, sem)
            return
        if len(pieces) == 1:
            for plane in range(self.planes):
                for s in range(self.seq):
                    send(
                        pieces[0].at[pl.ds((plane * self.seq + s) * self.strip, self.strip), lanes],
                        target.at[pl.ds((s * self.planes + plane) * self.strip, self.strip)],
                        sem,
                    )
            return
        for step, piece in enumerate(pieces):
            plane = lax.rem(place - step + self.planes, self.planes)
            for s in range(self.seq):
                first = pl.multiple_of((s * self.planes + plane) * self.strip, self.strip)
                send(
                    piece.at[pl.ds(s * self.strip, self.strip), lanes],
                    target.at[pl.ds(first, self.strip)],
                    sem,
                )

    def fill_channels(self, place, pieces, target, sem):
        if len(pieces) == 1:
            send(pieces[0], target, sem)
            return
        for step, piece in enumerate(pieces):
            plane = lax.rem(place - step + self.planes, self.planes)
            first = pl.multiple_of(plane * self.block, self.block)
            send(piece, target.at[pl.ds(first, self.block)], sem)

    def strip_row(self, index):
        if not self.pieces:
            return index * self.strip
        return pl.multiple_of(
            ((index % self.planes) * self.seq + index // self.planes) * self.strip, self.strip
        )

    def weight_grads(self, out, staged, sem, step, value):
        if not self.pieces:
            rows = pl.ds(pl.multiple_of(step * TILE, TILE), TILE)
            staged[rows, :] = value
            send(staged.at[rows], out.at[rows], sem)
            return
        per = TILE // self.strip
        for i in range(per):
            rows = pl.ds(self.strip_row(step * per + i), self.strip)
            staged[rows, :] = value[i * self.strip : (i + 1) * self.strip]
            send(staged.at[rows], out.at[rows], sem)


def to_channels_kernel(layout, *refs):
    *weights, out = refs
    block, width = layout.block, layout.block * layout.planes
    for i, weight in enumerate(weights):
        for s in range(layout.seq):
            for z in range(layout.planes):
                for x in range(layout.buckets):
                    first = ((s * layout.planes + z) * layout.buckets + x) * block
                    to = i * width + z * block
                    out[s * layout.buckets + x, :, to : to + block] = weight[
                        :, first : first + block
                    ]


def from_channels_kernel(layout, grads, gains, *refs):
    count = (len(refs) - 1) // 2
    weights, outs, gain_out = refs[:count], refs[count:-1], refs[-1]
    block, width = layout.block, layout.block * layout.planes
    total = jnp.zeros((block, 1), F32)
    for i, (weight, out) in enumerate(zip(weights, outs)):
        for s in range(layout.seq):
            for z in range(layout.planes):
                for x in range(layout.buckets):
                    first = ((s * layout.planes + z) * layout.buckets + x) * block
                    at = i * width + z * block
                    out[:, first : first + block] = grads[
                        s * layout.buckets + x, :, at : at + block
                    ].astype(F32)
        total = total + jnp.sum(out[...] * weight[...].astype(F32), axis=1, keepdims=True)
    gain_out[...] = total / gains[...]


def to_hidden_kernel(layout, first, size, *refs):
    *weights, out = refs
    share = weights[0].shape[1] // layout.parts
    for i, weight in enumerate(weights):
        for part in range(layout.parts):
            at = part * share + first
            out[part, :, i * size : (i + 1) * size] = weight[:, at : at + size]
    used = len(weights) * size
    if used < out.shape[2]:
        out[:, :, used:] = jnp.zeros((layout.parts, layout.block, out.shape[2] - used), LOW)


def from_hidden_kernel(layout, first, second, gains, *refs):
    *weights, gate_out, up_out, down_out, gain_out = refs
    split, rest = layout.split, layout.rest
    share = split + rest
    total = jnp.zeros((layout.block, 1), F32)
    for i, out in enumerate((gate_out, up_out, down_out)):
        for part in range(layout.parts):
            at = part * share
            out[:, at : at + split] = first[part, :, i * split : (i + 1) * split].astype(F32)
            out[:, at + split : at + share] = second[part, :, i * rest : (i + 1) * rest].astype(F32)
        if i < len(weights):
            total = total + jnp.sum(out[...] * weights[i][...].astype(F32), axis=1, keepdims=True)
    gain_out[...] = total / gains[...]


def channel_gain_kernel(grads, weight, gains, floors, out, gain_out, floor_out):
    width = weight.shape[1]
    out[...] = grads[:, :width].astype(F32)
    total = jnp.sum(out[...] * weight[...].astype(F32), axis=1, keepdims=True)
    gain_out[...] = total / gains[...]
    floor = jax.nn.sigmoid(floors[...])
    floor_out[...] = grads[:, width : width + 1].astype(F32) * floor * (1.0 - floor)


def hold_kernel(value, out):
    out[...] = value[...]


def hold(value, after):
    return call(hold_kernel, "hold", [(value.shape, value.dtype)], [value], after=after)[0]


def halves_kernel(by_x, by_y, top, end):
    half = top.shape[0]
    top[...] = by_x[:half, :]
    end[...] = by_y[half:, :]


def row_marks(ends, bucket, first, shape):
    rows = first + lax.broadcasted_iota(jnp.int32, shape, 0)
    docs = ends.shape[1]
    hit = rows == 0
    for doc in range(docs - 1):
        hit = jnp.logical_or(hit, rows == ends[bucket, doc])
    keep = jnp.where(hit, 0.0, 1.0)
    live = jnp.where(rows < ends[bucket, docs - 1], 1.0, 0.0)
    return (keep, live)


def prefix(decay, term, forward):
    rows = lax.broadcasted_iota(jnp.int32, decay.shape, 0)
    for step in (1, 2, 4):
        shift = step if forward else 8 - step
        inside = rows >= step if forward else rows < 8 - step
        moved_term = jnp.where(inside, pltpu.roll(term, shift, 0), 0.0)
        moved_decay = jnp.where(inside, pltpu.roll(decay, shift, 0), 1.0)
        term = term + decay * moved_term
        decay = decay * moved_decay
    return (decay, term)


def mixer_forward_kernel(
    layout,
    slots,
    ends,
    place,
    floors,
    gains,
    *refs,
):
    rows_in = refs[: layout.row_count]
    weights_in = refs[layout.row_count : layout.row_count + layout.plane_count]
    outs, refs = refs[layout.row_count + layout.plane_count :][:7], refs[-14:]
    squares_out, rows_ref, weights, pre = refs[:4]
    row_sems, weight_sem, out_sems = refs[4:7]
    kept = refs[7:]
    (
        forget_out,
        floor_out,
        slope_forget_out,
        slope_input_out,
        gate_out,
        states_out,
        scaled_out,
    ) = kept
    width = floors.shape[1]
    seg_rows = layout.slot_rows
    buckets, segments = layout.buckets, layout.seq
    layout.fill_weights(place[0], weights_in, weights, weight_sem)
    layout.fill_rows(rows_in, rows_ref, row_sems)
    await_copies(weights, weight_sem)

    def multiply(step, _):
        at = layout.step(step)
        layout.await_step(rows_ref, row_sems, step)
        pre[at, :] = product(rows_ref[at, :], weights[...])
        return 0

    lax.fori_loop(0, layout.steps, multiply, 0)
    floor = floors[...]
    gain = gains[...]
    first_row = lax.broadcasted_iota(jnp.int32, (8, width), 0) == 0

    def one(bucket, segment, block, carry):
        base = pl.multiple_of(slots[bucket * segments + segment] * seg_rows + block * ROWS, ROWS)
        at = pl.ds(base, ROWS)
        keep, live = row_marks(ends, bucket, segment * seg_rows + block * ROWS, (ROWS, width))
        input_pre = pre[at, :width].astype(LOW).astype(F32)
        forget_pre = pre[at, width : 2 * width].astype(LOW).astype(F32)
        gate_pre = pre[at, 2 * width :]
        gate_out[at, :] = gate_pre
        sig_forget = jax.nn.sigmoid(forget_pre)
        forget = (floor + (1.0 - floor) * sig_forget) * keep
        sig_input = jax.nn.sigmoid(input_pre)
        drive = input_pre * sig_input * live
        term = (1.0 - forget) * drive
        hidden, previous = [], []
        for low in range(0, ROWS, 8):
            decay_part, term_part = prefix(forget[low : low + 8], term[low : low + 8], True)
            here = term_part + decay_part * carry
            previous.append(jnp.where(first_row, carry, pltpu.roll(here, 1, 0)))
            hidden.append(here)
            carry = here[7:8]
        hidden = jnp.concatenate(hidden, axis=0)
        previous = jnp.concatenate(previous, axis=0)
        forget_out[at, :] = forget
        floor_term = (previous - drive) * keep * (1.0 - sig_forget)
        floor_out[at, :] = floor_term
        slope_forget_out[at, :] = floor_term * (1.0 - floor) * sig_forget
        slope_input_out[at, :] = (
            (1.0 - forget) * live * (sig_input * (1.0 + input_pre * (1.0 - sig_input)))
        )
        states = hidden.astype(LOW)
        states_out[at, :] = states
        scaled_out[at, :] = (
            states.astype(F32) * gain * (gate_pre * jax.nn.sigmoid(gate_pre))
        ).astype(LOW)
        return carry

    def over_segments(segment, carries):
        def over_blocks(block, carries):
            return tuple(one(b, segment, block, carries[b]) for b in range(buckets))

        carries = lax.fori_loop(0, seg_rows // ROWS, over_blocks, carries)
        for b in range(buckets):
            first = pl.multiple_of(slots[b * segments + segment] * seg_rows, seg_rows)
            at = pl.ds(first, seg_rows)
            for i, (ref, out) in enumerate(zip(kept, outs)):
                send(ref.at[at], out.at[at], out_sems.at[i])
        return carries

    lax.fori_loop(
        0, segments, over_segments, tuple(jnp.zeros((1, width), F32) for _ in range(buckets))
    )
    ones = jnp.ones((8, width), LOW)
    for part in range(layout.parts):
        first = pl.multiple_of(slots[part] * seg_rows, seg_rows)
        states = states_out[pl.ds(first, seg_rows), :].astype(F32)
        squares = states * states
        high = squares.astype(LOW)
        rest = (squares - high.astype(F32)).astype(LOW)
        squares_out[part : part + 1, :] = (product_nt(ones, high) + product_nt(ones, rest))[0:1]
    for i, ref in enumerate(kept):
        await_copies(ref, out_sems.at[i])


def mixer_forward(layout, slots, ends, place, floors, gains, rows, weights, after):
    count = layout.parts * layout.slot_rows
    width = floors.shape[1]
    depth = rows[0].shape[1]
    wide = (count, width)
    return call(
        functools.partial(mixer_forward_kernel, layout),
        "mixer_forward",
        [(wide, F32)] * 5 + [(wide, LOW)] * 2 + [((layout.parts, layout.slot_rows), F32)],
        [slots, ends, place, floors, gains, *rows, *weights],
        [
            pltpu.VMEM((count, depth), LOW),
            pltpu.VMEM((depth, 3 * width), LOW),
            pltpu.VMEM((count, 3 * width), F32),
            pltpu.SemaphoreType.DMA((layout.parts,)),
            pltpu.SemaphoreType.DMA,
            pltpu.SemaphoreType.DMA((7,)),
        ]
        + [pltpu.VMEM(wide, F32)] * 5
        + [pltpu.VMEM(wide, LOW)] * 2,
        smem=3,
        any_from=5,
        any_outs=tuple(range(7)),
        after=after,
        cost=(6 * count * width * depth, 2 * count * depth + 6 * depth * width + 24 * count * width),
    )


def branch_kernel(layout, place, scaled, *refs):
    weights_in = refs[:1]
    outs = refs[1:-4]
    weights, staged, sem, out_sem = refs[-4:]
    layout.fill_channels(place[0], weights_in, weights, sem)
    await_copies(weights, sem)
    write_parts(
        layout, outs, staged, out_sem, lambda at: product(scaled[at, :], weights[...])
    )
    await_copies(staged, out_sem)


def write_parts(layout, outs, staged, sem, rows_of):
    per = layout.steps // len(outs)
    for i, out in enumerate(outs):
        start = (len(outs) - 1 - i) * per

        def one(step, _):
            at = layout.step(start + step)
            staged[at, :] = rows_of(at).astype(LOW)
            send(staged.at[at], out.at[layout.step(step)], sem)
            return 0

        lax.fori_loop(0, per, one, 0)


def part_shapes(layout, width):
    count = layout.parts * layout.slot_rows
    if layout.pieces:
        return [((count // 2, width), LOW)] * 2
    return [((count, width), LOW)]


def branch_parts(layout, place, scaled, weights, after):
    count, channels = scaled.shape
    width = weights[0].shape[1]
    return call(
        functools.partial(branch_kernel, layout),
        "branch_parts",
        part_shapes(layout, width),
        [place, scaled, *weights],
        [
            pltpu.VMEM((channels, width), LOW),
            pltpu.VMEM((count, width), LOW),
            pltpu.SemaphoreType.DMA,
            pltpu.SemaphoreType.DMA,
        ],
        smem=1,
        any_from=2,
        any_outs=(0, 1),
        after=after,
        cost=(2 * count * channels * width, 2 * count * width + 2 * channels * width),
    )


def mixer_backward_kernel(
    layout,
    slots,
    place,
    gains,
    *refs,
):
    saved, refs = refs[:6], refs[6:]
    rows_in = refs[: layout.row_count]
    refs = refs[layout.row_count :]
    weights_in, refs = refs[:1], refs[1:]
    mixed_in, refs = refs[: layout.row_count], refs[layout.row_count :]
    (
        grads_out,
        out_grads,
        mixer_grads,
        rows_ref,
        weights,
        mixed,
        grad_branch,
        branch,
        staged_out,
        staged,
        row_sems,
        weight_sem,
        mixed_sems,
        out_sems,
        saved_sems,
        *kept,
    ) = refs
    gate_in, states_in, forget_in, floor_in, slope_forget_in, slope_input_in = kept
    width = gains.shape[1]
    depth = weights.shape[1]
    seg_rows = layout.slot_rows
    buckets, segments = layout.buckets, layout.seq
    layout.fill_channels(place[0], weights_in, weights, weight_sem)
    layout.fill_rows(rows_in, rows_ref, row_sems)
    for i, (source, target) in enumerate(zip(saved, kept)):
        send(source, target, saved_sems.at[i])
    layout.fill_rows(mixed_in, mixed, mixed_sems)
    await_copies(weights, weight_sem)

    def multiply(step, _):
        at = layout.step(step)
        layout.await_step(rows_ref, row_sems, step)
        grad_branch[at, :] = product_nt(rows_ref[at, :depth], weights[...])
        return 0

    lax.fori_loop(0, layout.steps, multiply, 0)
    for i, target in enumerate(kept):
        await_copies(target, saved_sems.at[i])
    gain = gains[...]
    last_row = lax.broadcasted_iota(jnp.int32, (8, width), 0) == 7

    def one(bucket, segment, block, carry, floor_sum):
        base = pl.multiple_of(slots[bucket * segments + segment] * seg_rows + block * ROWS, ROWS)
        at = pl.ds(base, ROWS)
        grad_in = grad_branch[at, :]
        gate_pre = gate_in[at, :]
        factors = rows_ref[at, depth : depth + 4].astype(F32)
        inverse = factors[:, 0:1] + factors[:, 1:2]
        mean = factors[:, 2:3] + factors[:, 3:4]
        normed = states_in[at, :].astype(F32) * inverse
        sig_gate = jax.nn.sigmoid(gate_pre)
        silu_gate = gate_pre * sig_gate
        scaled = normed * gain
        branch[at, :] = (scaled * silu_gate).astype(LOW)
        grads_out[at, 2 * width :] = (
            grad_in * scaled * (sig_gate * (1.0 + gate_pre * (1.0 - sig_gate)))
        ).astype(LOW)
        grad_scaled = grad_in * silu_gate
        grad_hidden = (inverse * (grad_scaled * gain - normed * mean)).astype(LOW).astype(F32)
        forget = forget_in[at, :]
        term = forget * grad_hidden
        later = []
        for low in reversed(range(0, ROWS, 8)):
            decay_part, term_part = prefix(forget[low : low + 8], term[low : low + 8], False)
            here = term_part + decay_part * carry
            later.insert(0, jnp.where(last_row, carry, pltpu.roll(here, 7, 0)))
            carry = here[0:1]
        grad_total = grad_hidden + jnp.concatenate(later, axis=0)
        grads_out[at, :width] = (grad_total * slope_input_in[at, :]).astype(LOW)
        grads_out[at, width : 2 * width] = (grad_total * slope_forget_in[at, :]).astype(LOW)
        floor_sum = floor_sum + grad_total * floor_in[at, :]
        return (carry, floor_sum)

    def over_segments(step, state):
        segment = segments - 1 - step

        def over_blocks(block_step, state):
            block = seg_rows // ROWS - 1 - block_step
            carries, floor_sum = state
            fresh = []
            for b in range(buckets):
                carry, floor_sum = one(b, segment, block, carries[b], floor_sum)
                fresh.append(carry)
            return (tuple(fresh), floor_sum)

        return lax.fori_loop(0, seg_rows // ROWS, over_blocks, state)

    zeros = jnp.zeros((ROWS, width), F32)
    carries = tuple(jnp.zeros((1, width), F32) for _ in range(buckets))
    _, floor_sum = lax.fori_loop(0, segments, over_segments, (carries, zeros))
    staged_out[:, :depth] = product_tn(branch[...], rows_ref[:, :depth]).astype(LOW)
    ones = jnp.ones((ROWS, 128), LOW)
    high = floor_sum.astype(LOW)
    rest = (floor_sum - high.astype(F32)).astype(LOW)
    staged_out[:, depth:] = (product_tn(high, ones) + product_tn(rest, ones)).astype(LOW)
    send(staged_out, out_grads, out_sems.at[0])
    for slot in range(layout.parts):
        at = pl.ds(slot * seg_rows, seg_rows)
        await_copies(mixed.at[at], mixed_sems.at[slot])

    def over_features(step, _):
        columns = pl.ds(pl.multiple_of(step * TILE, TILE), TILE)
        value = product_tn(mixed[:, columns], grads_out[...]).astype(LOW)
        layout.weight_grads(mixer_grads, staged, out_sems.at[1], step, value)
        return 0

    lax.fori_loop(0, mixed.shape[1] // TILE, over_features, 0)
    await_copies(staged_out, out_sems.at[0])
    await_copies(staged, out_sems.at[1])


def mixer_backward(layout, slots, place, gains, saved, rows, weights, mixed, after):
    count = layout.parts * layout.slot_rows
    width = gains.shape[1]
    depth = mixed[0].shape[1]
    wide = depth + 128
    return call(
        functools.partial(mixer_backward_kernel, layout),
        "mixer_backward",
        [
            ((count, 3 * width), LOW),
            ((width, wide), LOW),
            ((depth, 3 * width), LOW),
        ],
        [slots, place, gains, *saved, *rows, *weights, *mixed],
        [
            pltpu.VMEM((count, wide), LOW),
            pltpu.VMEM((width, depth), LOW),
            pltpu.VMEM((count, depth), LOW),
            pltpu.VMEM((count, width), F32),
            pltpu.VMEM((count, width), LOW),
            pltpu.VMEM((width, wide), LOW),
            pltpu.VMEM((depth, 3 * width), LOW),
            pltpu.SemaphoreType.DMA((layout.parts,)),
            pltpu.SemaphoreType.DMA,
            pltpu.SemaphoreType.DMA((layout.parts,)),
            pltpu.SemaphoreType.DMA((2,)),
            pltpu.SemaphoreType.DMA((6,)),
        ]
        + [pltpu.VMEM(array.shape, array.dtype) for array in saved],
        smem=2,
        any_from=3,
        any_outs=(1, 2),
        after=after,
        cost=(10 * count * width * depth, 4 * count * depth + 8 * depth * width + 30 * count * width),
    )


def mixed_grad_kernel(layout, place, grads, *refs):
    weights_in = refs[: layout.plane_count]
    outs = refs[layout.plane_count : -4]
    weights, staged, sem, out_sem = refs[-4:]
    layout.fill_weights(place[0], weights_in, weights, sem)
    await_copies(weights, sem)
    write_parts(
        layout, outs, staged, out_sem, lambda at: product_nt(grads[at, :], weights[...])
    )
    await_copies(staged, out_sem)


def mixed_grad_parts(layout, place, grads, weights, depth, after):
    count, columns = grads.shape
    return call(
        functools.partial(mixed_grad_kernel, layout),
        "mixed_grad_parts",
        part_shapes(layout, depth),
        [place, grads, *weights],
        [
            pltpu.VMEM((depth, columns), LOW),
            pltpu.VMEM((count, depth), LOW),
            pltpu.SemaphoreType.DMA,
            pltpu.SemaphoreType.DMA,
        ],
        smem=1,
        any_from=2,
        any_outs=(0, 1),
        after=after,
        cost=(2 * count * columns * depth, 2 * count * depth + 4 * depth * columns),
    )


def glu_rows(rows_ref, grads_ref, weights, acts, at, width):
    pre = product(rows_ref[at, :], weights[:, : 2 * width])
    gate_pre, up_pre = pre[:, :width], pre[:, width:]
    grad_middle = product(grads_ref[at, :], weights[:, 2 * width : 3 * width])
    sig_gate = jax.nn.sigmoid(gate_pre)
    silu_gate = gate_pre * sig_gate
    acts[at, :width] = (
        grad_middle * up_pre * (sig_gate * (1.0 + gate_pre * (1.0 - sig_gate)))
    ).astype(LOW)
    acts[at, width : 2 * width] = (grad_middle * silu_gate).astype(LOW)
    acts[at, 2 * width : 3 * width] = (silu_gate * up_pre).astype(LOW)
    if 3 * width < acts.shape[1]:
        acts[at, 3 * width :] = jnp.zeros((at.size, acts.shape[1] - 3 * width), LOW)


def glu_grads(layout, rows_ref, grads_ref, acts, out, staged, sem, width):
    def over_features(step, _):
        columns = pl.ds(pl.multiple_of(step * TILE, TILE), TILE)
        left = product_tn(rows_ref[:, columns], acts[:, : 2 * width])
        right = product_tn(grads_ref[:, columns], acts[:, 2 * width :])
        value = jnp.concatenate([left, right], axis=1).astype(LOW)
        layout.weight_grads(out, staged, sem, step, value)
        return 0

    lax.fori_loop(0, rows_ref.shape[1] // TILE, over_features, 0)


def glu_first_kernel(layout, first_count, place, *refs):
    rows_in, refs = refs[: layout.row_count], refs[layout.row_count :]
    grads_in, refs = refs[: layout.row_count], refs[layout.row_count :]
    weights_in, refs = refs[:first_count], refs[first_count:]
    (
        acts_out,
        weight_grads,
        rows_ref,
        grads_ref,
        weights,
        acts,
        staged,
        row_sems,
        grad_sems,
        weight_sem,
        acts_sem,
        out_sem,
    ) = refs
    width = layout.split
    layout.fill_weights(place[0], weights_in, weights, weight_sem)
    layout.fill_rows(rows_in, rows_ref, row_sems)
    layout.fill_rows(grads_in, grads_ref, grad_sems)
    await_copies(weights, weight_sem)

    def one(step, _):
        at = layout.step(step)
        layout.await_step(rows_ref, row_sems, step)
        layout.await_step(grads_ref, grad_sems, step)
        glu_rows(rows_ref, grads_ref, weights, acts, at, width)
        send(acts.at[at], acts_out.at[at], acts_sem)
        return 0

    lax.fori_loop(0, layout.steps, one, 0)
    glu_grads(layout, rows_ref, grads_ref, acts, weight_grads, staged, out_sem, width)
    await_copies(acts, acts_sem)
    await_copies(staged, out_sem)


def glu_first(layout, place, rows, grads, weights):
    count = layout.parts * layout.slot_rows
    depth, columns = rows[0].shape[1], weights[0].shape[1]
    sems = pltpu.SemaphoreType.DMA
    return call(
        functools.partial(glu_first_kernel, layout, len(weights)),
        "glu_first",
        [((count, columns), LOW), ((depth, columns), LOW)],
        [place, *rows, *grads, *weights],
        [
            pltpu.VMEM((count, depth), LOW),
            pltpu.VMEM((count, depth), LOW),
            pltpu.VMEM((depth, columns), LOW),
            pltpu.VMEM((count, columns), LOW),
            pltpu.VMEM((depth, columns), LOW),
            sems((layout.parts,)),
            sems((layout.parts,)),
            sems,
            sems,
            sems,
        ],
        smem=1,
        any_from=1,
        any_outs=(0, 1),
        cost=(4 * count * depth * columns, 4 * count * depth + 4 * depth * columns),
    )


def glu_second_kernel(layout, first_count, place, *refs):
    rows_in, refs = refs[: layout.row_count], refs[layout.row_count :]
    grads_in, refs = refs[: layout.row_count], refs[layout.row_count :]
    first_in, refs = refs[:first_count], refs[first_count:]
    second_in, refs = refs[:first_count], refs[first_count:]
    first_acts_in, acts_out = refs[0], refs[1]
    outs = refs[2:-14]
    (
        rows_ref,
        grads_ref,
        first,
        second,
        first_acts,
        acts,
        row_sems,
        grad_sems,
        first_sem,
        second_sem,
        first_acts_sem,
        acts_sem,
        staged,
        out_sem,
    ) = refs[-14:]
    width = layout.rest
    layout.fill_weights(place[0], second_in, second, second_sem)
    layout.fill_rows(rows_in, rows_ref, row_sems)
    layout.fill_rows(grads_in, grads_ref, grad_sems)
    layout.fill_weights(place[0], first_in, first, first_sem)
    send(first_acts_in.at[:, pl.ds(0, first.shape[1])], first_acts, first_acts_sem)
    await_copies(second, second_sem)

    def one(step, _):
        at = layout.step(step)
        layout.await_step(rows_ref, row_sems, step)
        layout.await_step(grads_ref, grad_sems, step)
        glu_rows(rows_ref, grads_ref, second, acts, at, width)
        send(acts.at[at], acts_out.at[at], acts_sem)
        return 0

    lax.fori_loop(0, layout.steps, one, 0)
    await_copies(first, first_sem)
    await_copies(first_acts, first_acts_sem)
    write_parts(
        layout,
        outs,
        staged,
        out_sem,
        lambda at: product_nt(first_acts[at, :], first[...])
        + product_nt(acts[at, : 2 * width], second[:, : 2 * width]),
    )
    await_copies(acts, acts_sem)
    await_copies(staged, out_sem)


def glu_second(layout, place, rows, grads, first, second, first_acts):
    count = layout.parts * layout.slot_rows
    depth, columns = rows[0].shape[1], second[0].shape[1]
    first_columns = 2 * layout.split
    sems = pltpu.SemaphoreType.DMA
    return call(
        functools.partial(glu_second_kernel, layout, len(first)),
        "glu_second",
        [((count, columns), LOW)] + part_shapes(layout, depth),
        [place, *rows, *grads, *first, *second, first_acts],
        [
            pltpu.VMEM((count, depth), LOW),
            pltpu.VMEM((count, depth), LOW),
            pltpu.VMEM((depth, first_columns), LOW),
            pltpu.VMEM((depth, columns), LOW),
            pltpu.VMEM((count, first_columns), LOW),
            pltpu.VMEM((count, columns), LOW),
            sems((layout.parts,)),
            sems((layout.parts,)),
            sems,
            sems,
            sems,
            sems,
            pltpu.VMEM((count, depth), LOW),
            sems,
        ],
        smem=1,
        any_from=1,
        any_outs=(0, 1, 2),
        cost=(5 * count * depth * columns, 6 * count * depth + 4 * depth * columns),
    )


def glu_third_kernel(layout, place, *refs):
    rows_in, refs = refs[: layout.row_count], refs[layout.row_count :]
    grads_in, refs = refs[: layout.row_count], refs[layout.row_count :]
    acts_in, weight_grads = refs[:2]
    rows_ref, grads_ref, acts, staged, row_sems, grad_sems, acts_sem, out_sem = refs[2:]
    width = layout.rest
    send(acts_in, acts, acts_sem)
    layout.fill_rows(rows_in, rows_ref, row_sems)
    layout.fill_rows(grads_in, grads_ref, grad_sems)
    for slot in range(layout.parts):
        at = pl.ds(slot * layout.slot_rows, layout.slot_rows)
        await_copies(rows_ref.at[at], row_sems.at[slot])
        await_copies(grads_ref.at[at], grad_sems.at[slot])
    await_copies(acts, acts_sem)
    glu_grads(layout, rows_ref, grads_ref, acts, weight_grads, staged, out_sem, width)
    await_copies(staged, out_sem)


def glu_third(layout, place, rows, grads, acts, after):
    count, columns = acts.shape
    depth = rows[0].shape[1]
    sems = pltpu.SemaphoreType.DMA
    return call(
        functools.partial(glu_third_kernel, layout),
        "glu_third",
        [((depth, columns), LOW)],
        [place, *rows, *grads, acts],
        [
            pltpu.VMEM((count, depth), LOW),
            pltpu.VMEM((count, depth), LOW),
            pltpu.VMEM((count, columns), LOW),
            pltpu.VMEM((depth, columns), LOW),
            sems((layout.parts,)),
            sems((layout.parts,)),
            sems,
            sems,
        ],
        smem=1,
        any_from=1,
        any_outs=(0,),
        after=after,
        cost=(2 * count * depth * columns, 4 * count * depth + 2 * depth * columns),
    )[0]


def output_kernel(layout, first_count, place, *refs):
    first_in, refs = refs[:first_count], refs[first_count:]
    second_in, refs = refs[:first_count], refs[first_count:]
    first_acts_in, second_acts_in = refs[:2]
    outs = refs[2:-6]
    first, second, first_acts, second_acts, staged, sems = refs[-6:]
    for weights_in, weights, acts_in, acts, width, i in (
        (first_in, first, first_acts_in, first_acts, layout.split, 0),
        (second_in, second, second_acts_in, second_acts, layout.rest, 2),
    ):
        lanes = pl.ds(2 * width, weights.shape[1])
        layout.fill_weights(
            place[0], [piece.at[:, lanes] for piece in weights_in], weights, sems.at[i]
        )
        send(acts_in.at[:, lanes], acts, sems.at[i + 1])
    await_copies(first, sems.at[0])
    await_copies(first_acts, sems.at[1])
    await_copies(second, sems.at[2])
    await_copies(second_acts, sems.at[3])
    write_parts(
        layout,
        outs,
        staged,
        sems.at[4],
        lambda at: product_nt(first_acts[at, :], first[...])
        + product_nt(second_acts[at, :], second[...]),
    )
    await_copies(staged, sems.at[4])


def output_parts(layout, place, first, second, first_acts, second_acts, depth, after):
    count = first_acts.shape[0]
    widths = first_acts.shape[1] - 2 * layout.split, second_acts.shape[1] - 2 * layout.rest
    return call(
        functools.partial(output_kernel, layout, len(first)),
        "output_parts",
        part_shapes(layout, depth),
        [place, *first, *second, first_acts, second_acts],
        [pltpu.VMEM((depth, width), LOW) for width in widths]
        + [pltpu.VMEM((count, width), LOW) for width in widths]
        + [pltpu.VMEM((count, depth), LOW), pltpu.SemaphoreType.DMA((5,))],
        smem=1,
        any_from=1,
        any_outs=(0, 1),
        after=after,
        cost=(2 * count * depth * sum(widths), 2 * count * depth + 2 * depth * sum(widths)),
    )


def summed(parts, at):
    total = parts[0][at, :]
    if len(parts) > 1:
        half = parts[1].shape[0]
        part = parts[1] if at.start < half else parts[2]
        first = at.start % half
        total = total + part[first : first + ROWS, :].astype(F32)
    return total


def row_steps(count):
    return [slice(first, first + ROWS) for first in range(0, count, ROWS)]


def inverse_rms(values):
    return lax.rsqrt(jnp.mean(values * values, axis=1, keepdims=True) + EPSILON)


def norm_kernel(tokens, gains, out):
    for at in row_steps(tokens.shape[0]):
        values = tokens[at, :].astype(F32)
        out[at, :] = (values * inverse_rms(values) * gains[...]).astype(LOW)


def residual_kernel(tokens, gains, squares, *refs):
    parts, (residual_out, ffn_out, inverse_out) = refs[:-3], refs[-3:]
    width = tokens.shape[1]
    for at in row_steps(tokens.shape[0]):
        inverse = lax.rsqrt(squares[at, :] * (1.0 / width) + EPSILON)
        inverse_out[at, :] = inverse
        residual = tokens[at, :].astype(F32) + summed(parts, at) * inverse
        residual_out[at, :] = residual
        ffn_out[at, :] = (residual * inverse_rms(residual) * gains[...]).astype(LOW)


def grad_residual_kernel(tokens, cotangent, gains, residual_in, inverse_in, *refs):
    parts, (grad_out, low_out) = refs[:-2], refs[-2:]
    width = tokens.shape[1]
    lane = lax.broadcasted_iota(jnp.int32, (ROWS, 128), 1)
    for at in row_steps(tokens.shape[0]):
        residual = residual_in[at, :]
        inverse = inverse_rms(residual)
        normed = residual * inverse
        grad_normed = summed(parts, at) * gains[...]
        mean = jnp.mean(grad_normed * normed, axis=1, keepdims=True)
        grad = cotangent[at, :].astype(F32) + inverse * (grad_normed - normed * mean)
        grad_out[at, :] = grad
        low = grad.astype(LOW)
        low_out[at, :width] = low
        branch = residual - tokens[at, :].astype(F32)
        factors = jnp.zeros((ROWS, 128), F32)
        for i, factor in enumerate(
            (inverse_in[at, :], jnp.mean(low.astype(F32) * branch, axis=1, keepdims=True))
        ):
            high = factor.astype(LOW).astype(F32)
            factors = jnp.where(lane == 2 * i, high, factors)
            factors = jnp.where(lane == 2 * i + 1, factor - high, factors)
        low_out[at, width:] = factors.astype(LOW)


def output_rows_kernel(residual, *refs):
    parts, out = refs[:-1], refs[-1]
    for at in row_steps(residual.shape[0]):
        out[at, :] = (residual[at, :] + summed(parts, at)).astype(LOW)


def grad_tokens_kernel(tokens, gains, grad_residual, *refs):
    parts, out = refs[:-1], refs[-1]
    for at in row_steps(tokens.shape[0]):
        values = tokens[at, :].astype(F32)
        inverse = inverse_rms(values)
        normed = values * inverse
        grad_normed = summed(parts, at) * gains[...]
        mean = jnp.mean(grad_normed * normed, axis=1, keepdims=True)
        out[at, :] = (
            grad_residual[at, :] + inverse * (grad_normed - normed * mean)
        ).astype(LOW)


def core_sum_kernel(rows, mine, other, top_out, end_out, top_keep, end_keep):
    half = rows // 2
    for x in range(2):
        for y in range(2):
            slot = x * 2 + y
            for first in range(0, rows, ROWS):
                at = slice(slot * rows + first, slot * rows + first + ROWS)
                total = mine[at, :].astype(F32) + other[at, :].astype(F32)
                low = total.astype(LOW)
                if first < half:
                    if x:
                        top_out[y * half + first : y * half + first + ROWS, :] = low
                    else:
                        top_keep[y * half + first : y * half + first + ROWS, :] = low
                else:
                    to = x * half + first - half
                    if y:
                        end_out[to : to + ROWS, :] = low
                    else:
                        end_keep[to : to + ROWS, :] = low


def chip_sum_kernel(top, end, top_in, end_in, top_out, end_out, keep):
    half = top.shape[0] // 2
    for i, (mine, other, out) in enumerate(((top, top_in, top_out), (end, end_in, end_out))):
        for first in range(0, half, ROWS):
            at = slice(first, first + ROWS)
            keep[i * half + first : i * half + first + ROWS, :] = mine[at, :].astype(
                F32
            ) + other[at, :].astype(F32)
            at = slice(half + first, half + first + ROWS)
            out[first : first + ROWS, :] = (
                mine[at, :].astype(F32) + other[at, :].astype(F32)
            ).astype(LOW)


class Links:
    def __init__(self, sizes):
        self.sizes = sizes
        self.pairs = sizes["y"] == sizes["core"] == sizes["x"] == 2
        self.plane = ("x", "y", "core")
        self.owners = ("y", "core", "x")

    def place(self, axis):
        return lax.axis_index(axis)

    def slots(self):
        sizes = self.sizes
        x, y, core = jnp.meshgrid(
            jnp.arange(sizes["x"]), jnp.arange(sizes["y"]), jnp.arange(sizes["core"]), indexing="ij"
        )
        if self.pairs:
            x, y, core = x ^ self.place("x"), y ^ self.place("y"), core ^ self.place("core")
            slot = (core * 2 + x) * 2 + y
        else:
            slot = (x * sizes["y"] + y) * sizes["core"] + core
        return slot.reshape(-1).astype(jnp.int32)

    def swap(self, axis, value):
        return lax.ppermute(value, axis, SWAP)

    def rows(self, value, after=()):
        if not self.pairs:
            return [lax.all_gather(value, self.plane, axis=0, tiled=True)]
        half = value.shape[0] // 2
        by_x, by_y = self.swap("x", value), self.swap("y", value)
        top, end = call(
            halves_kernel, "halves", [((half, value.shape[1]), LOW)] * 2, [by_x, by_y], after=after
        )
        own = [value, by_y, by_x, self.swap("y", top), self.swap("x", end)]
        return own + [self.swap("core", piece) for piece in own]

    def sum_cores(self, parts, after=()):
        if not self.pairs:
            return parts
        away, mine = parts
        rows, width = mine.shape[0] // 4, mine.shape[1]
        return call(
            functools.partial(core_sum_kernel, rows),
            "core_sum",
            [((rows, width), LOW)] * 4,
            [mine, self.swap("core", away)],
            cost=(8 * rows * width, 24 * rows * width),
            after=after,
        )

    def sum_chips(self, parts, after=()):
        if not self.pairs:
            return [
                lax.psum_scatter(parts[0], self.plane, scatter_dimension=0, tiled=True).astype(F32)
            ]
        top, end, top_keep, end_keep = parts
        rows, width = top.shape
        top, end, keep = call(
            chip_sum_kernel,
            "chip_sum",
            [((rows // 2, width), LOW)] * 2 + [((rows, width), F32)],
            [top_keep, end_keep, self.swap("x", top), self.swap("y", end)],
            cost=(2 * rows * width, 12 * rows * width),
            after=after,
        )
        return [keep, self.swap("y", top), self.swap("x", end)]

    def sum_rows_small(self, parts):
        parts = lax.all_to_all(parts, self.plane, split_axis=0, concat_axis=0, tiled=True)
        return jnp.sum(parts, axis=0)

    def sum_planes_small(self, value):
        planes = self.sizes["z"]
        if not (self.pairs and planes & (planes - 1) == 0):
            return lax.psum(value, "z")
        step = 1
        while step < planes:
            value = value + lax.ppermute(value, "z", [(i, i ^ step) for i in range(planes)])
            step *= 2
        return value

    def sum_plane_small(self, value):
        if not self.pairs:
            return lax.psum(value, self.plane)
        for axis in ("x", "y", "core"):
            value = value + self.swap(axis, value)
        return value

    def exchange(self, value):
        return lax.all_to_all(value, self.owners, split_axis=0, concat_axis=0, tiled=True)

    def ring(self, value):
        planes = self.sizes["z"]

        def shift(value, by):
            return lax.ppermute(value, "z", [(i, (i + by) % planes) for i in range(planes)])

        up, down = [value], []
        while 1 + len(up) + len(down) <= planes:
            up.append(shift(up[-1], 1))
            if 1 + len(up) + len(down) <= planes:
                down.insert(0, shift(down[0] if down else value, -1))
        return up + down

    def sum_planes(self, value):
        return lax.psum_scatter(value, "z", scatter_dimension=0, tiled=True)

    def both_x(self, value):
        if self.sizes["x"] == 1:
            return value
        if self.sizes["x"] != 2:
            return lax.all_gather(value, "x", axis=0, tiled=True)
        other = self.swap("x", value)
        return jnp.where(
            self.place("x") == 0,
            jnp.concatenate([value, other], axis=0),
            jnp.concatenate([other, value], axis=0),
        )


def on_device(
    sizes,
    tokens,
    doc_lengths,
    w_in,
    w_forget,
    w_gate_out,
    w_out,
    w_gate,
    w_up,
    w_down,
    g_mix,
    g_out,
    g_ffn,
    floor_logit,
    cotangent,
):
    links = Links(sizes)
    tokens, cotangent = tokens[0], cotangent[0]
    row_count, width = tokens.shape
    block = w_in.shape[0]
    hidden = w_gate.shape[1]
    layout = Layout(sizes, row_count, block, hidden)
    seq, planes, buckets, parts = layout.seq, layout.planes, layout.buckets, layout.parts
    slab = width // parts
    seq_place = links.place("y") * sizes["core"] + links.place("core")
    x_place, z_place = links.place("x"), links.place("z")
    owner = (seq_place * planes + z_place) * buckets + x_place
    place = z_place.astype(jnp.int32).reshape(1)
    wide, low_wide = ((row_count, width), F32), ((row_count, width), LOW)
    column = ((row_count, 1), F32)
    row_cost = (20 * row_count * width, 8 * row_count * width)

    def own_channels(vector):
        return lax.dynamic_index_in_dim(
            lax.dynamic_index_in_dim(
                vector.reshape(-1, seq, planes, buckets, block), seq_place, 1, keepdims=False
            ),
            x_place,
            2,
            keepdims=False,
        ).reshape(-1, slab)

    def to_hidden(first, size, after):
        return call(
            functools.partial(to_hidden_kernel, layout, first, size),
            "to_hidden",
            [((parts, block, -(-3 * size // 128) * 128), LOW)],
            [w_gate, w_up, w_down],
            after=after,
        )[0]

    def gather_weights(weight, ring=True):
        weight = weight.reshape(parts * block, -1)
        if layout.pieces and ring:
            return links.ring(weight)
        if layout.pieces:
            return [lax.all_gather(weight, "z", axis=0, tiled=True)]
        full = lax.all_gather(weight, "z", axis=0)
        full = full.reshape(planes, seq, layout.strip, -1)
        return [jnp.swapaxes(full, 0, 1).reshape(width, -1)]

    def gather_channels(weight):
        if layout.pieces:
            return links.ring(weight)
        return [lax.all_gather(weight, "z", axis=0, tiled=True)]

    def scatter_weights(grads):
        if not layout.pieces:
            grads = grads.reshape(seq, planes, layout.strip, -1)
            grads = jnp.swapaxes(grads, 0, 1).reshape(width, -1)
        return links.sum_planes(grads).reshape(parts, block, -1)

    (mixer,) = call(
        functools.partial(to_channels_kernel, layout),
        "to_channels",
        [((parts, block, 3 * slab), LOW)],
        [w_in, w_forget, w_gate_out],
    )
    vectors = jnp.stack([g_mix, g_ffn, g_out, floor_logit]).astype(F32)
    vectors = links.sum_planes_small(
        lax.dynamic_update_slice(jnp.zeros((4, width), F32), vectors, (0, owner * block))
    )
    mixer = gather_weights(hold(links.exchange(mixer), [vectors]))
    vectors = links.sum_plane_small(vectors)
    out_weights = [lax.all_gather(w_out, "z", axis=0, tiled=True)]
    gain_mix, gain_ffn = vectors[0:1], vectors[1:2]
    own_vectors = own_channels(vectors[2:])
    gain_out = own_vectors[0:1]
    floors = jax.nn.sigmoid(own_vectors[1:2])
    slots = links.slots()
    ends = links.both_x(jnp.cumsum(doc_lengths, axis=1).astype(jnp.int32))

    (mixed,) = call(
        norm_kernel, "mixed_in", [low_wide], [tokens, gain_mix], cost=row_cost
    )
    first = links.exchange(to_hidden(0, layout.split, [mixed, *out_weights]))
    mixed = links.rows(mixed)
    first = gather_weights(hold(first, [*mixer[1:2], *mixer[-1:], *mixed[3:5]]), False)
    second = links.exchange(to_hidden(layout.split, layout.rest, mixer[1:2] + mixer[-1:]))
    early = [second]
    second = gather_weights(second, False)
    grads_all = links.rows(hold(cotangent, early))
    forget, floor_term, slope_forget, slope_input, gate_pre, states, scaled, squares = (
        mixer_forward(layout, slots, ends, place, floors, gain_out, mixed, mixer, early)
    )
    squares = links.sum_rows_small(squares).reshape(row_count, 1)
    branch = branch_parts(layout, place, scaled, out_weights, grads_all[1:3])
    branch = links.sum_cores(branch, grads_all[3:5])
    branch = links.sum_chips(branch)
    residual, ffn, inverse_h = call(
        residual_kernel,
        "residual",
        [wide, low_wide, column],
        [tokens, gain_ffn, squares, *branch],
        cost=row_cost,
    )

    ffn = links.rows(ffn)
    first_acts, first_grads = glu_first(layout, place, ffn, grads_all, first)
    first_grads = scatter_weights(first_grads)
    second_acts, *ffn_parts = glu_second(
        layout, place, ffn, grads_all, first, second, first_acts
    )
    ffn_parts = links.sum_cores(ffn_parts)
    second_grads = glu_third(layout, place, ffn, grads_all, second_acts, [])
    grad_ffn = links.sum_chips(ffn_parts, [second_grads])
    second_grads = scatter_weights(second_grads)
    grad_residual, grad_low = call(
        grad_residual_kernel,
        "grad_residual",
        [wide, ((row_count, width + 128), LOW)],
        [tokens, cotangent, gain_ffn, residual, inverse_h, *grad_ffn],
        cost=row_cost,
    )
    out_parts = output_parts(
        layout, place, first, second, first_acts, second_acts, width, []
    )

    grads_low = links.rows(grad_low, out_parts[:1])
    saved = [gate_pre, states, forget, floor_term, slope_forget, slope_input]
    mixer_grads, out_grads, mixer_weight_grads = mixer_backward(
        layout,
        slots,
        place,
        gain_out,
        saved,
        grads_low,
        out_weights,
        mixed,
        [],
    )
    mixer_weight_grads = scatter_weights(mixer_weight_grads)
    out_grads = links.sum_planes(out_grads)
    mixed_parts = links.sum_cores(
        mixed_grad_parts(layout, place, mixer_grads, mixer, width, [])
    )
    grad_mixed = links.sum_chips(mixed_parts)
    (grad_tokens,) = call(
        grad_tokens_kernel,
        "grad_tokens",
        [low_wide],
        [tokens, gain_mix, grad_residual, *grad_mixed],
        cost=row_cost,
    )
    output = links.sum_chips(links.sum_cores(out_parts, [grad_tokens]))
    (output,) = call(
        output_rows_kernel, "output_rows", [low_wide], [residual, *output], cost=row_cost
    )
    first_grads = links.exchange(hold(first_grads, [grad_tokens]))
    second_grads = links.exchange(hold(second_grads, [output]))
    mixer_weight_grads = links.exchange(mixer_weight_grads)

    def as_column(vector):
        return vector.astype(F32).reshape(block, 1)

    square, long, single = ((block, width), F32), ((block, hidden), F32), ((block, 1), F32)
    gate_w, up_w, down_w, grad_g_ffn = call(
        functools.partial(from_hidden_kernel, layout),
        "from_hidden",
        [long] * 3 + [single],
        [first_grads, second_grads, as_column(g_ffn), w_gate, w_up],
    )
    out_w, grad_g_out, grad_floor = call(
        channel_gain_kernel,
        "from_out",
        [square, single, single],
        [out_grads, w_out, as_column(g_out), as_column(floor_logit)],
    )
    in_w, forget_w, gate_out_w, grad_g_mix = call(
        functools.partial(from_channels_kernel, layout),
        "from_channels",
        [square] * 3 + [single],
        [mixer_weight_grads, as_column(g_mix), w_in, w_forget, w_gate_out],
    )
    return (
        output[None],
        grad_tokens[None],
        in_w,
        forget_w,
        gate_out_w,
        out_w,
        gate_w,
        up_w,
        down_w,
        grad_g_mix.reshape(block),
        grad_g_out.reshape(block),
        grad_g_ffn.reshape(block),
        grad_floor.reshape(block),
    )


def solution(mesh):
    seq, dp = mesh.shape["seq"], mesh.shape["dp"]
    core = 2 if seq % 2 == 0 else 1
    x = max(1, TENSOR_PARTS // seq)
    if dp % x:
        x = 1
    sizes = {"y": seq // core, "core": core, "z": dp // x, "x": x}
    split = Mesh(mesh.devices.reshape(tuple(sizes.values())), tuple(sizes))
    rows = P(("z", "x"), ("y", "core"), None)
    lengths = P(("z", "x"), None)
    matrix = P(("y", "core", "z", "x"), None)
    vector = P(("y", "core", "z", "x"))
    return jax.shard_map(
        functools.partial(on_device, sizes),
        mesh=split,
        in_specs=(rows, lengths) + (matrix,) * 7 + (vector,) * 4 + (rows,),
        out_specs=(rows, rows) + (matrix,) * 7 + (vector,) * 4,
        check_vma=False,
    )
```

time: 776 us -> 616 us (0.79)
  Pallas kernels: 15.4 us -> 173 us
  local copies, waits for them, and re-layouts: 194 us -> 51.5 us
  matrix products: 123 us -> 0 us
  other arithmetic: 70.2 us -> 4.96 us
  waiting for transfers between devices: 221 us -> 279 us
  blocking collectives: 30.9 us -> 9.59 us
  starting transfers between devices: 94.3 us -> 74.3 us
    pallas_call x2 -> x36, Pallas kernels: 15.4 us -> 173 us  [call(): pl.pallas_call(kernel, out_shape=tuple((jax.ShapeDtypeStruct(*out) for ou...]
    dot_general x15 -> x0, matrix products: 123 us -> none  [the longest x5 44.8 us: product(): return jnp.dot(left_op, right_op, preferred_element_type=F32).astype(kind)]
    ppermute x61 -> x60, waiting for transfers between devices: 142 us -> 214 us  [swap(): return lax.ppermute(value, axis, SWAP)]
    all_gather x5 -> x3, waiting for transfers between devices: 59.4 us -> 0.02 us  [the longest x2 0.02 us: gather_weights(): return [lax.all_gather(weight, 'z', axis=0, tiled=True)]]
    concatenate x22 -> x0, local copies, waits for them, and re-layouts: 48.8 us -> none  [the longest x14 27.6 us: sum_rows(): jnp.concatenate([top[0] + top_in.astype(F32), end[0] + end_in.astype(F32)...]
    convert_element_type x31 -> x0, local copies, waits for them, and re-layouts: 43.3 us -> none  [the longest x6 17.5 us: on_device(): grad_gate_w, grad_up_w, grad_down_w = (from_hidden(links.exchange(links.s...]
    ppermute x4 -> x5, waiting for transfers between devices: 5.74 us -> 44.2 us  [the longest x3 37 us: shift(): lax.ppermute(value, 'z', [(i, (i + by) % planes) for i in range(planes)])]
    convert_element_type x9 -> x0, other arithmetic: 25 us -> none  [the longest x4 16 us: sum_rows(): (parts[0].astype(F32) + other.astype(F32)).astype(kind)]
  transfers between devices with their start and end apart: 81 -> 78, of which waited for: 36 -> 41; matrix products, arithmetic and copies ran while one was open for 44% -> 1% of each run, Pallas kernels for 2% -> 28%
where the time goes in v2:
time: 616 us; the launch traced here: 608 us
  waiting for transfers between devices  279 us (45%)
  Pallas kernels  173 us (28%)
  starting transfers between devices  74.3 us (12%)
  local copies, waits for them, and re-layouts  51.5 us (8%)
  between operations  15.4 us (2%)
  blocking collectives  9.59 us (2%)
    ppermute x60, waiting for transfers between devices, swap(): return lax.ppermute(value, axis, SWAP)  214 us
    pallas_call x36, Pallas kernels, call(): pl.pallas_call(kernel, out_shape=tuple((jax.ShapeDtypeStruct(*out) for ou...  173 us
    unnamed x180, local copies, waits for them, and re-layouts  48.7 us
    ppermute x60, starting transfers between devices, swap(): return lax.ppermute(value, axis, SWAP)  44.7 us
    ppermute x3, waiting for transfers between devices, shift(): lax.ppermute(value, 'z', [(i, (i + by) % planes) for i in range(planes)])  37 us
    all_to_all x6, starting transfers between devices, exchange(): lax.all_to_all(value, self.owners, split_axis=0, concat_axis=0, tiled=True)  23.5 us
    all_to_all x6, waiting for transfers between devices, exchange(): lax.all_to_all(value, self.owners, split_axis=0, concat_axis=0, tiled=True)  19 us
  transfers between devices with their start and end apart: 78, of which 41 were waited for; matrix products, arithmetic and copies ran while one was open for 1% of the time, Pallas kernels for 28%

profile of v2, /device:TPU:16, one launch (start us, length us, event | category | flops | bytes accessed | tf_op | source)
XLA Modules:
  0.0 607.6 jit_solution(1639854355509377983)
XLA Ops:
  10.5 2.3 collective-permute-done
  13.8 4.8 collective-permute-done.1
  24.6 3.7 all-to-all-start
  28.3 2.0 collective-permute-start.3
  30.3 10.3 %collective-permute-done.3 = f32[4,2048]{1,0:T(4,128)S(1)} collective-permute-done((f32[4,2048]{1,0:T(4,128)S(1)}, f32[4,2048]{1,0:T(4,128)S(1)}, u32[]{:S(2)}, u32[]{:S(2)}) %collective-permute-start.3) | collective-permute-done | bytes 32800 | tf_op jit(solution)/shard_map/ppermute | solution.py:1093
  49.6 3.6 all-to-all-start.3
  56.5 7.3 %collective-permute-done.7.by_x.refs_7_.refs_19_ = bf16[192,2048]{1,0:T(8,128)(2,1)} collective-permute-done((bf16[192,2048]{1,0:T(8,128)(2,1)}, bf16[192,2048]{1,0:T(8,128)(2,1)}, u32[]{:S(2)}, u32[]{:S(2)}) %collective-permute-start.7) | collective-permute-done | bytes 786464 | tf_op jit(solution)/shard_map/ppermute | solution.py:1093
  68.0 17.1 %collective-permute-done.8.refs_8_.refs_3_.refs_20_ = bf16[96,2048]{1,0:T(8,128)(2,1)S(1)} collective-permute-done((bf16[96,2048]{1,0:T(8,128)(2,1)S(1)}, bf16[96,2048]{1,0:T(8,128)(2,1)S(1)}, u32[]{:S(2)}, u32[]{:S(2)}) %collective-permute-start.8) | collective-permute-done | bytes 393248 | tf_op jit(solution)/shard_map/ppermute | solution.py:1093
  87.5 3.7 collective-permute-done.15.refs_3_.refs_16_.refs_1_
  102.2 4.0 all-to-all-start.1
  110.7 9.9 %collective-permute-done.5 = s32[1,4]{1,0:T(1,128)S(1)} collective-permute-done((s32[1,4]{1,0:T(1,128)S(1)}, s32[1,4]{1,0:T(1,128)S(1)}, u32[]{:S(2)}, u32[]{:S(2)}) %collective-permute-start.5) | collective-permute-done | bytes 48 | tf_op jit(solution)/shard_map/ppermute | solution.py:1093
  128.4 33.3 %collective-permute-done.16.refs_17_.refs_2_ = bf16[512,768]{1,0:T(8,128)(2,1)} collective-permute-done((bf16[512,768]{1,0:T(8,128)(2,1)}, bf16[512,768]{1,0:T(8,128)(2,1)}, u32[]{:S(2)}, u32[]{:S(2)}) %collective-permute-start.16) | collective-permute-done | bytes 786464 | tf_op jit(solution)/shard_map/ppermute | solution.py:1165
  161.7 16.2 %mixer_forward.1 = (f32[1536,256]{1,0:T(8,128)}, f32[1536,256]{1,0:T(8,128)}, f32[1536,256]{1,0:T(8,128)}, f32[1536,256]{1,0:T(8,128)}, f32[1536,256]{1,0:T(8,12...) custom-call(s32[8]{0:T(128)} %add.84.refs_0_.slots, s32[2,4]{1,0:T(2,128)} %add_select_fusion.refs_1_, ...), custom_call_target="tpu_custom_call" | custom-call | flops 4831838208 | bytes 18874368 | tf_op jit(solution)/shard_map/mixer_forward/pallas_call | solution.py:73
  177.9 5.9 branch_parts.1
  188.8 8.3 %collective-permute-done.21.refs_2_.refs_13_ = bf16[96,2048]{1,0:T(8,128)(2,1)S(1)} collective-permute-done((bf16[96,2048]{1,0:T(8,128)(2,1)S(1)}, bf16[96,2048]{1,0:T(8,128)(2,1)S(1)}, u32[]{:S(2)}, u32[]{:S(2)}) %collective-permute-start.21) | collective-permute-done | bytes 393248 | tf_op jit(solution)/shard_map/ppermute | solution.py:1093
  198.4 2.0 copy-done.14
  200.5 2.6 core_sum.4
  205.2 16.7 %collective-permute-done.23.top_in = bf16[192,2048]{1,0:T(8,128)(2,1)S(1)} collective-permute-done((bf16[192,2048]{1,0:T(8,128)(2,1)S(1)}, bf16[192,2048]{1,0:T(8,128)(2,1)S(1)}, u32[]{:S(2)}, u32[]{:S(2)}) %collective-permute-start.23) | collective-permute-done | bytes 786464 | tf_op jit(solution)/shard_map/ppermute | solution.py:1093
  226.7 9.6 %all_to_all.39 = f32[8,1,192]{2,1,0:T(1,128)S(1)} all-to-all(f32[8,1,192]{2,1,0:T(1,128)S(1)} %copy.36), channel_id=1, replica_groups=mesh['y'=2,'core'=2,'z'=4,'x'=2] {'x','y','core'}, dimensions={0} | all-to-all | bytes 12288 | tf_op jit(solution)/shard_map/all_to_all | solution.py:1138
  242.8 17.3 %collective-permute-done.28.by_x.refs_2_ = bf16[192,2048]{1,0:T(8,128)(2,1)S(1)} collective-permute-done((bf16[192,2048]{1,0:T(8,128)(2,1)S(1)}, bf16[192,2048]{1,0:T(8,128)(2,1)S(1)}, u32[]{:S(2)}, u32[]{:S(2)}) %collective-permute-start.28) | collective-permute-done | bytes 786464 | tf_op jit(solution)/shard_map/ppermute | solution.py:1093
  264.2 8.4 %collective-permute-done.29.refs_3_ = bf16[96,2048]{1,0:T(8,128)(2,1)S(1)} collective-permute-done((bf16[96,2048]{1,0:T(8,128)(2,1)S(1)}, bf16[96,2048]{1,0:T(8,128)(2,1)S(1)}, u32[]{:S(2)}, u32[]{:S(2)}) %collective-permute-start.29) | collective-permute-done | bytes 393248 | tf_op jit(solution)/shard_map/ppermute | solution.py:1093
  276.5 24.9 %glu_first.1 = (bf16[1536,1152]{1,0:T(8,128)(2,1)}, bf16[2048,1152]{1,0:T(8,128)(2,1)}) custom-call(s32[1]{0:T(128)} %bitcast.5.refs_2_.refs_0_.place, bf16[192,2048]{1,0:T(8,128)(2,1)} %copy-done.65, bf16[192,2048]{1,0:T(8,128)(2,1)} %copy-done.51, bf16[192,2048]{1,0:T(8,128)(2,1)} %copy-done.50, bf16[96,2048]{1,0:T(8,128)(2,1)} %copy-done.85, ...), custom_call_target="tpu_custom_call" | custom-call | flops 14495514624 | bytes 22020096 | tf_op jit(solution)/shard_map/glu_first/pallas_call | solution.py:73
  301.5 27.6 %glu_second.1 = (bf16[1536,1024]{1,0:T(8,128)(2,1)}, bf16[768,2048]{1,0:T(8,128)(2,1)}, bf16[768,2048]{1,0:T(8,128)(2,1)}) custom-call(s32[1]{0:T(128)} %bitcast.5.refs_2_.refs_0_.place, bf16[192,2048]{1,0:T(8,128)(2,1)} %copy-done.65, bf16[192,2048]{1,0:T(8,128)(2,1)} %copy-done.51, bf16[192,2048]{1,0:T(8,128)(2,1)} %copy-done.50, ...), custom_call_target="tpu_custom_call" | custom-call | flops 16106127360 | bytes 27262976 | tf_op jit(solution)/shard_map/glu_second/pallas_call | solution.py:73
  329.1 15.8 %glu_third.1.refs_4_ = bf16[2048,1024]{1,0:T(8,128)(2,1)} custom-call(s32[1]{0:T(128)} %bitcast.5.refs_2_.refs_0_.place, bf16[192,2048]{1,0:T(8,128)(2,1)} %copy-done.65, bf16[192,2048]{1,0:T(8,128)(2,1)} %copy-done.51, bf16[192,2048]{1,0:T(8,128)(2,1)} %copy-done.50, bf16[96,2048]{1,0:T(8,128)(2,1)} %copy-done.85, bf16[96,2048]{1,0:T(8,128)(2,1)} %copy-done.86, ...), custom_call_target="tpu_custom_call" | custom-call | flops 6442450944 | bytes 16777216 | tf_op jit(solution)/shard_map/glu_third/pallas_call | solution.py:73
  345.4 5.8 collective-permute-done.42.other
  356.1 17.4 %collective-permute-done.43.refs_2_ = bf16[192,2048]{1,0:T(8,128)(2,1)S(1)} collective-permute-done((bf16[192,2048]{1,0:T(8,128)(2,1)S(1)}, bf16[192,2048]{1,0:T(8,128)(2,1)S(1)}, u32[]{:S(2)}, u32[]{:S(2)}) %collective-permute-start.43) | collective-permute-done | bytes 786464 | tf_op jit(solution)/shard_map/ppermute | solution.py:1093
  376.8 8.6 %collective-permute-done.45.refs_1_ = bf16[96,2048]{1,0:T(8,128)(2,1)S(1)} collective-permute-done((bf16[96,2048]{1,0:T(8,128)(2,1)S(1)}, bf16[96,2048]{1,0:T(8,128)(2,1)S(1)}, u32[]{:S(2)}, u32[]{:S(2)}) %collective-permute-start.45) | collective-permute-done | bytes 393248 | tf_op jit(solution)/shard_map/ppermute | solution.py:1093
  390.2 11.2 %output_parts.1 = (bf16[768,2048]{1,0:T(8,128)(2,1)}, bf16[768,2048]{1,0:T(8,128)(2,1)}) custom-call(s32[1]{0:T(128)} %bitcast.5.refs_2_.refs_0_.place, bf16[2048,1152]{1,0:T(8,128)(2,1)} %all-gather.6.cloned.1.call-done.refs_20_.refs_0_, bf16[2048,1024]{1,0:T(8,128)(2,1)} %all-gather.8.cloned.1.call-done.refs_21_.refs_1_, ...), custom_call_target="tpu_custom_call" | custom-call | flops 4831838208 | bytes 9437184 | tf_op jit(solution)/shard_map/output_parts/pallas_call | solution.py:73
  401.6 5.2 collective-permute-done.48.refs_0_.refs_8_
  407.2 2.2 copy-done.21
  412.5 5.7 collective-permute-done.49.refs_9_
  418.2 4.8 collective-permute-done.50.refs_10_
  425.8 29.4 %mixer_backward.1 = (bf16[1536,768]{1,0:T(8,128)(2,1)}, bf16[256,2176]{1,0:T(8,128)(2,1)}, bf16[2048,768]{1,0:T(8,128)(2,1)}) custom-call(s32[8]{0:T(128)} %add.84.refs_0_.slots, s32[1]{0:T(128)} %bitcast.5.refs_2_.refs_0_.place, f32[1,256]{1,0:T(1,128)} %slice.23.refs_4_.gains, f32[1536,256]{1,0:T(8,128)} %get-tuple-element.121.refs_0_, ...), custom_call_target="tpu_custom_call" | custom-call | flops 8053063680 | bytes 28573696 | tf_op jit(solution)/shard_map/mixer_backward/pallas_call | solution.py:73
  455.2 10.7 %mixed_grad_parts.1 = (bf16[768,2048]{1,0:T(8,128)(2,1)}, bf16[768,2048]{1,0:T(8,128)(2,1)}) custom-call(s32[1]{0:T(128)} %bitcast.5.refs_2_.refs_0_.place, bf16[1536,768]{1,0:T(8,128)(2,1)} %get-tuple-element.130.grads, bf16[512,768]{1,0:T(8,128)(2,1)} %bitcast.43, bf16[512,768]{1,0:T(8,128)(2,1)} %copy-done.18, ...), custom_call_target="tpu_custom_call" | custom-call | flops 4831838208 | bytes 12582912 | tf_op jit(solution)/shard_map/mixed_grad_parts/pallas_call | solution.py:73
  466.4 8.7 %collective-permute-done.56.other = bf16[768,2048]{1,0:T(8,128)(2,1)S(1)} collective-permute-done((bf16[768,2048]{1,0:T(8,128)(2,1)}, bf16[768,2048]{1,0:T(8,128)(2,1)S(1)}, u32[]{:S(2)}, u32[]{:S(2)}) %collective-permute-start.56) | collective-permute-done | bytes 3145760 | tf_op jit(solution)/shard_map/ppermute | solution.py:1093
  475.1 2.2 copy-done.24
  479.6 18.1 %collective-permute-done.57.top_in = bf16[192,2048]{1,0:T(8,128)(2,1)S(1)} collective-permute-done((bf16[192,2048]{1,0:T(8,128)(2,1)S(1)}, bf16[192,2048]{1,0:T(8,128)(2,1)S(1)}, u32[]{:S(2)}, u32[]{:S(2)}) %collective-permute-start.57) | collective-permute-done | bytes 786464 | tf_op jit(solution)/shard_map/ppermute | solution.py:1093
  500.2 9.3 %collective-permute-done.59.refs_1_ = bf16[96,2048]{1,0:T(8,128)(2,1)S(1)} collective-permute-done((bf16[96,2048]{1,0:T(8,128)(2,1)S(1)}, bf16[96,2048]{1,0:T(8,128)(2,1)S(1)}, u32[]{:S(2)}, u32[]{:S(2)}) %collective-permute-start.59) | collective-permute-done | bytes 393248 | tf_op jit(solution)/shard_map/ppermute | solution.py:1093
  521.1 3.7 all-to-all-start.5
  525.6 11.9 %collective-permute-done.61.top_in = bf16[192,2048]{1,0:T(8,128)(2,1)} collective-permute-done((bf16[192,2048]{1,0:T(8,128)(2,1)}, bf16[192,2048]{1,0:T(8,128)(2,1)}, u32[]{:S(2)}, u32[]{:S(2)}) %collective-permute-start.61) | collective-permute-done | bytes 786464 | tf_op jit(solution)/shard_map/ppermute | solution.py:1093
  544.2 4.6 collective-permute-start.64
  548.7 7.0 %collective-permute-done.63.refs_1_ = bf16[96,2048]{1,0:T(8,128)(2,1)S(1)} collective-permute-done((bf16[96,2048]{1,0:T(8,128)(2,1)S(1)}, bf16[96,2048]{1,0:T(8,128)(2,1)S(1)}, u32[]{:S(2)}, u32[]{:S(2)}) %collective-permute-start.63) | collective-permute-done | bytes 393248 | tf_op jit(solution)/shard_map/ppermute | solution.py:1093
  560.3 4.4 all-to-all-start.6
  564.8 14.9 %all-to-all-done.6.second = bf16[8,64,1024]{2,1,0:T(8,128)(2,1)} async-done(((bf16[8,64,1024]{2,1,0:T(8,128)(2,1)}), bf16[8,64,1024]{2,1,0:T(8,128)(2,1)}, u32[]{:S(2)}, u32[]{:S(2)}) %all-to-all-start.6) | async-done | bytes 1048608 | tf_op jit(solution)/shard_map/all_to_all | solution.py:1159
  579.7 4.2 all-to-all-start.4
  587.4 3.9 from_hidden.1
  591.9 4.0 all-to-all-done.4.grads
  597.0 2.7 from_channels.1
  (368 shorter events, 134.2 us)
Async XLA Ops:
  7.2 37.9 %all-gather.4.cloned.1.call-start = ((), (), s32[]{:S(2)}) async-start(), calls=%async_computation.11 | async-start | bytes 1310720 | tf_op jit(solution)/shard_map/all_gather | solution.py:1275
  24.6 24.1 %all-to-all-start = ((bf16[8,64,768]{2,1,0:T(8,128)(2,1)}), bf16[8,64,768]{2,1,0:T(8,128)(2,1)S(1)}, u32[]{:S(2)}, u32[]{:S(2)}) async-start(bf16[8,64,768]{2,1,0:T(8,128)(2,1)} %copy-done.28), calls=%async_computation | async-start | bytes 1572864 | tf_op jit(solution)/shard_map/all_to_all | solution.py:1159
  28.3 12.2 %collective-permute-start.3 = (f32[4,2048]{1,0:T(4,128)S(1)}, f32[4,2048]{1,0:T(4,128)S(1)}, u32[]{:S(2)}, u32[]{:S(2)}) collective-permute-start(f32[4,2048]{1,0:T(4,128)S(1)} %add.79), channel_id=1, source_target_pairs={{0,16},{16,0},{1,17},{17,1},{2,18},{18,2},{3,19},{19,3},{4,20},{20... | collective-permute-start | bytes 98312 | tf_op jit(solution)/shard_map/ppermute | solution.py:1093
  43.0 20.7 %collective-permute-start.7 = (bf16[192,2048]{1,0:T(8,128)(2,1)}, bf16[192,2048]{1,0:T(8,128)(2,1)}, u32[]{:S(2)}, u32[]{:S(2)}) collective-permute-start(bf16[192,2048]{1,0:T(8,128)(2,1)} %mixed_in.1.refs_5_.refs_3_.refs_17_), channel_id=1, source_target_pairs={{0,1},{1,0},{2,3},{3,2},{4,5},{5,4},{6,7},{7,6},{8,9},{9,8},{10,11... | collective-permute-start | bytes 2359304 | tf_op jit(solution)/shard_map/ppermute | solution.py:1093
  44.5 20.9 %collective-permute-start.6 = (bf16[192,2048]{1,0:T(8,128)(2,1)}, bf16[192,2048]{1,0:T(8,128)(2,1)}, u32[]{:S(2)}, u32[]{:S(2)}) collective-permute-start(bf16[192,2048]{1,0:T(8,128)(2,1)} %mixed_in.1.refs_5_.refs_3_.refs_17_), channel_id=1, source_target_pairs={{0,16},{16,0},{1,17},{17,1},{2,18},{18,2},{3,19},{19,3},{4,20},{20... | collective-permute-start | bytes 2359304 | tf_op jit(solution)/shard_map/ppermute | solution.py:1093
  49.6 42.6 %all-to-all-start.3 = ((bf16[8,64,1152]{2,1,0:T(8,128)(2,1)}), bf16[8,64,1152]{2,1,0:T(8,128)(2,1)S(1)}, u32[]{:S(2)}, u32[]{:S(2)}) async-start(bf16[8,64,1152]{2,1,0:T(8,128)(2,1)} %to_hidden.3), calls=%async_computation.3 | async-start | bytes 2359296 | tf_op jit(solution)/shard_map/all_to_all | solution.py:1159
  53.1 223.3 %all-gather.6.cloned.1.call-start = ((), (), s32[]{:S(2)}) async-start(), calls=%async_computation.12 | async-start | bytes 5898240 | tf_op jit(solution)/shard_map/all_gather | solution.py:1247
  54.4 32.2 %collective-permute-start.17 = (bf16[512,768]{1,0:T(8,128)(2,1)S(1)}, bf16[512,768]{1,0:T(8,128)(2,1)S(1)}, u32[]{:S(2)}, u32[]{:S(2)}) collective-permute-start(bf16[512,768]{1,0:T(8,128)(2,1)S(1)} %bitcast.40), channel_id=1, source_target_pairs={{0,6},{2,0},{4,2},{6,4},{1,7},{3,1},{5,3},{7,5},{8,14},{10,8},{12,... | collective-permute-start | bytes 2359304 | tf_op jit(solution)/shard_map/ppermute | solution.py:1165
  54.9 36.4 %collective-permute-start.15 = (bf16[512,768]{1,0:T(8,128)(2,1)S(1)}, bf16[512,768]{1,0:T(8,128)(2,1)S(1)}, u32[]{:S(2)}, u32[]{:S(2)}) collective-permute-start(bf16[512,768]{1,0:T(8,128)(2,1)S(1)} %bitcast.41), channel_id=1, source_target_pairs={{0,2},{2,4},{4,6},{6,0},{1,3},{3,5},{5,7},{7,1},{8,10},{10,12},{12... | collective-permute-start | bytes 2359304 | tf_op jit(solution)/shard_map/ppermute | solution.py:1165
  66.8 18.3 %collective-permute-start.8 = (bf16[96,2048]{1,0:T(8,128)(2,1)S(1)}, bf16[96,2048]{1,0:T(8,128)(2,1)S(1)}, u32[]{:S(2)}, u32[]{:S(2)}) collective-permute-start(bf16[96,2048]{1,0:T(8,128)(2,1)S(1)} %get-tuple-element.87), channel_id=1, source_target_pairs={{0,16},{16,0},{1,17},{17,1},{2,18},{18,2},{3,19},{19,3},{4,20},{20... | collective-permute-start | bytes 1179656 | tf_op jit(solution)/shard_map/ppermute | solution.py:1093
  67.3 18.6 %collective-permute-start.9 = (bf16[96,2048]{1,0:T(8,128)(2,1)S(1)}, bf16[96,2048]{1,0:T(8,128)(2,1)S(1)}, u32[]{:S(2)}, u32[]{:S(2)}) collective-permute-start(bf16[96,2048]{1,0:T(8,128)(2,1)S(1)} %get-tuple-element.88), channel_id=1, source_target_pairs={{0,1},{1,0},{2,3},{3,2},{4,5},{5,4},{6,7},{7,6},{8,9},{9,8},{10,11... | collective-permute-start | bytes 1179656 | tf_op jit(solution)/shard_map/ppermute | solution.py:1093
  102.2 19.0 %all-to-all-start.1 = ((bf16[8,64,1024]{2,1,0:T(8,128)(2,1)}), bf16[8,64,1024]{2,1,0:T(8,128)(2,1)S(1)}, u32[]{:S(2)}, u32[]{:S(2)}) async-start(bf16[8,64,1024]{2,1,0:T(8,128)(2,1)} %copy-done.11), calls=%async_computation.1 | async-start | bytes 2097152 | tf_op jit(solution)/shard_map/all_to_all | solution.py:1159
  106.2 195.3 %all-gather.8.cloned.1.call-start = ((), (), s32[]{:S(2)}) async-start(), calls=%async_computation.13 | async-start | bytes 5242880 | tf_op jit(solution)/shard_map/all_gather | solution.py:1247
  106.2 14.5 %collective-permute-start.10 = (bf16[192,2048]{1,0:T(8,128)(2,1)}, bf16[192,2048]{1,0:T(8,128)(2,1)}, u32[]{:S(2)}, u32[]{:S(2)}) collective-permute-start(bf16[192,2048]{1,0:T(8,128)(2,1)} %mixed_in.1.refs_5_.refs_3_.refs_17_), channel_id=1, source_target_pairs={{0,8},{8,0},{1,9},{9,1},{2,10},{10,2},{3,11},{11,3},{4,12},{12,4},... | collective-permute-start | bytes 2359304 | tf_op jit(solution)/shard_map/ppermute | solution.py:1093
  106.7 17.0 %collective-permute-start.12 = (bf16[192,2048]{1,0:T(8,128)(2,1)}, bf16[192,2048]{1,0:T(8,128)(2,1)}, u32[]{:S(2)}, u32[]{:S(2)}) collective-permute-start(bf16[192,2048]{1,0:T(8,128)(2,1)} %collective-permute-done.7.by_x.refs_7_.refs_19_), channel_id=1, source_target_pairs={{0,8},{8,0},{1,9},{9,1},{2,10},{10,2},{3,11},{11,3},{4,12},{12,4},... | collective-permute-start | bytes 2359304 | tf_op jit(solution)/shard_map/ppermute | solution.py:1093
  106.8 21.6 %collective-permute-start.11 = (bf16[192,2048]{1,0:T(8,128)(2,1)}, bf16[192,2048]{1,0:T(8,128)(2,1)}, u32[]{:S(2)}, u32[]{:S(2)}) collective-permute-start(bf16[192,2048]{1,0:T(8,128)(2,1)} %collective-permute-done.6.by_y.refs_6_.refs_18_), channel_id=1, source_target_pairs={{0,8},{8,0},{1,9},{9,1},{2,10},{10,2},{3,11},{11,3},{4,12},{12,4},... | collective-permute-start | bytes 2359304 | tf_op jit(solution)/shard_map/ppermute | solution.py:1093
  107.2 54.5 %collective-permute-start.16 = (bf16[512,768]{1,0:T(8,128)(2,1)}, bf16[512,768]{1,0:T(8,128)(2,1)}, u32[]{:S(2)}, u32[]{:S(2)}) collective-permute-start(bf16[512,768]{1,0:T(8,128)(2,1)} %copy-done.18), channel_id=1, source_target_pairs={{0,2},{2,4},{4,6},{6,0},{1,3},{3,5},{5,7},{7,1},{8,10},{10,12},{12... | collective-permute-start | bytes 2359304 | tf_op jit(solution)/shard_map/ppermute | solution.py:1165
  123.7 54.2 %collective-permute-start.19 = (bf16[192,2048]{1,0:T(8,128)(2,1)}, bf16[192,2048]{1,0:T(8,128)(2,1)}, u32[]{:S(2)}, u32[]{:S(2)}) collective-permute-start(bf16[192,2048]{1,0:T(8,128)(2,1)} %hold.6.refs_10_), channel_id=1, source_target_pairs={{0,1},{1,0},{2,3},{3,2},{4,5},{5,4},{6,7},{7,6},{8,9},{9,8},{10,11... | collective-permute-start | bytes 2359304 | tf_op jit(solution)/shard_map/ppermute | solution.py:1093
  124.6 53.3 %collective-permute-start.18 = (bf16[192,2048]{1,0:T(8,128)(2,1)}, bf16[192,2048]{1,0:T(8,128)(2,1)}, u32[]{:S(2)}, u32[]{:S(2)}) collective-permute-start(bf16[192,2048]{1,0:T(8,128)(2,1)} %hold.6.refs_10_), channel_id=1, source_target_pairs={{0,16},{16,0},{1,17},{17,1},{2,18},{18,2},{3,19},{19,3},{4,20},{20... | collective-permute-start | bytes 2359304 | tf_op jit(solution)/shard_map/ppermute | solution.py:1093
  183.8 14.6 %collective-permute-start.20 = (bf16[768,2048]{1,0:T(8,128)(2,1)}, bf16[768,2048]{1,0:T(8,128)(2,1)}, u32[]{:S(2)}, u32[]{:S(2)}) collective-permute-start(bf16[768,2048]{1,0:T(8,128)(2,1)} %get-tuple-element.92), channel_id=1, source_target_pairs={{0,8},{8,0},{1,9},{9,1},{2,10},{10,2},{3,11},{11,3},{4,12},{12,4},... | collective-permute-start | bytes 9437192 | tf_op jit(solution)/shard_map/ppermute | solution.py:1093
  184.0 334.7 %reduce-scatter.9.cloned.1.call-start = ((), (), s32[]{:S(2)}) async-start(), calls=%async_computation.16 | async-start | bytes 5898240 | tf_op jit(solution)/shard_map/reduce_scatter | solution.py:1175
  203.1 18.9 %collective-permute-start.23 = (bf16[192,2048]{1,0:T(8,128)(2,1)S(1)}, bf16[192,2048]{1,0:T(8,128)(2,1)S(1)}, u32[]{:S(2)}, u32[]{:S(2)}) collective-permute-start(bf16[192,2048]{1,0:T(8,128)(2,1)S(1)} %get-tuple-element.97), channel_id=1, source_target_pairs={{0,1},{1,0},{2,3},{3,2},{4,5},{5,4},{6,7},{7,6},{8,9},{9,8},{10,11... | collective-permute-start | bytes 2359304 | tf_op jit(solution)/shard_map/ppermute | solution.py:1093
  204.6 18.6 %collective-permute-start.24 = (bf16[192,2048]{1,0:T(8,128)(2,1)S(1)}, bf16[192,2048]{1,0:T(8,128)(2,1)S(1)}, u32[]{:S(2)}, u32[]{:S(2)}) collective-permute-start(bf16[192,2048]{1,0:T(8,128)(2,1)S(1)} %get-tuple-element.98), channel_id=1, source_target_pairs={{0,16},{16,0},{1,17},{17,1},{2,18},{18,2},{3,19},{19,3},{4,20},{20... | collective-permute-start | bytes 2359304 | tf_op jit(solution)/shard_map/ppermute | solution.py:1093
  240.9 19.3 %collective-permute-start.28 = (bf16[192,2048]{1,0:T(8,128)(2,1)S(1)}, bf16[192,2048]{1,0:T(8,128)(2,1)S(1)}, u32[]{:S(2)}, u32[]{:S(2)}) collective-permute-start(bf16[192,2048]{1,0:T(8,128)(2,1)S(1)} %get-tuple-element.103.refs_0_), channel_id=1, source_target_pairs={{0,1},{1,0},{2,3},{3,2},{4,5},{5,4},{6,7},{7,6},{8,9},{9,8},{10,11... | collective-permute-start | bytes 2359304 | tf_op jit(solution)/shard_map/ppermute | solution.py:1093
  241.5 19.4 %collective-permute-start.27 = (bf16[192,2048]{1,0:T(8,128)(2,1)S(1)}, bf16[192,2048]{1,0:T(8,128)(2,1)S(1)}, u32[]{:S(2)}, u32[]{:S(2)}) collective-permute-start(bf16[192,2048]{1,0:T(8,128)(2,1)S(1)} %get-tuple-element.103.refs_0_), channel_id=1, source_target_pairs={{0,16},{16,0},{1,17},{17,1},{2,18},{18,2},{3,19},{19,3},{4,20},{20... | collective-permute-start | bytes 2359304 | tf_op jit(solution)/shard_map/ppermute | solution.py:1093
  242.3 18.6 %collective-permute-start.36 = (bf16[192,2048]{1,0:T(8,128)(2,1)}, bf16[192,2048]{1,0:T(8,128)(2,1)S(1)}, u32[]{:S(2)}, u32[]{:S(2)}) collective-permute-start(bf16[192,2048]{1,0:T(8,128)(2,1)} %hold.6.refs_10_), channel_id=1, source_target_pairs={{0,8},{8,0},{1,9},{9,1},{2,10},{10,2},{3,11},{11,3},{4,12},{12,4},... | collective-permute-start | bytes 2359304 | tf_op jit(solution)/shard_map/ppermute | solution.py:1093
  242.3 19.2 %collective-permute-start.38 = (bf16[192,2048]{1,0:T(8,128)(2,1)}, bf16[192,2048]{1,0:T(8,128)(2,1)S(1)}, u32[]{:S(2)}, u32[]{:S(2)}) collective-permute-start(bf16[192,2048]{1,0:T(8,128)(2,1)} %collective-permute-done.19.refs_4_.by_x.refs_12_), channel_id=1, source_target_pairs={{0,8},{8,0},{1,9},{9,1},{2,10},{10,2},{3,11},{11,3},{4,12},{12,4},... | collective-permute-start | bytes 2359304 | tf_op jit(solution)/shard_map/ppermute | solution.py:1093
  242.8 21.2 %collective-permute-start.37 = (bf16[192,2048]{1,0:T(8,128)(2,1)}, bf16[192,2048]{1,0:T(8,128)(2,1)S(1)}, u32[]{:S(2)}, u32[]{:S(2)}) collective-permute-start(bf16[192,2048]{1,0:T(8,128)(2,1)} %collective-permute-done.18.refs_3_.by_y.refs_11_), channel_id=1, source_target_pairs={{0,8},{8,0},{1,9},{9,1},{2,10},{10,2},{3,11},{11,3},{4,12},{12,4},... | collective-permute-start | bytes 2359304 | tf_op jit(solution)/shard_map/ppermute | solution.py:1093
  260.9 13.0 %collective-permute-start.31 = (bf16[192,2048]{1,0:T(8,128)(2,1)S(1)}, bf16[192,2048]{1,0:T(8,128)(2,1)S(1)}, u32[]{:S(2)}, u32[]{:S(2)}) collective-permute-start(bf16[192,2048]{1,0:T(8,128)(2,1)S(1)} %get-tuple-element.103.refs_0_), channel_id=1, source_target_pairs={{0,8},{8,0},{1,9},{9,1},{2,10},{10,2},{3,11},{11,3},{4,12},{12,4},... | collective-permute-start | bytes 2359304 | tf_op jit(solution)/shard_map/ppermute | solution.py:1093
  264.0 12.5 %collective-permute-start.32 = (bf16[192,2048]{1,0:T(8,128)(2,1)S(1)}, bf16[192,2048]{1,0:T(8,128)(2,1)}, u32[]{:S(2)}, u32[]{:S(2)}) collective-permute-start(bf16[192,2048]{1,0:T(8,128)(2,1)S(1)} %collective-permute-done.27.by_y.refs_1_), channel_id=1, source_target_pairs={{0,8},{8,0},{1,9},{9,1},{2,10},{10,2},{3,11},{11,3},{4,12},{12,4},... | collective-permute-start | bytes 2359304 | tf_op jit(solution)/shard_map/ppermute | solution.py:1093
  301.4 255.5 %reduce-scatter.11.cloned.1.call-start = ((), (), s32[]{:S(2)}) async-start(), calls=%async_computation.17 | async-start | bytes 5242880 | tf_op jit(solution)/shard_map/reduce_scatter | solution.py:1175
  345.0 219.8 %reduce-scatter.5.cloned.1.call-start = ((), (), s32[]{:S(2)}) async-start(), calls=%async_computation.14 | async-start | bytes 3932160 | tf_op jit(solution)/shard_map/reduce_scatter | solution.py:1175
  353.8 19.7 %collective-permute-start.43 = (bf16[192,2048]{1,0:T(8,128)(2,1)S(1)}, bf16[192,2048]{1,0:T(8,128)(2,1)S(1)}, u32[]{:S(2)}, u32[]{:S(2)}) collective-permute-start(bf16[192,2048]{1,0:T(8,128)(2,1)S(1)} %get-tuple-element.115), channel_id=1, source_target_pairs={{0,1},{1,0},{2,3},{3,2},{4,5},{5,4},{6,7},{7,6},{8,9},{9,8},{10,11... | collective-permute-start | bytes 2359304 | tf_op jit(solution)/shard_map/ppermute | solution.py:1093
  355.4 19.4 %collective-permute-start.44 = (bf16[192,2048]{1,0:T(8,128)(2,1)S(1)}, bf16[192,2048]{1,0:T(8,128)(2,1)S(1)}, u32[]{:S(2)}, u32[]{:S(2)}) collective-permute-start(bf16[192,2048]{1,0:T(8,128)(2,1)S(1)} %get-tuple-element.116), channel_id=1, source_target_pairs={{0,16},{16,0},{1,17},{17,1},{2,18},{18,2},{3,19},{19,3},{4,20},{20... | collective-permute-start | bytes 2359304 | tf_op jit(solution)/shard_map/ppermute | solution.py:1093
  388.1 18.6 %collective-permute-start.48 = (bf16[192,2176]{1,0:T(8,128)(2,1)S(1)}, bf16[192,2176]{1,0:T(8,128)(2,1)S(1)}, u32[]{:S(2)}, u32[]{:S(2)}) collective-permute-start(bf16[192,2176]{1,0:T(8,128)(2,1)S(1)} %get-tuple-element.127.refs_6_), channel_id=1, source_target_pairs={{0,1},{1,0},{2,3},{3,2},{4,5},{5,4},{6,7},{7,6},{8,9},{9,8},{10,11... | collective-permute-start | bytes 2506760 | tf_op jit(solution)/shard_map/ppermute | solution.py:1093
  389.1 18.1 %collective-permute-start.47 = (bf16[192,2176]{1,0:T(8,128)(2,1)S(1)}, bf16[192,2176]{1,0:T(8,128)(2,1)S(1)}, u32[]{:S(2)}, u32[]{:S(2)}) collective-permute-start(bf16[192,2176]{1,0:T(8,128)(2,1)S(1)} %get-tuple-element.127.refs_6_), channel_id=1, source_target_pairs={{0,16},{16,0},{1,17},{17,1},{2,18},{18,2},{3,19},{19,3},{4,20},{20... | collective-permute-start | bytes 2506760 | tf_op jit(solution)/shard_map/ppermute | solution.py:1093
  401.5 21.5 %collective-permute-start.51 = (bf16[192,2176]{1,0:T(8,128)(2,1)S(1)}, bf16[192,2176]{1,0:T(8,128)(2,1)S(1)}, u32[]{:S(2)}, u32[]{:S(2)}) collective-permute-start(bf16[192,2176]{1,0:T(8,128)(2,1)S(1)} %get-tuple-element.127.refs_6_), channel_id=1, source_target_pairs={{0,8},{8,0},{1,9},{9,1},{2,10},{10,2},{3,11},{11,3},{4,12},{12,4},... | collective-permute-start | bytes 2506760 | tf_op jit(solution)/shard_map/ppermute | solution.py:1093
  412.3 12.5 %collective-permute-start.52 = (bf16[192,2176]{1,0:T(8,128)(2,1)S(1)}, bf16[192,2176]{1,0:T(8,128)(2,1)S(1)}, u32[]{:S(2)}, u32[]{:S(2)}) collective-permute-start(bf16[192,2176]{1,0:T(8,128)(2,1)S(1)} %collective-permute-done.47.refs_1_.refs_7_), channel_id=1, source_target_pairs={{0,8},{8,0},{1,9},{9,1},{2,10},{10,2},{3,11},{11,3},{4,12},{12,4},... | collective-permute-start | bytes 2506760 | tf_op jit(solution)/shard_map/ppermute | solution.py:1093
  466.0 45.5 %collective-permute-start.41 = (bf16[768,2048]{1,0:T(8,128)(2,1)S(1)}, bf16[768,2048]{1,0:T(8,128)(2,1)S(1)}, u32[]{:S(2)}, u32[]{:S(2)}) collective-permute-start(bf16[768,2048]{1,0:T(8,128)(2,1)S(1)} %copy-done.22), channel_id=1, source_target_pairs={{0,8},{8,0},{1,9},{9,1},{2,10},{10,2},{3,11},{11,3},{4,12},{12,4},... | collective-permute-start | bytes 9437192 | tf_op jit(solution)/shard_map/ppermute | solution.py:1093
  478.0 19.7 %collective-permute-start.57 = (bf16[192,2048]{1,0:T(8,128)(2,1)S(1)}, bf16[192,2048]{1,0:T(8,128)(2,1)S(1)}, u32[]{:S(2)}, u32[]{:S(2)}) collective-permute-start(bf16[192,2048]{1,0:T(8,128)(2,1)S(1)} %get-tuple-element.135), channel_id=1, source_target_pairs={{0,1},{1,0},{2,3},{3,2},{4,5},{5,4},{6,7},{7,6},{8,9},{9,8},{10,11... | collective-permute-start | bytes 2359304 | tf_op jit(solution)/shard_map/ppermute | solution.py:1093
  479.6 19.3 %collective-permute-start.58 = (bf16[192,2048]{1,0:T(8,128)(2,1)S(1)}, bf16[192,2048]{1,0:T(8,128)(2,1)S(1)}, u32[]{:S(2)}, u32[]{:S(2)}) collective-permute-start(bf16[192,2048]{1,0:T(8,128)(2,1)S(1)} %get-tuple-element.136), channel_id=1, source_target_pairs={{0,16},{16,0},{1,17},{17,1},{2,18},{18,2},{3,19},{19,3},{4,20},{20... | collective-permute-start | bytes 2359304 | tf_op jit(solution)/shard_map/ppermute | solution.py:1093
  516.7 20.8 %collective-permute-start.61 = (bf16[192,2048]{1,0:T(8,128)(2,1)}, bf16[192,2048]{1,0:T(8,128)(2,1)}, u32[]{:S(2)}, u32[]{:S(2)}) collective-permute-start(bf16[192,2048]{1,0:T(8,128)(2,1)} %get-tuple-element.142), channel_id=1, source_target_pairs={{0,1},{1,0},{2,3},{3,2},{4,5},{5,4},{6,7},{7,6},{8,9},{9,8},{10,11... | collective-permute-start | bytes 2359304 | tf_op jit(solution)/shard_map/ppermute | solution.py:1093
  517.1 22.4 %collective-permute-start.62 = (bf16[192,2048]{1,0:T(8,128)(2,1)}, bf16[192,2048]{1,0:T(8,128)(2,1)}, u32[]{:S(2)}, u32[]{:S(2)}) collective-permute-start(bf16[192,2048]{1,0:T(8,128)(2,1)} %get-tuple-element.143), channel_id=1, source_target_pairs={{0,16},{16,0},{1,17},{17,1},{2,18},{18,2},{3,19},{19,3},{4,20},{20... | collective-permute-start | bytes 2359304 | tf_op jit(solution)/shard_map/ppermute | solution.py:1093
  521.1 39.2 %all-to-all-start.5 = ((bf16[8,64,1152]{2,1,0:T(8,128)(2,1)}), bf16[8,64,1152]{2,1,0:T(8,128)(2,1)S(1)}, u32[]{:S(2)}, u32[]{:S(2)}) async-start(bf16[8,64,1152]{2,1,0:T(8,128)(2,1)} %copy-done.10), calls=%async_computation.8 | async-start | bytes 2359296 | tf_op jit(solution)/shard_map/all_to_all | solution.py:1159
  524.8 59.5 %reduce-scatter.7.cloned.1.call-start = ((), (), s32[]{:S(2)}) async-start(), calls=%async_computation.15 | async-start | bytes 1392640 | tf_op jit(solution)/shard_map/reduce_scatter | solution.py:1175
  542.4 13.4 %collective-permute-start.63 = (bf16[96,2048]{1,0:T(8,128)(2,1)S(1)}, bf16[96,2048]{1,0:T(8,128)(2,1)S(1)}, u32[]{:S(2)}, u32[]{:S(2)}) collective-permute-start(bf16[96,2048]{1,0:T(8,128)(2,1)S(1)} %get-tuple-element.145), channel_id=1, source_target_pairs={{0,16},{16,0},{1,17},{17,1},{2,18},{18,2},{3,19},{19,3},{4,20},{20... | collective-permute-start | bytes 1179656 | tf_op jit(solution)/shard_map/ppermute | solution.py:1093
  560.3 19.3 %all-to-all-start.6 = ((bf16[8,64,1024]{2,1,0:T(8,128)(2,1)}), bf16[8,64,1024]{2,1,0:T(8,128)(2,1)}, u32[]{:S(2)}, u32[]{:S(2)}) async-start(bf16[8,64,1024]{2,1,0:T(8,128)(2,1)} %copy-done.12), calls=%async_computation.10 | async-start | bytes 2097152 | tf_op jit(solution)/shard_map/all_to_all | solution.py:1159
  579.7 16.3 %all-to-all-start.4 = ((bf16[8,64,768]{2,1,0:T(8,128)(2,1)}), bf16[8,64,768]{2,1,0:T(8,128)(2,1)}, u32[]{:S(2)}, u32[]{:S(2)}) async-start(bf16[8,64,768]{2,1,0:T(8,128)(2,1)} %bitcast.44), calls=%async_computation.5 | async-start | bytes 1572864 | tf_op jit(solution)/shard_map/all_to_all | solution.py:1159
  (120 other events, 944.0 us)
Sparse Core Ops, SparseCore 0:
  9.6 28.4 all-gather.3
  97.7 105.9 all-gather.5
  205.8 79.2 all-gather.7
  301.5 85.8 reduce-scatter.8
  389.6 77.2 reduce-scatter.10
  469.1 60.2 reduce-scatter.4
  532.4 26.8 reduce-scatter.6

commit v3 on v2

--- a/solution.py
+++ b/solution.py
@@ -21,6 +21,7 @@
 VMEM_BYTES = 58 * 1024 * 1024
 SPARE_BYTES = 12 * 1024 * 1024
 VMEM_SPEC = pl.BlockSpec(memory_space=pltpu.VMEM)
+TOKEN = ((8, 128), F32)
 SMEM_SPEC = pl.BlockSpec(memory_space=pltpu.SMEM)
 ANY_SPEC = pl.BlockSpec(memory_space=pl.ANY)
 
@@ -52,6 +53,7 @@
     any_outs=(),
     cost=(0, 0),
     after=(),
+    token=False,
 ):
     any_from = len(operands) if any_from is None else any_from
     if after:
@@ -62,6 +64,15 @@
 
         operands = list(operands) + list(after)
         any_from = min(any_from, count)
+    if token:
+        plain, mark = kernel, len(operands) + len(outs)
+
+        def kernel(*refs):
+            refs[mark][...] = jnp.zeros(TOKEN[0], F32)
+            plain(*refs[:mark], *refs[mark + 1 :])
+
+        any_outs = [i for i in any_outs if i < len(outs)]
+        outs = list(outs) + [TOKEN]
     held = list(operands[smem:any_from]) + [
         jax.ShapeDtypeStruct(*out) for i, out in enumerate(outs) if i not in any_outs
     ]
@@ -267,6 +278,21 @@
     return call(hold_kernel, "hold", [(value.shape, value.dtype)], [value], after=after)[0]
 
 
+def pin_kernel(value, *refs):
+    del value, refs
+
+
+def pin(value, after):
+    return pl.pallas_call(
+        pin_kernel,
+        out_shape=jax.ShapeDtypeStruct(value.shape, value.dtype),
+        in_specs=[ANY_SPEC] * (1 + len(after)),
+        out_specs=ANY_SPEC,
+        input_output_aliases={0: 0},
+        name="pin",
+    )(value, *after)
+
+
 def halves_kernel(by_x, by_y, top, end):
     half = top.shape[0]
     top[...] = by_x[:half, :]
@@ -307,10 +333,8 @@
 ):
     rows_in = refs[: layout.row_count]
     weights_in = refs[layout.row_count : layout.row_count + layout.plane_count]
-    outs, refs = refs[layout.row_count + layout.plane_count :][:7], refs[-14:]
-    squares_out, rows_ref, weights, pre = refs[:4]
-    row_sems, weight_sem, out_sems = refs[4:7]
-    kept = refs[7:]
+    outs, refs = refs[layout.row_count + layout.plane_count :][:7], refs[-13:]
+    rows_ref, weights, pre, row_sems, weight_sem, out_sems, *kept = refs
     (
         forget_out,
         floor_out,
@@ -389,14 +413,6 @@
     lax.fori_loop(
         0, segments, over_segments, tuple(jnp.zeros((1, width), F32) for _ in range(buckets))
     )
-    ones = jnp.ones((8, width), LOW)
-    for part in range(layout.parts):
-        first = pl.multiple_of(slots[part] * seg_rows, seg_rows)
-        states = states_out[pl.ds(first, seg_rows), :].astype(F32)
-        squares = states * states
-        high = squares.astype(LOW)
-        rest = (squares - high.astype(F32)).astype(LOW)
-        squares_out[part : part + 1, :] = (product_nt(ones, high) + product_nt(ones, rest))[0:1]
     for i, ref in enumerate(kept):
         await_copies(ref, out_sems.at[i])
 
@@ -409,7 +425,7 @@
     return call(
         functools.partial(mixer_forward_kernel, layout),
         "mixer_forward",
-        [(wide, F32)] * 5 + [(wide, LOW)] * 2 + [((layout.parts, layout.slot_rows), F32)],
+        [(wide, F32)] * 5 + [(wide, LOW)] * 2,
         [slots, ends, place, floors, gains, *rows, *weights],
         [
             pltpu.VMEM((count, depth), LOW),
@@ -429,15 +445,31 @@
     )
 
 
-def branch_kernel(layout, place, scaled, *refs):
+def split_lanes(*columns):
+    shape = (columns[0].shape[0], 128)
+    lane = lax.broadcasted_iota(jnp.int32, shape, 1)
+    lanes = jnp.zeros(shape, F32)
+    for i, column in enumerate(columns):
+        high = column.astype(LOW).astype(F32)
+        lanes = jnp.where(lane == 2 * i, high, lanes)
+        lanes = jnp.where(lane == 2 * i + 1, column - high, lanes)
+    return lanes.astype(LOW)
+
+
+def branch_kernel(layout, place, scaled, states, *refs):
     weights_in = refs[:1]
     outs = refs[1:-4]
     weights, staged, sem, out_sem = refs[-4:]
     layout.fill_channels(place[0], weights_in, weights, sem)
     await_copies(weights, sem)
-    write_parts(
-        layout, outs, staged, out_sem, lambda at: product(scaled[at, :], weights[...])
-    )
+
+    def rows_of(at):
+        values = states[at, :].astype(F32)
+        squares = jnp.sum(values * values, axis=1, keepdims=True)
+        parts = product(scaled[at, :], weights[...]).astype(LOW)
+        return jnp.concatenate([parts, split_lanes(squares)], axis=1)
+
+    write_parts(layout, outs, staged, out_sem, rows_of)
     await_copies(staged, out_sem)
 
 
@@ -462,22 +494,22 @@
     return [((count, width), LOW)]
 
 
-def branch_parts(layout, place, scaled, weights, after):
+def branch_parts(layout, place, scaled, states, weights, after):
     count, channels = scaled.shape
     width = weights[0].shape[1]
     return call(
         functools.partial(branch_kernel, layout),
         "branch_parts",
-        part_shapes(layout, width),
-        [place, scaled, *weights],
+        part_shapes(layout, width + 128),
+        [place, scaled, states, *weights],
         [
             pltpu.VMEM((channels, width), LOW),
-            pltpu.VMEM((count, width), LOW),
+            pltpu.VMEM((count, width + 128), LOW),
             pltpu.SemaphoreType.DMA,
             pltpu.SemaphoreType.DMA,
         ],
         smem=1,
-        any_from=2,
+        any_from=3,
         any_outs=(0, 1),
         after=after,
         cost=(2 * count * channels * width, 2 * count * width + 2 * channels * width),
@@ -771,11 +803,11 @@
     )
 
 
-def glu_second_kernel(layout, first_count, place, *refs):
+def glu_second_kernel(layout, first_count, second_count, place, *refs):
     rows_in, refs = refs[: layout.row_count], refs[layout.row_count :]
     grads_in, refs = refs[: layout.row_count], refs[layout.row_count :]
     first_in, refs = refs[:first_count], refs[first_count:]
-    second_in, refs = refs[:first_count], refs[first_count:]
+    second_in, refs = refs[:second_count], refs[second_count:]
     first_acts_in, acts_out = refs[0], refs[1]
     outs = refs[2:-14]
     (
@@ -831,7 +863,7 @@
     first_columns = 2 * layout.split
     sems = pltpu.SemaphoreType.DMA
     return call(
-        functools.partial(glu_second_kernel, layout, len(first)),
+        functools.partial(glu_second_kernel, layout, len(first), len(second)),
         "glu_second",
         [((count, columns), LOW)] + part_shapes(layout, depth),
         [place, *rows, *grads, *first, *second, first_acts],
@@ -899,13 +931,14 @@
         any_from=1,
         any_outs=(0,),
         after=after,
+        token=True,
         cost=(2 * count * depth * columns, 4 * count * depth + 2 * depth * columns),
-    )[0]
-
-
-def output_kernel(layout, first_count, place, *refs):
+    )
+
+
+def output_kernel(layout, first_count, second_count, place, *refs):
     first_in, refs = refs[:first_count], refs[first_count:]
-    second_in, refs = refs[:first_count], refs[first_count:]
+    second_in, refs = refs[:second_count], refs[second_count:]
     first_acts_in, second_acts_in = refs[:2]
     outs = refs[2:-6]
     first, second, first_acts, second_acts, staged, sems = refs[-6:]
@@ -937,7 +970,7 @@
     count = first_acts.shape[0]
     widths = first_acts.shape[1] - 2 * layout.split, second_acts.shape[1] - 2 * layout.rest
     return call(
-        functools.partial(output_kernel, layout, len(first)),
+        functools.partial(output_kernel, layout, len(first), len(second)),
         "output_parts",
         part_shapes(layout, depth),
         [place, *first, *second, first_acts, second_acts],
@@ -948,6 +981,7 @@
         any_from=1,
         any_outs=(0, 1),
         after=after,
+        token=True,
         cost=(2 * count * depth * sum(widths), 2 * count * depth + 2 * depth * sum(widths)),
     )
 
@@ -976,13 +1010,15 @@
         out[at, :] = (values * inverse_rms(values) * gains[...]).astype(LOW)
 
 
-def residual_kernel(tokens, gains, squares, *refs):
+def residual_kernel(tokens, gains, *refs):
     parts, (residual_out, ffn_out, inverse_out) = refs[:-3], refs[-3:]
     width = tokens.shape[1]
     for at in row_steps(tokens.shape[0]):
-        inverse = lax.rsqrt(squares[at, :] * (1.0 / width) + EPSILON)
+        total = summed(parts, at)
+        squares = total[:, width : width + 1] + total[:, width + 1 : width + 2]
+        inverse = lax.rsqrt(squares * (1.0 / width) + EPSILON)
         inverse_out[at, :] = inverse
-        residual = tokens[at, :].astype(F32) + summed(parts, at) * inverse
+        residual = tokens[at, :].astype(F32) + total[:, :width] * inverse
         residual_out[at, :] = residual
         ffn_out[at, :] = (residual * inverse_rms(residual) * gains[...]).astype(LOW)
 
@@ -990,7 +1026,6 @@
 def grad_residual_kernel(tokens, cotangent, gains, residual_in, inverse_in, *refs):
     parts, (grad_out, low_out) = refs[:-2], refs[-2:]
     width = tokens.shape[1]
-    lane = lax.broadcasted_iota(jnp.int32, (ROWS, 128), 1)
     for at in row_steps(tokens.shape[0]):
         residual = residual_in[at, :]
         inverse = inverse_rms(residual)
@@ -1002,14 +1037,8 @@
         low = grad.astype(LOW)
         low_out[at, :width] = low
         branch = residual - tokens[at, :].astype(F32)
-        factors = jnp.zeros((ROWS, 128), F32)
-        for i, factor in enumerate(
-            (inverse_in[at, :], jnp.mean(low.astype(F32) * branch, axis=1, keepdims=True))
-        ):
-            high = factor.astype(LOW).astype(F32)
-            factors = jnp.where(lane == 2 * i, high, factors)
-            factors = jnp.where(lane == 2 * i + 1, factor - high, factors)
-        low_out[at, width:] = factors.astype(LOW)
+        mean = jnp.mean(low.astype(F32) * branch, axis=1, keepdims=True)
+        low_out[at, width:] = split_lanes(inverse_in[at, :], mean)
 
 
 def output_rows_kernel(residual, *refs):
@@ -1031,15 +1060,25 @@
         ).astype(LOW)
 
 
-def core_sum_kernel(rows, mine, other, top_out, end_out, top_keep, end_keep):
+def add_rows(mine, other, wide):
+    total = mine.astype(F32) + other.astype(F32)
+    low = total.astype(LOW)
+    if wide < total.shape[1]:
+        number = jnp.sum(total[:, wide:], axis=1, keepdims=True)
+        lanes = split_lanes(number)
+        low = jnp.concatenate([low[:, :wide], lanes], axis=1)
+        total = jnp.concatenate([total[:, :wide], lanes.astype(F32)], axis=1)
+    return (total, low)
+
+
+def core_sum_kernel(rows, wide, mine, other, top_out, end_out, top_keep, end_keep):
     half = rows // 2
     for x in range(2):
         for y in range(2):
             slot = x * 2 + y
             for first in range(0, rows, ROWS):
                 at = slice(slot * rows + first, slot * rows + first + ROWS)
-                total = mine[at, :].astype(F32) + other[at, :].astype(F32)
-                low = total.astype(LOW)
+                _, low = add_rows(mine[at, :], other[at, :], wide)
                 if first < half:
                     if x:
                         top_out[y * half + first : y * half + first + ROWS, :] = low
@@ -1053,18 +1092,15 @@
                         end_keep[to : to + ROWS, :] = low
 
 
-def chip_sum_kernel(top, end, top_in, end_in, top_out, end_out, keep):
+def chip_sum_kernel(wide, top, end, top_in, end_in, top_out, end_out, keep):
     half = top.shape[0] // 2
     for i, (mine, other, out) in enumerate(((top, top_in, top_out), (end, end_in, end_out))):
         for first in range(0, half, ROWS):
             at = slice(first, first + ROWS)
-            keep[i * half + first : i * half + first + ROWS, :] = mine[at, :].astype(
-                F32
-            ) + other[at, :].astype(F32)
+            to = i * half + first
+            keep[to : to + ROWS, :] = add_rows(mine[at, :], other[at, :], wide)[0]
             at = slice(half + first, half + first + ROWS)
-            out[first : first + ROWS, :] = (
-                mine[at, :].astype(F32) + other[at, :].astype(F32)
-            ).astype(LOW)
+            out[first : first + ROWS, :] = add_rows(mine[at, :], other[at, :], wide)[1]
 
 
 class Links:
@@ -1103,40 +1139,40 @@
         own = [value, by_y, by_x, self.swap("y", top), self.swap("x", end)]
         return own + [self.swap("core", piece) for piece in own]
 
-    def sum_cores(self, parts, after=()):
+    def sum_cores(self, parts, after=(), wide=None):
         if not self.pairs:
             return parts
         away, mine = parts
         rows, width = mine.shape[0] // 4, mine.shape[1]
         return call(
-            functools.partial(core_sum_kernel, rows),
+            functools.partial(core_sum_kernel, rows, width if wide is None else wide),
             "core_sum",
             [((rows, width), LOW)] * 4,
             [mine, self.swap("core", away)],
             cost=(8 * rows * width, 24 * rows * width),
             after=after,
+            token=True,
         )
 
-    def sum_chips(self, parts, after=()):
+    def swap_chips(self, parts):
+        return [self.swap("x", parts[0]), self.swap("y", parts[1])] if self.pairs else []
+
+    def sum_chips(self, parts, others, after=(), wide=None):
         if not self.pairs:
             return [
                 lax.psum_scatter(parts[0], self.plane, scatter_dimension=0, tiled=True).astype(F32)
             ]
-        top, end, top_keep, end_keep = parts
+        top, end, top_keep, end_keep, _ = parts
         rows, width = top.shape
         top, end, keep = call(
-            chip_sum_kernel,
+            functools.partial(chip_sum_kernel, width if wide is None else wide),
             "chip_sum",
             [((rows // 2, width), LOW)] * 2 + [((rows, width), F32)],
-            [top_keep, end_keep, self.swap("x", top), self.swap("y", end)],
+            [top_keep, end_keep, *others],
             cost=(2 * rows * width, 12 * rows * width),
             after=after,
         )
         return [keep, self.swap("y", top), self.swap("x", end)]
-
-    def sum_rows_small(self, parts):
-        parts = lax.all_to_all(parts, self.plane, split_axis=0, concat_axis=0, tiled=True)
-        return jnp.sum(parts, axis=0)
 
     def sum_planes_small(self, value):
         planes = self.sizes["z"]
@@ -1158,18 +1194,19 @@
     def exchange(self, value):
         return lax.all_to_all(value, self.owners, split_axis=0, concat_axis=0, tiled=True)
 
-    def ring(self, value):
+    def ring(self, value, gate=lambda pieces: pieces):
         planes = self.sizes["z"]
 
         def shift(value, by):
             return lax.ppermute(value, "z", [(i, (i + by) % planes) for i in range(planes)])
 
-        up, down = [value], []
-        while 1 + len(up) + len(down) <= planes:
-            up.append(shift(up[-1], 1))
-            if 1 + len(up) + len(down) <= planes:
-                down.insert(0, shift(down[0] if down else value, -1))
-        return up + down
+        pieces = {0: value, 1: shift(value, 1)}
+        if planes > 2:
+            pieces[planes - 1] = shift(value, -1)
+        pieces.update(zip([k for k in pieces if k], gate([pieces[k] for k in pieces if k])))
+        for k in range(2, planes - 1):
+            pieces[k] = shift(pieces[k - 1], 1)
+        return [pieces[k] for k in range(planes)]
 
     def sum_planes(self, value):
         return lax.psum_scatter(value, "z", scatter_dimension=0, tiled=True)
@@ -1239,10 +1276,10 @@
             after=after,
         )[0]
 
-    def gather_weights(weight, ring=True):
+    def gather_weights(weight, ring=True, gate=lambda pieces: pieces):
         weight = weight.reshape(parts * block, -1)
         if layout.pieces and ring:
-            return links.ring(weight)
+            return links.ring(weight, gate)
         if layout.pieces:
             return [lax.all_gather(weight, "z", axis=0, tiled=True)]
         full = lax.all_gather(weight, "z", axis=0)
@@ -1270,9 +1307,9 @@
     vectors = links.sum_planes_small(
         lax.dynamic_update_slice(jnp.zeros((4, width), F32), vectors, (0, owner * block))
     )
-    mixer = gather_weights(hold(links.exchange(mixer), [vectors]))
+    out_weights = [lax.all_gather(w_out, "z", axis=0, tiled=True)]
+    arrived = pin(links.exchange(mixer), [vectors, *out_weights])
     vectors = links.sum_plane_small(vectors)
-    out_weights = [lax.all_gather(w_out, "z", axis=0, tiled=True)]
     gain_mix, gain_ffn = vectors[0:1], vectors[1:2]
     own_vectors = own_channels(vectors[2:])
     gain_out = own_vectors[0:1]
@@ -1281,27 +1318,30 @@
     ends = links.both_x(jnp.cumsum(doc_lengths, axis=1).astype(jnp.int32))
 
     (mixed,) = call(
-        norm_kernel, "mixed_in", [low_wide], [tokens, gain_mix], cost=row_cost
-    )
-    first = links.exchange(to_hidden(0, layout.split, [mixed, *out_weights]))
+        norm_kernel, "mixed_in", [low_wide], [tokens, gain_mix], cost=row_cost, after=[arrived]
+    )
+    first = links.exchange(to_hidden(0, layout.split, [mixed]))
     mixed = links.rows(mixed)
-    first = gather_weights(hold(first, [*mixer[1:2], *mixer[-1:], *mixed[3:5]]), False)
-    second = links.exchange(to_hidden(layout.split, layout.rest, mixer[1:2] + mixer[-1:]))
-    early = [second]
+    mixer = gather_weights(
+        arrived,
+        gate=lambda pieces: [pin(pieces[0], [*pieces[1:], first, *mixed]), *pieces[1:]],
+    )
+    grads_all = links.rows(hold(cotangent, mixer[1:2]))
+    first = gather_weights(pin(first, mixer[1:2]), False)
+    second = links.exchange(to_hidden(layout.split, layout.rest, mixer[1:2]))
+    late = [second]
     second = gather_weights(second, False)
-    grads_all = links.rows(hold(cotangent, early))
-    forget, floor_term, slope_forget, slope_input, gate_pre, states, scaled, squares = (
-        mixer_forward(layout, slots, ends, place, floors, gain_out, mixed, mixer, early)
-    )
-    squares = links.sum_rows_small(squares).reshape(row_count, 1)
-    branch = branch_parts(layout, place, scaled, out_weights, grads_all[1:3])
-    branch = links.sum_cores(branch, grads_all[3:5])
-    branch = links.sum_chips(branch)
+    forget, floor_term, slope_forget, slope_input, gate_pre, states, scaled = mixer_forward(
+        layout, slots, ends, place, floors, gain_out, mixed, mixer, []
+    )
+    branch = branch_parts(layout, place, scaled, states, out_weights, late + grads_all[3:5])
+    branch = links.sum_cores(branch, wide=width)
+    branch = links.sum_chips(branch, links.swap_chips(branch), wide=width)
     residual, ffn, inverse_h = call(
         residual_kernel,
         "residual",
         [wide, low_wide, column],
-        [tokens, gain_ffn, squares, *branch],
+        [tokens, gain_ffn, *branch],
         cost=row_cost,
     )
 
@@ -1312,53 +1352,53 @@
         layout, place, ffn, grads_all, first, second, first_acts
     )
     ffn_parts = links.sum_cores(ffn_parts)
-    second_grads = glu_third(layout, place, ffn, grads_all, second_acts, [])
-    grad_ffn = links.sum_chips(ffn_parts, [second_grads])
-    second_grads = scatter_weights(second_grads)
-    grad_residual, grad_low = call(
+    others = links.swap_chips(ffn_parts)
+    second_grads, token = glu_third(
+        layout, place, ffn, grads_all, second_acts, ffn_parts[-1:]
+    )
+    second_grads = scatter_weights(pin(second_grads, others))
+    grad_ffn = links.sum_chips(ffn_parts, others, [token])
+    grad_residual, grad_low, token = call(
         grad_residual_kernel,
         "grad_residual",
         [wide, ((row_count, width + 128), LOW)],
         [tokens, cotangent, gain_ffn, residual, inverse_h, *grad_ffn],
         cost=row_cost,
-    )
-    out_parts = output_parts(
-        layout, place, first, second, first_acts, second_acts, width, []
-    )
-
-    grads_low = links.rows(grad_low, out_parts[:1])
+        token=True,
+    )
+
+    *out_parts, token = output_parts(
+        layout, place, first, second, first_acts, second_acts, width, [token]
+    )
+    grads_low = links.rows(grad_low, [token])
+    out_parts = [pin(out_parts[0], grads_low[1:3]), *out_parts[1:]]
+    output = links.sum_cores(out_parts, grads_low[3:5])
     saved = [gate_pre, states, forget, floor_term, slope_forget, slope_input]
     mixer_grads, out_grads, mixer_weight_grads = mixer_backward(
-        layout,
-        slots,
-        place,
-        gain_out,
-        saved,
-        grads_low,
-        out_weights,
-        mixed,
-        [],
+        layout, slots, place, gain_out, saved, grads_low, out_weights, mixed, output[-1:]
     )
     mixer_weight_grads = scatter_weights(mixer_weight_grads)
     out_grads = links.sum_planes(out_grads)
     mixed_parts = links.sum_cores(
         mixed_grad_parts(layout, place, mixer_grads, mixer, width, [])
     )
-    grad_mixed = links.sum_chips(mixed_parts)
-    (grad_tokens,) = call(
+    first_grads = links.exchange(hold(first_grads, mixed_parts[-1:]))
+    output = links.sum_chips(output, links.swap_chips(output))
+    (output,) = call(
+        output_rows_kernel, "output_rows", [low_wide], [residual, *output], cost=row_cost
+    )
+    grad_mixed = links.sum_chips(mixed_parts, links.swap_chips(mixed_parts))
+    grad_tokens, token = call(
         grad_tokens_kernel,
         "grad_tokens",
         [low_wide],
         [tokens, gain_mix, grad_residual, *grad_mixed],
         cost=row_cost,
-    )
-    output = links.sum_chips(links.sum_cores(out_parts, [grad_tokens]))
-    (output,) = call(
-        output_rows_kernel, "output_rows", [low_wide], [residual, *output], cost=row_cost
-    )
-    first_grads = links.exchange(hold(first_grads, [grad_tokens]))
-    second_grads = links.exchange(hold(second_grads, [output]))
-    mixer_weight_grads = links.exchange(mixer_weight_grads)
+        token=True,
+        after=[output, first_grads],
+    )
+    second_grads = links.exchange(hold(second_grads, [token]))
+    mixer_weight_grads = links.exchange(pin(mixer_weight_grads, [second_grads]))
 
     def as_column(vector):
         return vector.astype(F32).reshape(block, 1)

time: 616 us -> 561 us (0.911)
  waiting for transfers between devices: 279 us -> 214 us
  blocking collectives: 9.59 us -> 18 us
    ppermute x60, waiting for transfers between devices: 214 us -> 177 us  [swap(): return lax.ppermute(value, axis, SWAP)]
    all_to_all x6 -> x5, waiting for transfers between devices: 19 us -> 2.69 us  [exchange(): lax.all_to_all(value, self.owners, split_axis=0, concat_axis=0, tiled=True)]
    ppermute x3, waiting for transfers between devices: 37 us -> 25 us  [shift(): lax.ppermute(value, 'z', [(i, (i + by) % planes) for i in range(planes)])]
    all_to_all x1, blocking collectives: 9.59 us -> 18 us  [exchange(): lax.all_to_all(value, self.owners, split_axis=0, concat_axis=0, tiled=True)]
    pallas_call x36 -> x34, Pallas kernels: 173 us -> 176 us  [call(): pl.pallas_call(kernel, out_shape=tuple((jax.ShapeDtypeStruct(*out) for ou...]
    all_to_all x6 -> x5, starting transfers between devices: 23.5 us -> 20.8 us  [exchange(): lax.all_to_all(value, self.owners, split_axis=0, concat_axis=0, tiled=True)]
    unnamed x180 -> x174, local copies, waits for them, and re-layouts: 48.7 us -> 49 us
  transfers between devices with their start and end apart: 78 -> 77, of which waited for: 41 -> 41; matrix products, arithmetic and copies ran while one was open for 1% -> 1% of each run, Pallas kernels for 28% -> 31%
where the time goes in v3:
time: 561 us; the launch traced here: 551 us
  waiting for transfers between devices  214 us (38%)
  Pallas kernels  176 us (31%)
  starting transfers between devices  71.1 us (13%)
  local copies, waits for them, and re-layouts  51.7 us (9%)
  blocking collectives  18 us (3%)
  between operations  15.5 us (3%)
    ppermute x60, waiting for transfers between devices, swap(): return lax.ppermute(value, axis, SWAP)  177 us
    pallas_call x34, Pallas kernels, call(): pl.pallas_call(kernel, out_shape=tuple((jax.ShapeDtypeStruct(*out) for ou...  176 us
    unnamed x174, local copies, waits for them, and re-layouts  49 us
    ppermute x60, starting transfers between devices, swap(): return lax.ppermute(value, axis, SWAP)  43.9 us
    ppermute x3, waiting for transfers between devices, shift(): lax.ppermute(value, 'z', [(i, (i + by) % planes) for i in range(planes)])  25 us
    all_to_all x5, starting transfers between devices, exchange(): lax.all_to_all(value, self.owners, split_axis=0, concat_axis=0, tiled=True)  20.8 us
    all_to_all x1, blocking collectives, exchange(): lax.all_to_all(value, self.owners, split_axis=0, concat_axis=0, tiled=True)  18 us
  transfers between devices with their start and end apart: 77, of which 41 were waited for; matrix products, arithmetic and copies ran while one was open for 1% of the time, Pallas kernels for 31%

profile of v3, /device:TPU:16, one launch (start us, length us, event | category | flops | bytes accessed | tf_op | source)
XLA Modules:
  0.0 551.2 jit_solution(2356910152407640090)
XLA Ops:
  14.7 4.3 all-to-all-start
  19.7 5.3 collective-permute-done.1
  25.1 1.9 collective-permute-start.2
  27.0 4.4 collective-permute-done.2
  32.9 2.4 collective-permute-done.3
  36.7 2.2 all-gather.4.cloned.1.call-done.refs_1_.refs_3_.refs_19_
  45.6 4.3 all-to-all-start.1
  51.0 8.8 %collective-permute-done.7.by_x.refs_4_.refs_2_.refs_22_ = bf16[192,2048]{1,0:T(8,128)(2,1)} collective-permute-done((bf16[192,2048]{1,0:T(8,128)(2,1)S(1)}, bf16[192,2048]{1,0:T(8,128)(2,1)}, u32[]{:S(2)}, u32[]{:S(2)}) %collective-permute-start.7) | collective-permute-done | bytes 786464 | tf_op jit(solution)/shard_map/ppermute | solution.py:1129
  64.5 3.2 collective-permute-start.9
  67.9 12.9 %collective-permute-done.8.refs_5_.refs_3_.refs_23_ = bf16[96,2048]{1,0:T(8,128)(2,1)S(1)} collective-permute-done((bf16[96,2048]{1,0:T(8,128)(2,1)S(1)}, bf16[96,2048]{1,0:T(8,128)(2,1)S(1)}, u32[]{:S(2)}, u32[]{:S(2)}) %collective-permute-start.8) | collective-permute-done | bytes 393248 | tf_op jit(solution)/shard_map/ppermute | solution.py:1129
  95.1 4.2 all-to-all-start.2
  100.1 9.7 %collective-permute-done.5 = s32[1,4]{1,0:T(1,128)S(1)} collective-permute-done((s32[1,4]{1,0:T(1,128)S(1)}, s32[1,4]{1,0:T(1,128)S(1)}, u32[]{:S(2)}, u32[]{:S(2)}) %collective-permute-start.5) | collective-permute-done | bytes 48 | tf_op jit(solution)/shard_map/ppermute | solution.py:1129
  114.7 25.0 %collective-permute-done.17.refs_12_.refs_2_ = bf16[512,768]{1,0:T(8,128)(2,1)} collective-permute-done((bf16[512,768]{1,0:T(8,128)(2,1)S(1)}, bf16[512,768]{1,0:T(8,128)(2,1)}, u32[]{:S(2)}, u32[]{:S(2)}) %collective-permute-start.17) | collective-permute-done | bytes 786464 | tf_op jit(solution)/shard_map/ppermute | solution.py:1201
  139.7 15.6 %mixer_forward.1 = (f32[1536,256]{1,0:T(8,128)}, f32[1536,256]{1,0:T(8,128)}, f32[1536,256]{1,0:T(8,128)}, f32[1536,256]{1,0:T(8,128)}, f32[1536,256]{1,0:T(8,12...) custom-call(s32[8]{0:T(128)} %add.84.slots.refs_0_, s32[2,4]{1,0:T(2,128)} %add_select_fusion.ends, ...), custom_call_target="tpu_custom_call" | custom-call | flops 4831838208 | bytes 18874368 | tf_op jit(solution)/shard_map/mixer_forward/pallas_call | solution.py:84
  156.2 6.2 %branch_parts.1 = (bf16[768,2176]{1,0:T(8,128)(2,1)}, bf16[768,2176]{1,0:T(8,128)(2,1)}) custom-call(s32[1]{0:T(128)} %bitcast.5.place.refs_0_.refs_1_, bf16[1536,256]{1,0:T(8,128)(2,1)} %get-tuple-element.97.refs_1_, bf16[1536,256]{1,0:T(8,128)(2,1)} %get-tuple-element.98.refs_2_.refs_4_, ...), custom_call_target="tpu_custom_call" | custom-call | flops 1610612736 | bytes 7340032 | tf_op jit(solution)/shard_map/branch_parts/pallas_call | solution.py:84
  162.7 6.0 %collective-permute-done.22.refs_1_ = bf16[768,2176]{1,0:T(8,128)(2,1)} collective-permute-done((bf16[768,2176]{1,0:T(8,128)(2,1)}, bf16[768,2176]{1,0:T(8,128)(2,1)}, u32[]{:S(2)}, u32[]{:S(2)}) %collective-permute-start.22) | collective-permute-done | bytes 3342368 | tf_op jit(solution)/shard_map/ppermute | solution.py:1129
  168.7 1.9 copy-done.13
  170.6 3.5 core_sum.4
  175.3 19.5 %collective-permute-done.23.top_in = bf16[192,2176]{1,0:T(8,128)(2,1)S(1)} collective-permute-done((bf16[192,2176]{1,0:T(8,128)(2,1)S(1)}, bf16[192,2176]{1,0:T(8,128)(2,1)S(1)}, u32[]{:S(2)}, u32[]{:S(2)}) %collective-permute-start.23) | collective-permute-done | bytes 835616 | tf_op jit(solution)/shard_map/ppermute | solution.py:1129
  197.3 9.4 %collective-permute-done.25.refs_1_ = bf16[96,2176]{1,0:T(8,128)(2,1)S(1)} collective-permute-done((bf16[96,2176]{1,0:T(8,128)(2,1)S(1)}, bf16[96,2176]{1,0:T(8,128)(2,1)S(1)}, u32[]{:S(2)}, u32[]{:S(2)}) %collective-permute-start.25) | collective-permute-done | bytes 417824 | tf_op jit(solution)/shard_map/ppermute | solution.py:1129
  210.6 14.9 %collective-permute-done.28.by_x.refs_2_.refs_3_ = bf16[192,2048]{1,0:T(8,128)(2,1)S(1)} collective-permute-done((bf16[192,2048]{1,0:T(8,128)(2,1)S(1)}, bf16[192,2048]{1,0:T(8,128)(2,1)S(1)}, u32[]{:S(2)}, u32[]{:S(2)}) %collective-permute-start.28) | collective-permute-done | bytes 786464 | tf_op jit(solution)/shard_map/ppermute | solution.py:1129
  230.5 8.6 %collective-permute-done.29.refs_3_.refs_4_ = bf16[96,2048]{1,0:T(8,128)(2,1)} collective-permute-done((bf16[96,2048]{1,0:T(8,128)(2,1)S(1)}, bf16[96,2048]{1,0:T(8,128)(2,1)}, u32[]{:S(2)}, u32[]{:S(2)}) %collective-permute-start.29) | collective-permute-done | bytes 393248 | tf_op jit(solution)/shard_map/ppermute | solution.py:1129
  242.8 25.0 %glu_first.1 = (bf16[1536,1152]{1,0:T(8,128)(2,1)}, bf16[2048,1152]{1,0:T(8,128)(2,1)}) custom-call(s32[1]{0:T(128)} %bitcast.5.place.refs_0_.refs_1_, bf16[192,2048]{1,0:T(8,128)(2,1)} %copy-done.57, bf16[192,2048]{1,0:T(8,128)(2,1)} %collective-permute-done.27.by_y.refs_1_.refs_2_, bf16[192,2048]{1,0:T(8,128)(2,1)} %copy-done.37, ...), custom_call_target="tpu_custom_call" | custom-call | flops 14495514624 | bytes 22020096 | tf_op jit(solution)/shard_map/glu_first/pallas_call | solution.py:84
  268.1 27.6 %glu_second.1 = (bf16[1536,1024]{1,0:T(8,128)(2,1)}, bf16[768,2048]{1,0:T(8,128)(2,1)}, bf16[768,2048]{1,0:T(8,128)(2,1)}) custom-call(s32[1]{0:T(128)} %bitcast.5.place.refs_0_.refs_1_, bf16[192,2048]{1,0:T(8,128)(2,1)} %copy-done.57, bf16[192,2048]{1,0:T(8,128)(2,1)} %collective-permute-done.27.by_y.refs_1_.refs_2_, bf16[192,2048]{1,0:T(8,128)(2,1)} %copy-done.37, ...), custom_call_target="tpu_custom_call" | custom-call | flops 16106127360 | bytes 27262976 | tf_op jit(solution)/shard_map/glu_second/pallas_call | solution.py:84
  295.9 5.7 %collective-permute-done.41.refs_1_ = bf16[768,2048]{1,0:T(8,128)(2,1)S(1)} collective-permute-done((bf16[768,2048]{1,0:T(8,128)(2,1)}, bf16[768,2048]{1,0:T(8,128)(2,1)S(1)}, u32[]{:S(2)}, u32[]{:S(2)}) %collective-permute-start.41) | collective-permute-done | bytes 3145760 | tf_op jit(solution)/shard_map/ppermute | solution.py:1129
  301.7 1.9 copy-done.17
  308.7 16.3 %glu_third.1 = (bf16[2048,1024]{1,0:T(8,128)(2,1)}, f32[8,128]{1,0:T(8,128)}) custom-call(s32[1]{0:T(128)} %bitcast.5.place.refs_0_.refs_1_, bf16[192,2048]{1,0:T(8,128)(2,1)} %copy-done.57, bf16[192,2048]{1,0:T(8,128)(2,1)} %collective-permute-done.27.by_y.refs_1_.refs_2_, bf16[192,2048]{1,0:T(8,128)(2,1)} %copy-done.37, ...), custom_call_target="tpu_custom_call" | custom-call | flops 6442450944 | bytes 16777216 | tf_op jit(solution)/shard_map/glu_third/pallas_call | solution.py:84
  334.2 8.3 %collective-permute-done.44.refs_6_ = bf16[96,2048]{1,0:T(8,128)(2,1)S(1)} collective-permute-done((bf16[96,2048]{1,0:T(8,128)(2,1)S(1)}, bf16[96,2048]{1,0:T(8,128)(2,1)S(1)}, u32[]{:S(2)}, u32[]{:S(2)}) %collective-permute-start.44) | collective-permute-done | bytes 393248 | tf_op jit(solution)/shard_map/ppermute | solution.py:1129
  348.4 12.1 %output_parts.1 = (bf16[768,2048]{1,0:T(8,128)(2,1)}, bf16[768,2048]{1,0:T(8,128)(2,1)}, f32[8,128]{1,0:T(8,128)}) custom-call(s32[1]{0:T(128)} %bitcast.5.place.refs_0_.refs_1_, bf16[2048,1152]{1,0:T(8,128)(2,1)} %all-gather.6.cloned.1.call-done.refs_20_.refs_1_, bf16[2048,1024]{1,0:T(8,128)(2,1)} %all-gather.8.cloned.1.call-done.refs_21_.refs_2_, ...), custom_call_target="tpu_custom_call" | custom-call | flops 4831838208 | bytes 9437184 | tf_op jit(solution)/shard_map/output_parts/pallas_call | solution.py:84
  360.5 4.4 collective-permute-done.47.refs_1_.refs_0_.refs_11_
  370.5 9.0 %collective-permute-done.49.refs_2_.refs_12_ = bf16[96,2176]{1,0:T(8,128)(2,1)S(1)} collective-permute-done((bf16[96,2176]{1,0:T(8,128)(2,1)S(1)}, bf16[96,2176]{1,0:T(8,128)(2,1)S(1)}, u32[]{:S(2)}, u32[]{:S(2)}) %collective-permute-start.49) | collective-permute-done | bytes 417824 | tf_op jit(solution)/shard_map/ppermute | solution.py:1129
  380.9 1.9 copy-done.14
  387.9 29.3 %mixer_backward.1 = (bf16[1536,768]{1,0:T(8,128)(2,1)}, bf16[256,2176]{1,0:T(8,128)(2,1)}, bf16[2048,768]{1,0:T(8,128)(2,1)}) custom-call(s32[8]{0:T(128)} %add.84.slots.refs_0_, s32[1]{0:T(128)} %bitcast.5.place.refs_0_.refs_1_, f32[1,256]{1,0:T(1,128)} %slice.23.gains.refs_2_, f32[1536,256]{1,0:T(8,128)} %get-tuple-element.143.refs_3_, ...), custom_call_target="tpu_custom_call" | custom-call | flops 8053063680 | bytes 28573696 | tf_op jit(solution)/shard_map/mixer_backward/pallas_call | solution.py:84
  417.3 10.5 %mixed_grad_parts.1 = (bf16[768,2048]{1,0:T(8,128)(2,1)}, bf16[768,2048]{1,0:T(8,128)(2,1)}) custom-call(s32[1]{0:T(128)} %bitcast.5.place.refs_0_.refs_1_, bf16[1536,768]{1,0:T(8,128)(2,1)} %get-tuple-element.149.grads, bf16[512,768]{1,0:T(8,128)(2,1)} %bitcast.6.refs_10_.refs_0_, bf16[512,768]{1,0:T(8,128)(2,1)} %pin.7.refs_11_.refs_3_.refs_1_.refs_0_, ...), custom_call_target="tpu_custom_call" | custom-call | flops 4831838208 | bytes 12582912 | tf_op jit(solution)/shard_map/mixed_grad_parts/pallas_call | solution.py:84
  429.6 4.1 collective-permute-done.60.refs_1_
  433.7 1.9 copy-done.16
  442.9 3.6 all-to-all-start.3
  455.8 9.6 %collective-permute-done.61.top_in = bf16[192,2048]{1,0:T(8,128)(2,1)} collective-permute-done((bf16[192,2048]{1,0:T(8,128)(2,1)}, bf16[192,2048]{1,0:T(8,128)(2,1)}, u32[]{:S(2)}, u32[]{:S(2)}) %collective-permute-start.61) | collective-permute-done | bytes 786464 | tf_op jit(solution)/shard_map/ppermute | solution.py:1129
  466.2 2.4 chip_sum.7
  470.7 2.1 collective-permute-start.64
  472.8 14.4 %collective-permute-done.53.refs_1_ = bf16[96,2048]{1,0:T(8,128)(2,1)S(1)} collective-permute-done((bf16[96,2048]{1,0:T(8,128)(2,1)S(1)}, bf16[96,2048]{1,0:T(8,128)(2,1)S(1)}, u32[]{:S(2)}, u32[]{:S(2)}) %collective-permute-start.53) | collective-permute-done | bytes 393248 | tf_op jit(solution)/shard_map/ppermute | solution.py:1129
  488.3 6.7 %collective-permute-done.63.refs_4_ = bf16[96,2048]{1,0:T(8,128)(2,1)} collective-permute-done((bf16[96,2048]{1,0:T(8,128)(2,1)}, bf16[96,2048]{1,0:T(8,128)(2,1)}, u32[]{:S(2)}, u32[]{:S(2)}) %collective-permute-start.63) | collective-permute-done | bytes 393248 | tf_op jit(solution)/shard_map/ppermute | solution.py:1129
  499.0 2.8 grad_tokens.1
  503.1 18.0 %all_to_all.30.refs_0_.second = bf16[8,64,1024]{2,1,0:T(8,128)(2,1)} all-to-all(bf16[8,64,1024]{2,1,0:T(8,128)(2,1)S(1)} %hold.5), channel_id=1, replica_groups=mesh['y'=2,'core'=2,'z'=4,'x'=2] {'y','core','x'}, dimensions={0} | all-to-all | bytes 2097152 | tf_op jit(solution)/shard_map/all_to_all | solution.py:1195
  521.2 4.4 all-to-all-start.5
  532.0 2.3 from_hidden.1
  535.0 2.7 all-to-all-done.5.grads
  540.5 2.7 from_channels.1
  (361 shorter events, 131.5 us)
Async XLA Ops:
  7.2 31.7 %all-gather.4.cloned.1.call-start = ((), (), s32[]{:S(2)}) async-start(), calls=%async_computation.10 | async-start | bytes 1310720 | tf_op jit(solution)/shard_map/all_gather | solution.py:1310
  14.7 22.0 %all-to-all-start = ((bf16[8,64,768]{2,1,0:T(8,128)(2,1)}), bf16[8,64,768]{2,1,0:T(8,128)(2,1)}, u32[]{:S(2)}, u32[]{:S(2)}) async-start(bf16[8,64,768]{2,1,0:T(8,128)(2,1)} %to_channels.1), calls=%async_computation | async-start | bytes 1572864 | tf_op jit(solution)/shard_map/all_to_all | solution.py:1195
  39.3 20.6 %collective-permute-start.7 = (bf16[192,2048]{1,0:T(8,128)(2,1)S(1)}, bf16[192,2048]{1,0:T(8,128)(2,1)}, u32[]{:S(2)}, u32[]{:S(2)}) collective-permute-start(bf16[192,2048]{1,0:T(8,128)(2,1)S(1)} %mixed_in.1.refs_3_.refs_2_.refs_0_.refs_20_), channel_id=1, source_target_pairs={{0,1},{1,0},{2,3},{3,2},{4,5},{5,4},{6,7},{7,6},{8,9},{9,8},{10,11... | collective-permute-start | bytes 2359304 | tf_op jit(solution)/shard_map/ppermute | solution.py:1129
  40.7 20.6 %collective-permute-start.6 = (bf16[192,2048]{1,0:T(8,128)(2,1)S(1)}, bf16[192,2048]{1,0:T(8,128)(2,1)}, u32[]{:S(2)}, u32[]{:S(2)}) collective-permute-start(bf16[192,2048]{1,0:T(8,128)(2,1)S(1)} %mixed_in.1.refs_3_.refs_2_.refs_0_.refs_20_), channel_id=1, source_target_pairs={{0,16},{16,0},{1,17},{17,1},{2,18},{18,2},{3,19},{19,3},{4,20},{20... | collective-permute-start | bytes 2359304 | tf_op jit(solution)/shard_map/ppermute | solution.py:1129
  42.2 22.2 %collective-permute-start.10 = (bf16[192,2048]{1,0:T(8,128)(2,1)S(1)}, bf16[192,2048]{1,0:T(8,128)(2,1)}, u32[]{:S(2)}, u32[]{:S(2)}) collective-permute-start(bf16[192,2048]{1,0:T(8,128)(2,1)S(1)} %mixed_in.1.refs_3_.refs_2_.refs_0_.refs_20_), channel_id=1, source_target_pairs={{0,8},{8,0},{1,9},{9,1},{2,10},{10,2},{3,11},{11,3},{4,12},{12,4},... | collective-permute-start | bytes 2359304 | tf_op jit(solution)/shard_map/ppermute | solution.py:1129
  42.2 25.4 %collective-permute-start.16 = (bf16[512,768]{1,0:T(8,128)(2,1)}, bf16[512,768]{1,0:T(8,128)(2,1)}, u32[]{:S(2)}, u32[]{:S(2)}) collective-permute-start(bf16[512,768]{1,0:T(8,128)(2,1)} %bitcast.6.refs_10_.refs_0_), channel_id=1, source_target_pairs={{0,6},{2,0},{4,2},{6,4},{1,7},{3,1},{5,3},{7,5},{8,14},{10,8},{12,... | collective-permute-start | bytes 2359304 | tf_op jit(solution)/shard_map/ppermute | solution.py:1201
  45.6 35.7 %all-to-all-start.1 = ((bf16[8,64,1152]{2,1,0:T(8,128)(2,1)}), bf16[8,64,1152]{2,1,0:T(8,128)(2,1)}, u32[]{:S(2)}, u32[]{:S(2)}) async-start(bf16[8,64,1152]{2,1,0:T(8,128)(2,1)} %copy-done.11), calls=%async_computation.1 | async-start | bytes 2359296 | tf_op jit(solution)/shard_map/all_to_all | solution.py:1195
  49.9 190.9 %all-gather.6.cloned.1.call-start = ((), (), s32[]{:S(2)}) async-start(), calls=%async_computation.11 | async-start | bytes 5898240 | tf_op jit(solution)/shard_map/all_gather | solution.py:1284
  49.9 31.4 %collective-permute-start.15 = (bf16[512,768]{1,0:T(8,128)(2,1)}, bf16[512,768]{1,0:T(8,128)(2,1)S(1)}, u32[]{:S(2)}, u32[]{:S(2)}) collective-permute-start(bf16[512,768]{1,0:T(8,128)(2,1)} %bitcast.6.refs_10_.refs_0_), channel_id=1, source_target_pairs={{0,2},{2,4},{4,6},{6,0},{1,3},{3,5},{5,7},{7,1},{8,10},{10,12},{12... | collective-permute-start | bytes 2359304 | tf_op jit(solution)/shard_map/ppermute | solution.py:1201
  62.7 18.1 %collective-permute-start.8 = (bf16[96,2048]{1,0:T(8,128)(2,1)S(1)}, bf16[96,2048]{1,0:T(8,128)(2,1)S(1)}, u32[]{:S(2)}, u32[]{:S(2)}) collective-permute-start(bf16[96,2048]{1,0:T(8,128)(2,1)S(1)} %get-tuple-element.95), channel_id=1, source_target_pairs={{0,16},{16,0},{1,17},{17,1},{2,18},{18,2},{3,19},{19,3},{4,20},{20... | collective-permute-start | bytes 1179656 | tf_op jit(solution)/shard_map/ppermute | solution.py:1129
  64.5 16.9 %collective-permute-start.12 = (bf16[192,2048]{1,0:T(8,128)(2,1)}, bf16[192,2048]{1,0:T(8,128)(2,1)}, u32[]{:S(2)}, u32[]{:S(2)}) collective-permute-start(bf16[192,2048]{1,0:T(8,128)(2,1)} %collective-permute-done.7.by_x.refs_4_.refs_2_.refs_22_), channel_id=1, source_target_pairs={{0,8},{8,0},{1,9},{9,1},{2,10},{10,2},{3,11},{11,3},{4,12},{12,4},... | collective-permute-start | bytes 2359304 | tf_op jit(solution)/shard_map/ppermute | solution.py:1129
  64.5 16.4 %collective-permute-start.9 = (bf16[96,2048]{1,0:T(8,128)(2,1)S(1)}, bf16[96,2048]{1,0:T(8,128)(2,1)}, u32[]{:S(2)}, u32[]{:S(2)}) collective-permute-start(bf16[96,2048]{1,0:T(8,128)(2,1)S(1)} %get-tuple-element.96), channel_id=1, source_target_pairs={{0,1},{1,0},{2,3},{3,2},{4,5},{5,4},{6,7},{7,6},{8,9},{9,8},{10,11... | collective-permute-start | bytes 1179656 | tf_op jit(solution)/shard_map/ppermute | solution.py:1129
  67.7 15.8 %collective-permute-start.11 = (bf16[192,2048]{1,0:T(8,128)(2,1)}, bf16[192,2048]{1,0:T(8,128)(2,1)S(1)}, u32[]{:S(2)}, u32[]{:S(2)}) collective-permute-start(bf16[192,2048]{1,0:T(8,128)(2,1)} %collective-permute-done.6.by_y.refs_3_.refs_1_.refs_21_), channel_id=1, source_target_pairs={{0,8},{8,0},{1,9},{9,1},{2,10},{10,2},{3,11},{11,3},{4,12},{12,4},... | collective-permute-start | bytes 2359304 | tf_op jit(solution)/shard_map/ppermute | solution.py:1129
  87.5 24.3 %collective-permute-start.19 = (bf16[192,2048]{1,0:T(8,128)(2,1)}, bf16[192,2048]{1,0:T(8,128)(2,1)}, u32[]{:S(2)}, u32[]{:S(2)}) collective-permute-start(bf16[192,2048]{1,0:T(8,128)(2,1)} %hold.3.refs_10_.refs_11_), channel_id=1, source_target_pairs={{0,16},{16,0},{1,17},{17,1},{2,18},{18,2},{3,19},{19,3},{4,20},{20... | collective-permute-start | bytes 2359304 | tf_op jit(solution)/shard_map/ppermute | solution.py:1129
  89.0 22.8 %collective-permute-start.18 = (bf16[192,2048]{1,0:T(8,128)(2,1)}, bf16[192,2048]{1,0:T(8,128)(2,1)}, u32[]{:S(2)}, u32[]{:S(2)}) collective-permute-start(bf16[192,2048]{1,0:T(8,128)(2,1)} %hold.3.refs_10_.refs_11_), channel_id=1, source_target_pairs={{0,1},{1,0},{2,3},{3,2},{4,5},{5,4},{6,7},{7,6},{8,9},{9,8},{10,11... | collective-permute-start | bytes 2359304 | tf_op jit(solution)/shard_map/ppermute | solution.py:1129
  89.6 50.0 %collective-permute-start.17 = (bf16[512,768]{1,0:T(8,128)(2,1)S(1)}, bf16[512,768]{1,0:T(8,128)(2,1)}, u32[]{:S(2)}, u32[]{:S(2)}) collective-permute-start(bf16[512,768]{1,0:T(8,128)(2,1)S(1)} %copy-done.2), channel_id=1, source_target_pairs={{0,2},{2,4},{4,6},{6,0},{1,3},{3,5},{5,7},{7,1},{8,10},{10,12},{12... | collective-permute-start | bytes 2359304 | tf_op jit(solution)/shard_map/ppermute | solution.py:1201
  91.2 18.6 %collective-permute-start.5 = (s32[1,4]{1,0:T(1,128)S(1)}, s32[1,4]{1,0:T(1,128)S(1)}, u32[]{:S(2)}, u32[]{:S(2)}) collective-permute-start(s32[1,4]{1,0:T(1,128)S(1)} %reduce_window_sum.11), channel_id=1, source_target_pairs={{0,1},{1,0},{2,3},{3,2},{4,5},{5,4},{6,7},{7,6},{8,9},{9,8},{10,11... | collective-permute-start | bytes 56 | tf_op jit(solution)/shard_map/ppermute | solution.py:1129
  95.1 60.2 %all-to-all-start.2 = ((bf16[8,64,1024]{2,1,0:T(8,128)(2,1)}), bf16[8,64,1024]{2,1,0:T(8,128)(2,1)}, u32[]{:S(2)}, u32[]{:S(2)}) async-start(bf16[8,64,1024]{2,1,0:T(8,128)(2,1)} %copy-done.12), calls=%async_computation.2 | async-start | bytes 2097152 | tf_op jit(solution)/shard_map/all_to_all | solution.py:1195
  99.3 168.8 %all-gather.8.cloned.1.call-start = ((), (), s32[]{:S(2)}) async-start(), calls=%async_computation.12 | async-start | bytes 5242880 | tf_op jit(solution)/shard_map/all_gather | solution.py:1284
  113.2 42.0 %collective-permute-start.20 = (bf16[96,2048]{1,0:T(8,128)(2,1)S(1)}, bf16[96,2048]{1,0:T(8,128)(2,1)S(1)}, u32[]{:S(2)}, u32[]{:S(2)}) collective-permute-start(bf16[96,2048]{1,0:T(8,128)(2,1)S(1)} %get-tuple-element.99), channel_id=1, source_target_pairs={{0,16},{16,0},{1,17},{17,1},{2,18},{18,2},{3,19},{19,3},{4,20},{20... | collective-permute-start | bytes 1179656 | tf_op jit(solution)/shard_map/ppermute | solution.py:1129
  113.9 41.5 %collective-permute-start.21 = (bf16[96,2048]{1,0:T(8,128)(2,1)S(1)}, bf16[96,2048]{1,0:T(8,128)(2,1)S(1)}, u32[]{:S(2)}, u32[]{:S(2)}) collective-permute-start(bf16[96,2048]{1,0:T(8,128)(2,1)S(1)} %get-tuple-element.100), channel_id=1, source_target_pairs={{0,1},{1,0},{2,3},{3,2},{4,5},{5,4},{6,7},{7,6},{8,9},{9,8},{10,11... | collective-permute-start | bytes 1179656 | tf_op jit(solution)/shard_map/ppermute | solution.py:1129
  162.4 278.1 %reduce-scatter.5.cloned.1.call-start = ((), (), s32[]{:S(2)}) async-start(), calls=%async_computation.13 | async-start | bytes 5898240 | tf_op jit(solution)/shard_map/reduce_scatter | solution.py:1212
  174.1 20.6 %collective-permute-start.23 = (bf16[192,2176]{1,0:T(8,128)(2,1)S(1)}, bf16[192,2176]{1,0:T(8,128)(2,1)S(1)}, u32[]{:S(2)}, u32[]{:S(2)}) collective-permute-start(bf16[192,2176]{1,0:T(8,128)(2,1)S(1)} %get-tuple-element.105), channel_id=1, source_target_pairs={{0,1},{1,0},{2,3},{3,2},{4,5},{5,4},{6,7},{7,6},{8,9},{9,8},{10,11... | collective-permute-start | bytes 2506760 | tf_op jit(solution)/shard_map/ppermute | solution.py:1129
  175.3 20.4 %collective-permute-start.24 = (bf16[192,2176]{1,0:T(8,128)(2,1)S(1)}, bf16[192,2176]{1,0:T(8,128)(2,1)S(1)}, u32[]{:S(2)}, u32[]{:S(2)}) collective-permute-start(bf16[192,2176]{1,0:T(8,128)(2,1)S(1)} %get-tuple-element.106), channel_id=1, source_target_pairs={{0,16},{16,0},{1,17},{17,1},{2,18},{18,2},{3,19},{19,3},{4,20},{20... | collective-permute-start | bytes 2506760 | tf_op jit(solution)/shard_map/ppermute | solution.py:1129
  207.7 17.7 %collective-permute-start.28 = (bf16[192,2048]{1,0:T(8,128)(2,1)S(1)}, bf16[192,2048]{1,0:T(8,128)(2,1)S(1)}, u32[]{:S(2)}, u32[]{:S(2)}) collective-permute-start(bf16[192,2048]{1,0:T(8,128)(2,1)S(1)} %get-tuple-element.111.refs_0_.refs_1_), channel_id=1, source_target_pairs={{0,1},{1,0},{2,3},{3,2},{4,5},{5,4},{6,7},{7,6},{8,9},{9,8},{10,11... | collective-permute-start | bytes 2359304 | tf_op jit(solution)/shard_map/ppermute | solution.py:1129
  208.6 17.5 %collective-permute-start.27 = (bf16[192,2048]{1,0:T(8,128)(2,1)S(1)}, bf16[192,2048]{1,0:T(8,128)(2,1)}, u32[]{:S(2)}, u32[]{:S(2)}) collective-permute-start(bf16[192,2048]{1,0:T(8,128)(2,1)S(1)} %get-tuple-element.111.refs_0_.refs_1_), channel_id=1, source_target_pairs={{0,16},{16,0},{1,17},{17,1},{2,18},{18,2},{3,19},{19,3},{4,20},{20... | collective-permute-start | bytes 2359304 | tf_op jit(solution)/shard_map/ppermute | solution.py:1129
  210.0 17.3 %collective-permute-start.36 = (bf16[192,2048]{1,0:T(8,128)(2,1)}, bf16[192,2048]{1,0:T(8,128)(2,1)S(1)}, u32[]{:S(2)}, u32[]{:S(2)}) collective-permute-start(bf16[192,2048]{1,0:T(8,128)(2,1)} %hold.3.refs_10_.refs_11_), channel_id=1, source_target_pairs={{0,8},{8,0},{1,9},{9,1},{2,10},{10,2},{3,11},{11,3},{4,12},{12,4},... | collective-permute-start | bytes 2359304 | tf_op jit(solution)/shard_map/ppermute | solution.py:1129
  210.0 17.9 %collective-permute-start.37 = (bf16[192,2048]{1,0:T(8,128)(2,1)}, bf16[192,2048]{1,0:T(8,128)(2,1)S(1)}, u32[]{:S(2)}, u32[]{:S(2)}) collective-permute-start(bf16[192,2048]{1,0:T(8,128)(2,1)} %collective-permute-done.19.by_y.refs_11_.refs_12_), channel_id=1, source_target_pairs={{0,8},{8,0},{1,9},{9,1},{2,10},{10,2},{3,11},{11,3},{4,12},{12,4},... | collective-permute-start | bytes 2359304 | tf_op jit(solution)/shard_map/ppermute | solution.py:1129
  210.6 18.4 %collective-permute-start.38 = (bf16[192,2048]{1,0:T(8,128)(2,1)}, bf16[192,2048]{1,0:T(8,128)(2,1)S(1)}, u32[]{:S(2)}, u32[]{:S(2)}) collective-permute-start(bf16[192,2048]{1,0:T(8,128)(2,1)} %collective-permute-done.18.by_x.refs_12_.refs_13_), channel_id=1, source_target_pairs={{0,8},{8,0},{1,9},{9,1},{2,10},{10,2},{3,11},{11,3},{4,12},{12,4},... | collective-permute-start | bytes 2359304 | tf_op jit(solution)/shard_map/ppermute | solution.py:1129
  267.9 233.9 %reduce-scatter.9.cloned.1.call-start = ((), (), s32[]{:S(2)}) async-start(), calls=%async_computation.15 | async-start | bytes 5242880 | tf_op jit(solution)/shard_map/reduce_scatter | solution.py:1212
  306.6 19.6 %collective-permute-start.42 = (bf16[192,2048]{1,0:T(8,128)(2,1)S(1)}, bf16[192,2048]{1,0:T(8,128)(2,1)S(1)}, u32[]{:S(2)}, u32[]{:S(2)}) collective-permute-start(bf16[192,2048]{1,0:T(8,128)(2,1)S(1)} %get-tuple-element.121), channel_id=1, source_target_pairs={{0,1},{1,0},{2,3},{3,2},{4,5},{5,4},{6,7},{7,6},{8,9},{9,8},{10,11... | collective-permute-start | bytes 2359304 | tf_op jit(solution)/shard_map/ppermute | solution.py:1129
  307.8 19.4 %collective-permute-start.43 = (bf16[192,2048]{1,0:T(8,128)(2,1)S(1)}, bf16[192,2048]{1,0:T(8,128)(2,1)}, u32[]{:S(2)}, u32[]{:S(2)}) collective-permute-start(bf16[192,2048]{1,0:T(8,128)(2,1)S(1)} %get-tuple-element.122), channel_id=1, source_target_pairs={{0,16},{16,0},{1,17},{17,1},{2,18},{18,2},{3,19},{19,3},{4,20},{20... | collective-permute-start | bytes 2359304 | tf_op jit(solution)/shard_map/ppermute | solution.py:1129
  327.3 193.9 %reduce-scatter.7.cloned.1.call-start = ((), (), s32[]{:S(2)}) async-start(), calls=%async_computation.14 | async-start | bytes 3932160 | tf_op jit(solution)/shard_map/reduce_scatter | solution.py:1212
  346.2 18.8 %collective-permute-start.47 = (bf16[192,2176]{1,0:T(8,128)(2,1)S(1)}, bf16[192,2176]{1,0:T(8,128)(2,1)}, u32[]{:S(2)}, u32[]{:S(2)}) collective-permute-start(bf16[192,2176]{1,0:T(8,128)(2,1)S(1)} %get-tuple-element.131.refs_9_), channel_id=1, source_target_pairs={{0,1},{1,0},{2,3},{3,2},{4,5},{5,4},{6,7},{7,6},{8,9},{9,8},{10,11... | collective-permute-start | bytes 2506760 | tf_op jit(solution)/shard_map/ppermute | solution.py:1129
  347.3 18.6 %collective-permute-start.46 = (bf16[192,2176]{1,0:T(8,128)(2,1)S(1)}, bf16[192,2176]{1,0:T(8,128)(2,1)}, u32[]{:S(2)}, u32[]{:S(2)}) collective-permute-start(bf16[192,2176]{1,0:T(8,128)(2,1)S(1)} %get-tuple-element.131.refs_9_), channel_id=1, source_target_pairs={{0,16},{16,0},{1,17},{17,1},{2,18},{18,2},{3,19},{19,3},{4,20},{20... | collective-permute-start | bytes 2506760 | tf_op jit(solution)/shard_map/ppermute | solution.py:1129
  370.0 16.1 %collective-permute-start.55 = (bf16[192,2176]{1,0:T(8,128)(2,1)S(1)}, bf16[192,2176]{1,0:T(8,128)(2,1)S(1)}, u32[]{:S(2)}, u32[]{:S(2)}) collective-permute-start(bf16[192,2176]{1,0:T(8,128)(2,1)S(1)} %copy-done.56), channel_id=1, source_target_pairs={{0,8},{8,0},{1,9},{9,1},{2,10},{10,2},{3,11},{11,3},{4,12},{12,4},... | collective-permute-start | bytes 2506760 | tf_op jit(solution)/shard_map/ppermute | solution.py:1129
  370.0 16.1 %collective-permute-start.57 = (bf16[192,2176]{1,0:T(8,128)(2,1)}, bf16[192,2176]{1,0:T(8,128)(2,1)S(1)}, u32[]{:S(2)}, u32[]{:S(2)}) collective-permute-start(bf16[192,2176]{1,0:T(8,128)(2,1)} %collective-permute-done.47.refs_1_.refs_0_.refs_11_), channel_id=1, source_target_pairs={{0,8},{8,0},{1,9},{9,1},{2,10},{10,2},{3,11},{11,3},{4,12},{12,4},... | collective-permute-start | bytes 2506760 | tf_op jit(solution)/shard_map/ppermute | solution.py:1129
  427.9 20.7 %collective-permute-start.51 = (bf16[192,2048]{1,0:T(8,128)(2,1)}, bf16[192,2048]{1,0:T(8,128)(2,1)}, u32[]{:S(2)}, u32[]{:S(2)}) collective-permute-start(bf16[192,2048]{1,0:T(8,128)(2,1)} %get-tuple-element.137), channel_id=1, source_target_pairs={{0,1},{1,0},{2,3},{3,2},{4,5},{5,4},{6,7},{7,6},{8,9},{9,8},{10,11... | collective-permute-start | bytes 2359304 | tf_op jit(solution)/shard_map/ppermute | solution.py:1129
  428.7 20.7 %collective-permute-start.52 = (bf16[192,2048]{1,0:T(8,128)(2,1)}, bf16[192,2048]{1,0:T(8,128)(2,1)}, u32[]{:S(2)}, u32[]{:S(2)}) collective-permute-start(bf16[192,2048]{1,0:T(8,128)(2,1)} %get-tuple-element.138), channel_id=1, source_target_pairs={{0,16},{16,0},{1,17},{17,1},{2,18},{18,2},{3,19},{19,3},{4,20},{20... | collective-permute-start | bytes 2359304 | tf_op jit(solution)/shard_map/ppermute | solution.py:1129
  439.0 26.5 %collective-permute-start.61 = (bf16[192,2048]{1,0:T(8,128)(2,1)}, bf16[192,2048]{1,0:T(8,128)(2,1)}, u32[]{:S(2)}, u32[]{:S(2)}) collective-permute-start(bf16[192,2048]{1,0:T(8,128)(2,1)} %get-tuple-element.154), channel_id=1, source_target_pairs={{0,1},{1,0},{2,3},{3,2},{4,5},{5,4},{6,7},{7,6},{8,9},{9,8},{10,11... | collective-permute-start | bytes 2359304 | tf_op jit(solution)/shard_map/ppermute | solution.py:1129
  439.7 26.5 %collective-permute-start.62 = (bf16[192,2048]{1,0:T(8,128)(2,1)}, bf16[192,2048]{1,0:T(8,128)(2,1)}, u32[]{:S(2)}, u32[]{:S(2)}) collective-permute-start(bf16[192,2048]{1,0:T(8,128)(2,1)} %get-tuple-element.155), channel_id=1, source_target_pairs={{0,16},{16,0},{1,17},{17,1},{2,18},{18,2},{3,19},{19,3},{4,20},{20... | collective-permute-start | bytes 2359304 | tf_op jit(solution)/shard_map/ppermute | solution.py:1129
  442.9 45.4 %all-to-all-start.3 = ((bf16[8,64,1152]{2,1,0:T(8,128)(2,1)}), bf16[8,64,1152]{2,1,0:T(8,128)(2,1)S(1)}, u32[]{:S(2)}, u32[]{:S(2)}) async-start(bf16[8,64,1152]{2,1,0:T(8,128)(2,1)} %copy-done.10), calls=%async_computation.4 | async-start | bytes 2359296 | tf_op jit(solution)/shard_map/all_to_all | solution.py:1195
  446.5 80.4 %reduce-scatter.11.cloned.1.call-start = ((), (), s32[]{:S(2)}) async-start(), calls=%async_computation.16 | async-start | bytes 1392640 | tf_op jit(solution)/shard_map/reduce_scatter | solution.py:1212
  453.5 33.7 %collective-permute-start.53 = (bf16[96,2048]{1,0:T(8,128)(2,1)S(1)}, bf16[96,2048]{1,0:T(8,128)(2,1)S(1)}, u32[]{:S(2)}, u32[]{:S(2)}) collective-permute-start(bf16[96,2048]{1,0:T(8,128)(2,1)S(1)} %get-tuple-element.140), channel_id=1, source_target_pairs={{0,16},{16,0},{1,17},{17,1},{2,18},{18,2},{3,19},{19,3},{4,20},{20... | collective-permute-start | bytes 1179656 | tf_op jit(solution)/shard_map/ppermute | solution.py:1129
  454.5 32.7 %collective-permute-start.54 = (bf16[96,2048]{1,0:T(8,128)(2,1)S(1)}, bf16[96,2048]{1,0:T(8,128)(2,1)S(1)}, u32[]{:S(2)}, u32[]{:S(2)}) collective-permute-start(bf16[96,2048]{1,0:T(8,128)(2,1)S(1)} %get-tuple-element.141), channel_id=1, source_target_pairs={{0,1},{1,0},{2,3},{3,2},{4,5},{5,4},{6,7},{7,6},{8,9},{9,8},{10,11... | collective-permute-start | bytes 1179656 | tf_op jit(solution)/shard_map/ppermute | solution.py:1129
  469.8 25.2 %collective-permute-start.63 = (bf16[96,2048]{1,0:T(8,128)(2,1)}, bf16[96,2048]{1,0:T(8,128)(2,1)}, u32[]{:S(2)}, u32[]{:S(2)}) collective-permute-start(bf16[96,2048]{1,0:T(8,128)(2,1)} %get-tuple-element.157), channel_id=1, source_target_pairs={{0,16},{16,0},{1,17},{17,1},{2,18},{18,2},{3,19},{19,3},{4,20},{20... | collective-permute-start | bytes 1179656 | tf_op jit(solution)/shard_map/ppermute | solution.py:1129
  470.7 24.3 %collective-permute-start.64 = (bf16[96,2048]{1,0:T(8,128)(2,1)}, bf16[96,2048]{1,0:T(8,128)(2,1)}, u32[]{:S(2)}, u32[]{:S(2)}) collective-permute-start(bf16[96,2048]{1,0:T(8,128)(2,1)} %get-tuple-element.158), channel_id=1, source_target_pairs={{0,1},{1,0},{2,3},{3,2},{4,5},{5,4},{6,7},{7,6},{8,9},{9,8},{10,11... | collective-permute-start | bytes 1179656 | tf_op jit(solution)/shard_map/ppermute | solution.py:1129
  521.2 16.5 %all-to-all-start.5 = ((bf16[8,64,768]{2,1,0:T(8,128)(2,1)}), bf16[8,64,768]{2,1,0:T(8,128)(2,1)}, u32[]{:S(2)}, u32[]{:S(2)}) async-start(bf16[8,64,768]{2,1,0:T(8,128)(2,1)} %pin.11), calls=%async_computation.8 | async-start | bytes 1572864 | tf_op jit(solution)/shard_map/all_to_all | solution.py:1195
  (116 other events, 669.1 us)
Sparse Core Ops, SparseCore 0:
  9.6 29.2 all-gather.3
  84.5 102.4 all-gather.5
  188.6 78.3 all-gather.7
  269.2 85.7 reduce-scatter.4
  357.1 77.2 reduce-scatter.8
  436.7 60.2 reduce-scatter.6
  500.0 26.8 reduce-scatter.10

commit v4 on v3

--- a/solution.py
+++ b/solution.py
@@ -202,6 +202,19 @@
             send(staged.at[rows], out.at[rows], sem)
 
 
+def row_sums(values):
+    lanes = values[:, :128]
+    for first in range(128, values.shape[1], 128):
+        lanes = lanes + values[:, first : first + 128]
+    ones = jnp.ones((8, 128), LOW)
+    total = jnp.zeros((8, values.shape[0]), F32)
+    for _ in range(3):
+        high = lanes.astype(LOW)
+        total = total + product_nt(ones, high)
+        lanes = lanes - high.astype(F32)
+    return total[0:1]
+
+
 def to_channels_kernel(layout, *refs):
     *weights, out = refs
     block, width = layout.block, layout.block * layout.planes
@@ -220,7 +233,7 @@
     count = (len(refs) - 1) // 2
     weights, outs, gain_out = refs[:count], refs[count:-1], refs[-1]
     block, width = layout.block, layout.block * layout.planes
-    total = jnp.zeros((block, 1), F32)
+    total = jnp.zeros((1, block), F32)
     for i, (weight, out) in enumerate(zip(weights, outs)):
         for s in range(layout.seq):
             for z in range(layout.planes):
@@ -230,7 +243,7 @@
                     out[:, first : first + block] = grads[
                         s * layout.buckets + x, :, at : at + block
                     ].astype(F32)
-        total = total + jnp.sum(out[...] * weight[...].astype(F32), axis=1, keepdims=True)
+        total = total + row_sums(out[...] * weight[...].astype(F32))
     gain_out[...] = total / gains[...]
 
 
@@ -250,24 +263,25 @@
     *weights, gate_out, up_out, down_out, gain_out = refs
     split, rest = layout.split, layout.rest
     share = split + rest
-    total = jnp.zeros((layout.block, 1), F32)
+    total = jnp.zeros((1, layout.block), F32)
     for i, out in enumerate((gate_out, up_out, down_out)):
         for part in range(layout.parts):
             at = part * share
             out[:, at : at + split] = first[part, :, i * split : (i + 1) * split].astype(F32)
             out[:, at + split : at + share] = second[part, :, i * rest : (i + 1) * rest].astype(F32)
         if i < len(weights):
-            total = total + jnp.sum(out[...] * weights[i][...].astype(F32), axis=1, keepdims=True)
+            total = total + row_sums(out[...] * weights[i][...].astype(F32))
     gain_out[...] = total / gains[...]
 
 
 def channel_gain_kernel(grads, weight, gains, floors, out, gain_out, floor_out):
     width = weight.shape[1]
     out[...] = grads[:, :width].astype(F32)
-    total = jnp.sum(out[...] * weight[...].astype(F32), axis=1, keepdims=True)
-    gain_out[...] = total / gains[...]
+    gain_out[...] = row_sums(out[...] * weight[...].astype(F32)) / gains[...]
     floor = jax.nn.sigmoid(floors[...])
-    floor_out[...] = grads[:, width : width + 1].astype(F32) * floor * (1.0 - floor)
+    lane = lax.broadcasted_iota(jnp.int32, (grads.shape[0], 128), 1)
+    total = row_sums(jnp.where(lane == 0, grads[:, width:].astype(F32), 0.0))
+    floor_out[...] = total * floor * (1.0 - floor)
 
 
 def hold_kernel(value, out):
@@ -1377,17 +1391,18 @@
     mixer_grads, out_grads, mixer_weight_grads = mixer_backward(
         layout, slots, place, gain_out, saved, grads_low, out_weights, mixed, output[-1:]
     )
-    mixer_weight_grads = scatter_weights(mixer_weight_grads)
+    output = links.sum_chips(output, links.swap_chips(output))
+    mixer_weight_grads = scatter_weights(pin(mixer_weight_grads, output[:1]))
     out_grads = links.sum_planes(out_grads)
     mixed_parts = links.sum_cores(
-        mixed_grad_parts(layout, place, mixer_grads, mixer, width, [])
-    )
-    first_grads = links.exchange(hold(first_grads, mixed_parts[-1:]))
-    output = links.sum_chips(output, links.swap_chips(output))
+        mixed_grad_parts(layout, place, mixer_grads, mixer, width, output[:1])
+    )
+    first_grads = links.exchange(hold(first_grads, output[:1]))
     (output,) = call(
         output_rows_kernel, "output_rows", [low_wide], [residual, *output], cost=row_cost
     )
     grad_mixed = links.sum_chips(mixed_parts, links.swap_chips(mixed_parts))
+    second_grads = links.exchange(hold(second_grads, [first_grads]))
     grad_tokens, token = call(
         grad_tokens_kernel,
         "grad_tokens",
@@ -1395,32 +1410,33 @@
         [tokens, gain_mix, grad_residual, *grad_mixed],
         cost=row_cost,
         token=True,
-        after=[output, first_grads],
-    )
-    second_grads = links.exchange(hold(second_grads, [token]))
-    mixer_weight_grads = links.exchange(pin(mixer_weight_grads, [second_grads]))
-
-    def as_column(vector):
-        return vector.astype(F32).reshape(block, 1)
-
-    square, long, single = ((block, width), F32), ((block, hidden), F32), ((block, 1), F32)
+        after=[output],
+    )
+    mixer_weight_grads = links.exchange(pin(mixer_weight_grads, [token, second_grads]))
+
+    def as_row(vector):
+        return vector.astype(F32).reshape(1, block)
+
+    square, long, single = ((block, width), F32), ((block, hidden), F32), ((1, block), F32)
     gate_w, up_w, down_w, grad_g_ffn = call(
         functools.partial(from_hidden_kernel, layout),
         "from_hidden",
         [long] * 3 + [single],
-        [first_grads, second_grads, as_column(g_ffn), w_gate, w_up],
+        [first_grads, second_grads, as_row(g_ffn), w_gate, w_up],
+    )
+    in_w, forget_w, gate_out_w, grad_g_mix = call(
+        functools.partial(from_channels_kernel, layout),
+        "from_channels",
+        [square] * 3 + [single],
+        [mixer_weight_grads, as_row(g_mix), w_in, w_forget, w_gate_out],
+        after=[grad_g_ffn],
     )
     out_w, grad_g_out, grad_floor = call(
         channel_gain_kernel,
         "from_out",
         [square, single, single],
-        [out_grads, w_out, as_column(g_out), as_column(floor_logit)],
-    )
-    in_w, forget_w, gate_out_w, grad_g_mix = call(
-        functools.partial(from_channels_kernel, layout),
-        "from_channels",
-        [square] * 3 + [single],
-        [mixer_weight_grads, as_column(g_mix), w_in, w_forget, w_gate_out],
+        [out_grads, w_out, as_row(g_out), as_row(floor_logit)],
+        after=[grad_g_mix],
     )
     return (
         output[None],

time: 561 us -> 546 us (0.973)
  blocking collectives: 18 us -> 0 us
  local copies, waits for them, and re-layouts: 51.7 us -> 40.3 us
  waiting for transfers between devices: 214 us -> 224 us
  starting transfers between devices: 71.1 us -> 77.2 us
    all_to_all x1 -> x0, blocking collectives: 18 us -> none  [exchange(): lax.all_to_all(value, self.owners, split_axis=0, concat_axis=0, tiled=True)]
    all_to_all x5 -> x6, waiting for transfers between devices: 2.69 us -> 14 us  [exchange(): lax.all_to_all(value, self.owners, split_axis=0, concat_axis=0, tiled=True)]
    unnamed x174 -> x170, local copies, waits for them, and re-layouts: 49 us -> 38 us
    ppermute x60, waiting for transfers between devices: 177 us -> 168 us  [swap(): return lax.ppermute(value, axis, SWAP)]
    reduce_scatter x4, waiting for transfers between devices: 0.93 us -> 7.78 us  [sum_planes(): return lax.psum_scatter(value, 'z', scatter_dimension=0, tiled=True)]
    all_to_all x5 -> x6, starting transfers between devices: 20.8 us -> 25.4 us  [exchange(): lax.all_to_all(value, self.owners, split_axis=0, concat_axis=0, tiled=True)]
  transfers between devices with their start and end apart: 77 -> 78, of which waited for: 41 -> 40; matrix products, arithmetic and copies ran while one was open for 1% -> 1% of each run, Pallas kernels for 31% -> 33%
where the time goes in v4:
time: 546 us; the launch traced here: 536 us
  waiting for transfers between devices  224 us (41%)
  Pallas kernels  177 us (32%)
  starting transfers between devices  77.2 us (14%)
  local copies, waits for them, and re-layouts  40.3 us (7%)
  between operations  15.7 us (3%)
    pallas_call x34, Pallas kernels, call(): pl.pallas_call(kernel, out_shape=tuple((jax.ShapeDtypeStruct(*out) for ou...  177 us
    ppermute x60, waiting for transfers between devices, swap(): return lax.ppermute(value, axis, SWAP)  168 us
    ppermute x60, starting transfers between devices, swap(): return lax.ppermute(value, axis, SWAP)  45.6 us
    unnamed x170, local copies, waits for them, and re-layouts  38 us
    all_to_all x6, starting transfers between devices, exchange(): lax.all_to_all(value, self.owners, split_axis=0, concat_axis=0, tiled=True)  25.4 us
    ppermute x3, waiting for transfers between devices, shift(): lax.ppermute(value, 'z', [(i, (i + by) % planes) for i in range(planes)])  24.8 us
    all_to_all x6, waiting for transfers between devices, exchange(): lax.all_to_all(value, self.owners, split_axis=0, concat_axis=0, tiled=True)  14 us
  transfers between devices with their start and end apart: 78, of which 40 were waited for; matrix products, arithmetic and copies ran while one was open for 1% of the time, Pallas kernels for 33%

profile of v4, /device:TPU:16, one launch (start us, length us, event | category | flops | bytes accessed | tf_op | source)
XLA Modules:
  0.0 536.1 jit_solution(17110041986757901008)
XLA Ops:
  14.8 4.4 all-to-all-start
  19.8 5.3 collective-permute-done.1
  25.1 1.9 collective-permute-start.2
  27.1 4.4 collective-permute-done.2
  33.0 2.4 collective-permute-done.3
  36.8 2.2 all-gather.4.cloned.1.call-done.refs_1_.refs_3_.refs_19_
  45.6 4.3 all-to-all-start.1
  51.0 8.8 %collective-permute-done.7.by_x.refs_4_.refs_2_.refs_22_ = bf16[192,2048]{1,0:T(8,128)(2,1)} collective-permute-done((bf16[192,2048]{1,0:T(8,128)(2,1)S(1)}, bf16[192,2048]{1,0:T(8,128)(2,1)}, u32[]{:S(2)}, u32[]{:S(2)}) %collective-permute-start.7) | collective-permute-done | bytes 786464 | tf_op jit(solution)/shard_map/ppermute | solution.py:1143
  64.4 3.3 collective-permute-start.9
  67.9 12.9 %collective-permute-done.8.refs_5_.refs_3_.refs_23_ = bf16[96,2048]{1,0:T(8,128)(2,1)S(1)} collective-permute-done((bf16[96,2048]{1,0:T(8,128)(2,1)S(1)}, bf16[96,2048]{1,0:T(8,128)(2,1)S(1)}, u32[]{:S(2)}, u32[]{:S(2)}) %collective-permute-start.8) | collective-permute-done | bytes 393248 | tf_op jit(solution)/shard_map/ppermute | solution.py:1143
  95.1 4.2 all-to-all-start.2
  100.1 9.6 %collective-permute-done.5 = s32[1,4]{1,0:T(1,128)S(1)} collective-permute-done((s32[1,4]{1,0:T(1,128)S(1)}, s32[1,4]{1,0:T(1,128)S(1)}, u32[]{:S(2)}, u32[]{:S(2)}) %collective-permute-start.5) | collective-permute-done | bytes 48 | tf_op jit(solution)/shard_map/ppermute | solution.py:1143
  114.7 24.8 %collective-permute-done.17.refs_12_.refs_4_ = bf16[512,768]{1,0:T(8,128)(2,1)} collective-permute-done((bf16[512,768]{1,0:T(8,128)(2,1)S(1)}, bf16[512,768]{1,0:T(8,128)(2,1)}, u32[]{:S(2)}, u32[]{:S(2)}) %collective-permute-start.17) | collective-permute-done | bytes 786464 | tf_op jit(solution)/shard_map/ppermute | solution.py:1215
  139.5 15.6 %mixer_forward.1 = (f32[1536,256]{1,0:T(8,128)}, f32[1536,256]{1,0:T(8,128)}, f32[1536,256]{1,0:T(8,128)}, f32[1536,256]{1,0:T(8,128)}, f32[1536,256]{1,0:T(8,12...) custom-call(s32[8]{0:T(128)} %add.84.slots.refs_0_, s32[2,4]{1,0:T(2,128)} %add_select_fusion.ends, ...), custom_call_target="tpu_custom_call" | custom-call | flops 4831838208 | bytes 18874368 | tf_op jit(solution)/shard_map/mixer_forward/pallas_call | solution.py:84
  156.0 6.2 %branch_parts.1 = (bf16[768,2176]{1,0:T(8,128)(2,1)}, bf16[768,2176]{1,0:T(8,128)(2,1)}) custom-call(s32[1]{0:T(128)} %bitcast.5.place.refs_0_.refs_1_, bf16[1536,256]{1,0:T(8,128)(2,1)} %get-tuple-element.96.refs_1_, bf16[1536,256]{1,0:T(8,128)(2,1)} %get-tuple-element.97.refs_2_.refs_4_, ...), custom_call_target="tpu_custom_call" | custom-call | flops 1610612736 | bytes 7340032 | tf_op jit(solution)/shard_map/branch_parts/pallas_call | solution.py:84
  162.6 6.0 %collective-permute-done.22.refs_1_ = bf16[768,2176]{1,0:T(8,128)(2,1)} collective-permute-done((bf16[768,2176]{1,0:T(8,128)(2,1)}, bf16[768,2176]{1,0:T(8,128)(2,1)}, u32[]{:S(2)}, u32[]{:S(2)}) %collective-permute-start.22) | collective-permute-done | bytes 3342368 | tf_op jit(solution)/shard_map/ppermute | solution.py:1143
  168.6 1.9 copy-done.15
  170.5 3.5 core_sum.4
  175.3 19.3 %collective-permute-done.23.top_in = bf16[192,2176]{1,0:T(8,128)(2,1)S(1)} collective-permute-done((bf16[192,2176]{1,0:T(8,128)(2,1)S(1)}, bf16[192,2176]{1,0:T(8,128)(2,1)S(1)}, u32[]{:S(2)}, u32[]{:S(2)}) %collective-permute-start.23) | collective-permute-done | bytes 835616 | tf_op jit(solution)/shard_map/ppermute | solution.py:1143
  197.1 9.5 %collective-permute-done.25.refs_1_ = bf16[96,2176]{1,0:T(8,128)(2,1)S(1)} collective-permute-done((bf16[96,2176]{1,0:T(8,128)(2,1)S(1)}, bf16[96,2176]{1,0:T(8,128)(2,1)S(1)}, u32[]{:S(2)}, u32[]{:S(2)}) %collective-permute-start.25) | collective-permute-done | bytes 417824 | tf_op jit(solution)/shard_map/ppermute | solution.py:1143
  210.5 15.0 %collective-permute-done.28.by_x.refs_2_.refs_3_ = bf16[192,2048]{1,0:T(8,128)(2,1)S(1)} collective-permute-done((bf16[192,2048]{1,0:T(8,128)(2,1)S(1)}, bf16[192,2048]{1,0:T(8,128)(2,1)S(1)}, u32[]{:S(2)}, u32[]{:S(2)}) %collective-permute-start.28) | collective-permute-done | bytes 786464 | tf_op jit(solution)/shard_map/ppermute | solution.py:1143
  230.5 8.5 %collective-permute-done.29.refs_3_.refs_4_ = bf16[96,2048]{1,0:T(8,128)(2,1)} collective-permute-done((bf16[96,2048]{1,0:T(8,128)(2,1)S(1)}, bf16[96,2048]{1,0:T(8,128)(2,1)}, u32[]{:S(2)}, u32[]{:S(2)}) %collective-permute-start.29) | collective-permute-done | bytes 393248 | tf_op jit(solution)/shard_map/ppermute | solution.py:1143
  242.7 25.1 %glu_first.1 = (bf16[1536,1152]{1,0:T(8,128)(2,1)}, bf16[2048,1152]{1,0:T(8,128)(2,1)}) custom-call(s32[1]{0:T(128)} %bitcast.5.place.refs_0_.refs_1_, bf16[192,2048]{1,0:T(8,128)(2,1)} %copy-done.54, bf16[192,2048]{1,0:T(8,128)(2,1)} %collective-permute-done.27.by_y.refs_1_.refs_2_, bf16[192,2048]{1,0:T(8,128)(2,1)} %copy-done.37, ...), custom_call_target="tpu_custom_call" | custom-call | flops 14495514624 | bytes 22020096 | tf_op jit(solution)/shard_map/glu_first/pallas_call | solution.py:84
  268.1 27.6 %glu_second.1 = (bf16[1536,1024]{1,0:T(8,128)(2,1)}, bf16[768,2048]{1,0:T(8,128)(2,1)}, bf16[768,2048]{1,0:T(8,128)(2,1)}) custom-call(s32[1]{0:T(128)} %bitcast.5.place.refs_0_.refs_1_, bf16[192,2048]{1,0:T(8,128)(2,1)} %copy-done.54, bf16[192,2048]{1,0:T(8,128)(2,1)} %collective-permute-done.27.by_y.refs_1_.refs_2_, bf16[192,2048]{1,0:T(8,128)(2,1)} %copy-done.37, ...), custom_call_target="tpu_custom_call" | custom-call | flops 16106127360 | bytes 27262976 | tf_op jit(solution)/shard_map/glu_second/pallas_call | solution.py:84
  295.9 5.7 %collective-permute-done.41.refs_1_ = bf16[768,2048]{1,0:T(8,128)(2,1)S(1)} collective-permute-done((bf16[768,2048]{1,0:T(8,128)(2,1)}, bf16[768,2048]{1,0:T(8,128)(2,1)S(1)}, u32[]{:S(2)}, u32[]{:S(2)}) %collective-permute-start.41) | collective-permute-done | bytes 3145760 | tf_op jit(solution)/shard_map/ppermute | solution.py:1143
  301.6 1.9 copy-done.18
  308.3 16.3 %glu_third.1 = (bf16[2048,1024]{1,0:T(8,128)(2,1)}, f32[8,128]{1,0:T(8,128)}) custom-call(s32[1]{0:T(128)} %bitcast.5.place.refs_0_.refs_1_, bf16[192,2048]{1,0:T(8,128)(2,1)} %copy-done.54, bf16[192,2048]{1,0:T(8,128)(2,1)} %collective-permute-done.27.by_y.refs_1_.refs_2_, bf16[192,2048]{1,0:T(8,128)(2,1)} %copy-done.37, ...), custom_call_target="tpu_custom_call" | custom-call | flops 6442450944 | bytes 16777216 | tf_op jit(solution)/shard_map/glu_third/pallas_call | solution.py:84
  333.7 8.2 %collective-permute-done.44.refs_6_ = bf16[96,2048]{1,0:T(8,128)(2,1)S(1)} collective-permute-done((bf16[96,2048]{1,0:T(8,128)(2,1)S(1)}, bf16[96,2048]{1,0:T(8,128)(2,1)S(1)}, u32[]{:S(2)}, u32[]{:S(2)}) %collective-permute-start.44) | collective-permute-done | bytes 393248 | tf_op jit(solution)/shard_map/ppermute | solution.py:1143
  348.0 12.1 %output_parts.1 = (bf16[768,2048]{1,0:T(8,128)(2,1)}, bf16[768,2048]{1,0:T(8,128)(2,1)}, f32[8,128]{1,0:T(8,128)}) custom-call(s32[1]{0:T(128)} %bitcast.5.place.refs_0_.refs_1_, bf16[2048,1152]{1,0:T(8,128)(2,1)} %all-gather.6.cloned.1.call-done.refs_20_.refs_1_, bf16[2048,1024]{1,0:T(8,128)(2,1)} %all-gather.8.cloned.1.call-done.refs_21_.refs_2_, ...), custom_call_target="tpu_custom_call" | custom-call | flops 4831838208 | bytes 9437184 | tf_op jit(solution)/shard_map/output_parts/pallas_call | solution.py:84
  360.1 4.1 collective-permute-done.47.refs_1_.refs_0_.refs_11_
  369.8 9.3 %collective-permute-done.49.refs_2_.refs_12_ = bf16[96,2176]{1,0:T(8,128)(2,1)S(1)} collective-permute-done((bf16[96,2176]{1,0:T(8,128)(2,1)S(1)}, bf16[96,2176]{1,0:T(8,128)(2,1)S(1)}, u32[]{:S(2)}, u32[]{:S(2)}) %collective-permute-start.49) | collective-permute-done | bytes 417824 | tf_op jit(solution)/shard_map/ppermute | solution.py:1143
  381.4 1.9 copy-done.16
  387.4 29.3 %mixer_backward.1 = (bf16[1536,768]{1,0:T(8,128)(2,1)}, bf16[256,2176]{1,0:T(8,128)(2,1)}, bf16[2048,768]{1,0:T(8,128)(2,1)}) custom-call(s32[8]{0:T(128)} %add.84.slots.refs_0_, s32[1]{0:T(128)} %bitcast.5.place.refs_0_.refs_1_, f32[1,256]{1,0:T(1,128)} %slice.23.gains.refs_2_, f32[1536,256]{1,0:T(8,128)} %get-tuple-element.142.refs_3_, ...), custom_call_target="tpu_custom_call" | custom-call | flops 8053063680 | bytes 28573696 | tf_op jit(solution)/shard_map/mixer_backward/pallas_call | solution.py:84
  419.1 10.6 %mixed_grad_parts.1 = (bf16[768,2048]{1,0:T(8,128)(2,1)}, bf16[768,2048]{1,0:T(8,128)(2,1)}) custom-call(s32[1]{0:T(128)} %bitcast.5.place.refs_0_.refs_1_, bf16[1536,768]{1,0:T(8,128)(2,1)} %get-tuple-element.148.refs_1_, bf16[512,768]{1,0:T(8,128)(2,1)} %bitcast.6.refs_10_.refs_2_, bf16[512,768]{1,0:T(8,128)(2,1)} %pin.8.refs_11_.refs_3_.refs_1_.refs_0_, ...), custom_call_target="tpu_custom_call" | custom-call | flops 4831838208 | bytes 12582912 | tf_op jit(solution)/shard_map/mixed_grad_parts/pallas_call | solution.py:84
  432.1 4.3 all-to-all-start.3
  437.2 1.9 copy-done.17
  439.0 3.2 core_sum.7
  443.1 1.9 collective-permute-start.61
  446.5 6.2 %all-to-all-done.3.refs_1_.first = bf16[8,64,1152]{2,1,0:T(8,128)(2,1)} async-done(((bf16[8,64,1152]{2,1,0:T(8,128)(2,1)}), bf16[8,64,1152]{2,1,0:T(8,128)(2,1)}, u32[]{:S(2)}, u32[]{:S(2)}) %all-to-all-start.3) | async-done | bytes 1179680 | tf_op jit(solution)/shard_map/all_to_all | solution.py:1209
  455.0 4.5 all-to-all-start.4
  459.5 2.0 collective-permute-start.53
  463.0 6.5 %collective-permute-done.61.top_in = bf16[192,2048]{1,0:T(8,128)(2,1)} collective-permute-done((bf16[192,2048]{1,0:T(8,128)(2,1)}, bf16[192,2048]{1,0:T(8,128)(2,1)}, u32[]{:S(2)}, u32[]{:S(2)}) %collective-permute-start.61) | collective-permute-done | bytes 786464 | tf_op jit(solution)/shard_map/ppermute | solution.py:1143
  474.6 14.6 %collective-permute-done.53.refs_1_ = bf16[96,2048]{1,0:T(8,128)(2,1)S(1)} collective-permute-done((bf16[96,2048]{1,0:T(8,128)(2,1)}, bf16[96,2048]{1,0:T(8,128)(2,1)S(1)}, u32[]{:S(2)}, u32[]{:S(2)}) %collective-permute-start.53) | collective-permute-done | bytes 393248 | tf_op jit(solution)/shard_map/ppermute | solution.py:1143
  490.3 6.8 %collective-permute-done.63.refs_4_ = bf16[96,2048]{1,0:T(8,128)(2,1)S(1)} collective-permute-done((bf16[96,2048]{1,0:T(8,128)(2,1)S(1)}, bf16[96,2048]{1,0:T(8,128)(2,1)S(1)}, u32[]{:S(2)}, u32[]{:S(2)}) %collective-permute-start.63) | collective-permute-done | bytes 393248 | tf_op jit(solution)/shard_map/ppermute | solution.py:1143
  500.7 3.7 all-to-all-start.5
  504.5 4.1 from_hidden.1
  508.6 7.8 %all-to-all-done.5.refs_0_ = bf16[8,64,768]{2,1,0:T(8,128)(2,1)S(1)} async-done(((bf16[8,64,768]{2,1,0:T(8,128)(2,1)}), bf16[8,64,768]{2,1,0:T(8,128)(2,1)S(1)}, u32[]{:S(2)}, u32[]{:S(2)}) %all-to-all-start.5) | async-done | bytes 786464 | tf_op jit(solution)/shard_map/all_to_all | solution.py:1209
  518.5 7.7 %reduce-scatter.11.cloned.1.call-done.refs_0_ = bf16[64,2176]{1,0:T(8,128)(2,1)} async-done(((bf16[256,2176]{1,0:T(8,128)(2,1)}), bf16[64,2176]{1,0:T(8,128)(2,1)}) %reduce-scatter.11.cloned.1.call-update) | async-done | bytes 278544 | tf_op jit(solution)/shard_map/reduce_scatter | solution.py:1226
  (350 shorter events, 119.0 us)
Async XLA Ops:
  7.2 31.7 %all-gather.4.cloned.1.call-start = ((), (), s32[]{:S(2)}) async-start(), calls=%async_computation.10 | async-start | bytes 1310720 | tf_op jit(solution)/shard_map/all_gather | solution.py:1324
  14.8 22.0 %all-to-all-start = ((bf16[8,64,768]{2,1,0:T(8,128)(2,1)}), bf16[8,64,768]{2,1,0:T(8,128)(2,1)}, u32[]{:S(2)}, u32[]{:S(2)}) async-start(bf16[8,64,768]{2,1,0:T(8,128)(2,1)} %to_channels.1), calls=%async_computation | async-start | bytes 1572864 | tf_op jit(solution)/shard_map/all_to_all | solution.py:1209
  39.3 20.6 %collective-permute-start.7 = (bf16[192,2048]{1,0:T(8,128)(2,1)S(1)}, bf16[192,2048]{1,0:T(8,128)(2,1)}, u32[]{:S(2)}, u32[]{:S(2)}) collective-permute-start(bf16[192,2048]{1,0:T(8,128)(2,1)S(1)} %mixed_in.1.refs_3_.refs_2_.refs_0_.refs_20_), channel_id=1, source_target_pairs={{0,1},{1,0},{2,3},{3,2},{4,5},{5,4},{6,7},{7,6},{8,9},{9,8},{10,11... | collective-permute-start | bytes 2359304 | tf_op jit(solution)/shard_map/ppermute | solution.py:1143
  40.7 20.6 %collective-permute-start.6 = (bf16[192,2048]{1,0:T(8,128)(2,1)S(1)}, bf16[192,2048]{1,0:T(8,128)(2,1)}, u32[]{:S(2)}, u32[]{:S(2)}) collective-permute-start(bf16[192,2048]{1,0:T(8,128)(2,1)S(1)} %mixed_in.1.refs_3_.refs_2_.refs_0_.refs_20_), channel_id=1, source_target_pairs={{0,16},{16,0},{1,17},{17,1},{2,18},{18,2},{3,19},{19,3},{4,20},{20... | collective-permute-start | bytes 2359304 | tf_op jit(solution)/shard_map/ppermute | solution.py:1143
  42.2 22.2 %collective-permute-start.10 = (bf16[192,2048]{1,0:T(8,128)(2,1)S(1)}, bf16[192,2048]{1,0:T(8,128)(2,1)}, u32[]{:S(2)}, u32[]{:S(2)}) collective-permute-start(bf16[192,2048]{1,0:T(8,128)(2,1)S(1)} %mixed_in.1.refs_3_.refs_2_.refs_0_.refs_20_), channel_id=1, source_target_pairs={{0,8},{8,0},{1,9},{9,1},{2,10},{10,2},{3,11},{11,3},{4,12},{12,4},... | collective-permute-start | bytes 2359304 | tf_op jit(solution)/shard_map/ppermute | solution.py:1143
  42.2 25.5 %collective-permute-start.16 = (bf16[512,768]{1,0:T(8,128)(2,1)}, bf16[512,768]{1,0:T(8,128)(2,1)}, u32[]{:S(2)}, u32[]{:S(2)}) collective-permute-start(bf16[512,768]{1,0:T(8,128)(2,1)} %bitcast.6.refs_10_.refs_2_), channel_id=1, source_target_pairs={{0,6},{2,0},{4,2},{6,4},{1,7},{3,1},{5,3},{7,5},{8,14},{10,8},{12,... | collective-permute-start | bytes 2359304 | tf_op jit(solution)/shard_map/ppermute | solution.py:1215
  45.6 35.7 %all-to-all-start.1 = ((bf16[8,64,1152]{2,1,0:T(8,128)(2,1)}), bf16[8,64,1152]{2,1,0:T(8,128)(2,1)}, u32[]{:S(2)}, u32[]{:S(2)}) async-start(bf16[8,64,1152]{2,1,0:T(8,128)(2,1)} %copy-done.13), calls=%async_computation.1 | async-start | bytes 2359296 | tf_op jit(solution)/shard_map/all_to_all | solution.py:1209
  49.9 190.8 %all-gather.6.cloned.1.call-start = ((), (), s32[]{:S(2)}) async-start(), calls=%async_computation.11 | async-start | bytes 5898240 | tf_op jit(solution)/shard_map/all_gather | solution.py:1298
  50.0 31.4 %collective-permute-start.15 = (bf16[512,768]{1,0:T(8,128)(2,1)}, bf16[512,768]{1,0:T(8,128)(2,1)S(1)}, u32[]{:S(2)}, u32[]{:S(2)}) collective-permute-start(bf16[512,768]{1,0:T(8,128)(2,1)} %bitcast.6.refs_10_.refs_2_), channel_id=1, source_target_pairs={{0,2},{2,4},{4,6},{6,0},{1,3},{3,5},{5,7},{7,1},{8,10},{10,12},{12... | collective-permute-start | bytes 2359304 | tf_op jit(solution)/shard_map/ppermute | solution.py:1215
  62.7 18.1 %collective-permute-start.8 = (bf16[96,2048]{1,0:T(8,128)(2,1)S(1)}, bf16[96,2048]{1,0:T(8,128)(2,1)S(1)}, u32[]{:S(2)}, u32[]{:S(2)}) collective-permute-start(bf16[96,2048]{1,0:T(8,128)(2,1)S(1)} %get-tuple-element.94), channel_id=1, source_target_pairs={{0,16},{16,0},{1,17},{17,1},{2,18},{18,2},{3,19},{19,3},{4,20},{20... | collective-permute-start | bytes 1179656 | tf_op jit(solution)/shard_map/ppermute | solution.py:1143
  64.4 17.0 %collective-permute-start.12 = (bf16[192,2048]{1,0:T(8,128)(2,1)}, bf16[192,2048]{1,0:T(8,128)(2,1)}, u32[]{:S(2)}, u32[]{:S(2)}) collective-permute-start(bf16[192,2048]{1,0:T(8,128)(2,1)} %collective-permute-done.7.by_x.refs_4_.refs_2_.refs_22_), channel_id=1, source_target_pairs={{0,8},{8,0},{1,9},{9,1},{2,10},{10,2},{3,11},{11,3},{4,12},{12,4},... | collective-permute-start | bytes 2359304 | tf_op jit(solution)/shard_map/ppermute | solution.py:1143
  64.4 16.4 %collective-permute-start.9 = (bf16[96,2048]{1,0:T(8,128)(2,1)S(1)}, bf16[96,2048]{1,0:T(8,128)(2,1)}, u32[]{:S(2)}, u32[]{:S(2)}) collective-permute-start(bf16[96,2048]{1,0:T(8,128)(2,1)S(1)} %get-tuple-element.95), channel_id=1, source_target_pairs={{0,1},{1,0},{2,3},{3,2},{4,5},{5,4},{6,7},{7,6},{8,9},{9,8},{10,11... | collective-permute-start | bytes 1179656 | tf_op jit(solution)/shard_map/ppermute | solution.py:1143
  67.7 15.7 %collective-permute-start.11 = (bf16[192,2048]{1,0:T(8,128)(2,1)}, bf16[192,2048]{1,0:T(8,128)(2,1)S(1)}, u32[]{:S(2)}, u32[]{:S(2)}) collective-permute-start(bf16[192,2048]{1,0:T(8,128)(2,1)} %collective-permute-done.6.by_y.refs_3_.refs_1_.refs_21_), channel_id=1, source_target_pairs={{0,8},{8,0},{1,9},{9,1},{2,10},{10,2},{3,11},{11,3},{4,12},{12,4},... | collective-permute-start | bytes 2359304 | tf_op jit(solution)/shard_map/ppermute | solution.py:1143
  87.5 24.3 %collective-permute-start.19 = (bf16[192,2048]{1,0:T(8,128)(2,1)}, bf16[192,2048]{1,0:T(8,128)(2,1)}, u32[]{:S(2)}, u32[]{:S(2)}) collective-permute-start(bf16[192,2048]{1,0:T(8,128)(2,1)} %hold.3.refs_10_.refs_11_), channel_id=1, source_target_pairs={{0,16},{16,0},{1,17},{17,1},{2,18},{18,2},{3,19},{19,3},{4,20},{20... | collective-permute-start | bytes 2359304 | tf_op jit(solution)/shard_map/ppermute | solution.py:1143
  89.0 22.8 %collective-permute-start.18 = (bf16[192,2048]{1,0:T(8,128)(2,1)}, bf16[192,2048]{1,0:T(8,128)(2,1)}, u32[]{:S(2)}, u32[]{:S(2)}) collective-permute-start(bf16[192,2048]{1,0:T(8,128)(2,1)} %hold.3.refs_10_.refs_11_), channel_id=1, source_target_pairs={{0,1},{1,0},{2,3},{3,2},{4,5},{5,4},{6,7},{7,6},{8,9},{9,8},{10,11... | collective-permute-start | bytes 2359304 | tf_op jit(solution)/shard_map/ppermute | solution.py:1143
  89.6 50.0 %collective-permute-start.17 = (bf16[512,768]{1,0:T(8,128)(2,1)S(1)}, bf16[512,768]{1,0:T(8,128)(2,1)}, u32[]{:S(2)}, u32[]{:S(2)}) collective-permute-start(bf16[512,768]{1,0:T(8,128)(2,1)S(1)} %copy-done.3), channel_id=1, source_target_pairs={{0,2},{2,4},{4,6},{6,0},{1,3},{3,5},{5,7},{7,1},{8,10},{10,12},{12... | collective-permute-start | bytes 2359304 | tf_op jit(solution)/shard_map/ppermute | solution.py:1215
  91.2 18.6 %collective-permute-start.5 = (s32[1,4]{1,0:T(1,128)S(1)}, s32[1,4]{1,0:T(1,128)S(1)}, u32[]{:S(2)}, u32[]{:S(2)}) collective-permute-start(s32[1,4]{1,0:T(1,128)S(1)} %reduce_window_sum.11), channel_id=1, source_target_pairs={{0,1},{1,0},{2,3},{3,2},{4,5},{5,4},{6,7},{7,6},{8,9},{9,8},{10,11... | collective-permute-start | bytes 56 | tf_op jit(solution)/shard_map/ppermute | solution.py:1143
  95.1 60.0 %all-to-all-start.2 = ((bf16[8,64,1024]{2,1,0:T(8,128)(2,1)}), bf16[8,64,1024]{2,1,0:T(8,128)(2,1)}, u32[]{:S(2)}, u32[]{:S(2)}) async-start(bf16[8,64,1024]{2,1,0:T(8,128)(2,1)} %copy-done.14), calls=%async_computation.2 | async-start | bytes 2097152 | tf_op jit(solution)/shard_map/all_to_all | solution.py:1209
  99.4 168.7 %all-gather.8.cloned.1.call-start = ((), (), s32[]{:S(2)}) async-start(), calls=%async_computation.12 | async-start | bytes 5242880 | tf_op jit(solution)/shard_map/all_gather | solution.py:1298
  113.2 41.9 %collective-permute-start.20 = (bf16[96,2048]{1,0:T(8,128)(2,1)S(1)}, bf16[96,2048]{1,0:T(8,128)(2,1)S(1)}, u32[]{:S(2)}, u32[]{:S(2)}) collective-permute-start(bf16[96,2048]{1,0:T(8,128)(2,1)S(1)} %get-tuple-element.98), channel_id=1, source_target_pairs={{0,16},{16,0},{1,17},{17,1},{2,18},{18,2},{3,19},{19,3},{4,20},{20... | collective-permute-start | bytes 1179656 | tf_op jit(solution)/shard_map/ppermute | solution.py:1143
  113.8 41.3 %collective-permute-start.21 = (bf16[96,2048]{1,0:T(8,128)(2,1)S(1)}, bf16[96,2048]{1,0:T(8,128)(2,1)S(1)}, u32[]{:S(2)}, u32[]{:S(2)}) collective-permute-start(bf16[96,2048]{1,0:T(8,128)(2,1)S(1)} %get-tuple-element.99), channel_id=1, source_target_pairs={{0,1},{1,0},{2,3},{3,2},{4,5},{5,4},{6,7},{7,6},{8,9},{9,8},{10,11... | collective-permute-start | bytes 1179656 | tf_op jit(solution)/shard_map/ppermute | solution.py:1143
  162.3 267.4 %reduce-scatter.9.cloned.1.call-start = ((), (), s32[]{:S(2)}) async-start(), calls=%async_computation.15 | async-start | bytes 5898240 | tf_op jit(solution)/shard_map/reduce_scatter | solution.py:1226
  174.0 20.6 %collective-permute-start.23 = (bf16[192,2176]{1,0:T(8,128)(2,1)S(1)}, bf16[192,2176]{1,0:T(8,128)(2,1)S(1)}, u32[]{:S(2)}, u32[]{:S(2)}) collective-permute-start(bf16[192,2176]{1,0:T(8,128)(2,1)S(1)} %get-tuple-element.104), channel_id=1, source_target_pairs={{0,1},{1,0},{2,3},{3,2},{4,5},{5,4},{6,7},{7,6},{8,9},{9,8},{10,11... | collective-permute-start | bytes 2506760 | tf_op jit(solution)/shard_map/ppermute | solution.py:1143
  175.3 20.4 %collective-permute-start.24 = (bf16[192,2176]{1,0:T(8,128)(2,1)S(1)}, bf16[192,2176]{1,0:T(8,128)(2,1)S(1)}, u32[]{:S(2)}, u32[]{:S(2)}) collective-permute-start(bf16[192,2176]{1,0:T(8,128)(2,1)S(1)} %get-tuple-element.105), channel_id=1, source_target_pairs={{0,16},{16,0},{1,17},{17,1},{2,18},{18,2},{3,19},{19,3},{4,20},{20... | collective-permute-start | bytes 2506760 | tf_op jit(solution)/shard_map/ppermute | solution.py:1143
  207.7 17.7 %collective-permute-start.28 = (bf16[192,2048]{1,0:T(8,128)(2,1)S(1)}, bf16[192,2048]{1,0:T(8,128)(2,1)S(1)}, u32[]{:S(2)}, u32[]{:S(2)}) collective-permute-start(bf16[192,2048]{1,0:T(8,128)(2,1)S(1)} %get-tuple-element.110.refs_0_.refs_1_), channel_id=1, source_target_pairs={{0,1},{1,0},{2,3},{3,2},{4,5},{5,4},{6,7},{7,6},{8,9},{9,8},{10,11... | collective-permute-start | bytes 2359304 | tf_op jit(solution)/shard_map/ppermute | solution.py:1143
  208.5 17.5 %collective-permute-start.27 = (bf16[192,2048]{1,0:T(8,128)(2,1)S(1)}, bf16[192,2048]{1,0:T(8,128)(2,1)}, u32[]{:S(2)}, u32[]{:S(2)}) collective-permute-start(bf16[192,2048]{1,0:T(8,128)(2,1)S(1)} %get-tuple-element.110.refs_0_.refs_1_), channel_id=1, source_target_pairs={{0,16},{16,0},{1,17},{17,1},{2,18},{18,2},{3,19},{19,3},{4,20},{20... | collective-permute-start | bytes 2359304 | tf_op jit(solution)/shard_map/ppermute | solution.py:1143
  209.9 17.2 %collective-permute-start.36 = (bf16[192,2048]{1,0:T(8,128)(2,1)}, bf16[192,2048]{1,0:T(8,128)(2,1)S(1)}, u32[]{:S(2)}, u32[]{:S(2)}) collective-permute-start(bf16[192,2048]{1,0:T(8,128)(2,1)} %hold.3.refs_10_.refs_11_), channel_id=1, source_target_pairs={{0,8},{8,0},{1,9},{9,1},{2,10},{10,2},{3,11},{11,3},{4,12},{12,4},... | collective-permute-start | bytes 2359304 | tf_op jit(solution)/shard_map/ppermute | solution.py:1143
  209.9 17.8 %collective-permute-start.37 = (bf16[192,2048]{1,0:T(8,128)(2,1)}, bf16[192,2048]{1,0:T(8,128)(2,1)S(1)}, u32[]{:S(2)}, u32[]{:S(2)}) collective-permute-start(bf16[192,2048]{1,0:T(8,128)(2,1)} %collective-permute-done.19.by_y.refs_11_.refs_12_), channel_id=1, source_target_pairs={{0,8},{8,0},{1,9},{9,1},{2,10},{10,2},{3,11},{11,3},{4,12},{12,4},... | collective-permute-start | bytes 2359304 | tf_op jit(solution)/shard_map/ppermute | solution.py:1143
  210.4 18.4 %collective-permute-start.38 = (bf16[192,2048]{1,0:T(8,128)(2,1)}, bf16[192,2048]{1,0:T(8,128)(2,1)S(1)}, u32[]{:S(2)}, u32[]{:S(2)}) collective-permute-start(bf16[192,2048]{1,0:T(8,128)(2,1)} %collective-permute-done.18.by_x.refs_12_.refs_13_), channel_id=1, source_target_pairs={{0,8},{8,0},{1,9},{9,1},{2,10},{10,2},{3,11},{11,3},{4,12},{12,4},... | collective-permute-start | bytes 2359304 | tf_op jit(solution)/shard_map/ppermute | solution.py:1143
  267.8 184.9 %reduce-scatter.7.cloned.1.call-start = ((), (), s32[]{:S(2)}) async-start(), calls=%async_computation.14 | async-start | bytes 5242880 | tf_op jit(solution)/shard_map/reduce_scatter | solution.py:1226
  306.0 19.6 %collective-permute-start.42 = (bf16[192,2048]{1,0:T(8,128)(2,1)S(1)}, bf16[192,2048]{1,0:T(8,128)(2,1)S(1)}, u32[]{:S(2)}, u32[]{:S(2)}) collective-permute-start(bf16[192,2048]{1,0:T(8,128)(2,1)S(1)} %get-tuple-element.120), channel_id=1, source_target_pairs={{0,1},{1,0},{2,3},{3,2},{4,5},{5,4},{6,7},{7,6},{8,9},{9,8},{10,11... | collective-permute-start | bytes 2359304 | tf_op jit(solution)/shard_map/ppermute | solution.py:1143
  307.4 19.4 %collective-permute-start.43 = (bf16[192,2048]{1,0:T(8,128)(2,1)S(1)}, bf16[192,2048]{1,0:T(8,128)(2,1)}, u32[]{:S(2)}, u32[]{:S(2)}) collective-permute-start(bf16[192,2048]{1,0:T(8,128)(2,1)S(1)} %get-tuple-element.121), channel_id=1, source_target_pairs={{0,16},{16,0},{1,17},{17,1},{2,18},{18,2},{3,19},{19,3},{4,20},{20... | collective-permute-start | bytes 2359304 | tf_op jit(solution)/shard_map/ppermute | solution.py:1143
  326.8 173.8 %reduce-scatter.5.cloned.1.call-start = ((), (), s32[]{:S(2)}) async-start(), calls=%async_computation.13 | async-start | bytes 3932160 | tf_op jit(solution)/shard_map/reduce_scatter | solution.py:1226
  345.5 18.6 %collective-permute-start.47 = (bf16[192,2176]{1,0:T(8,128)(2,1)S(1)}, bf16[192,2176]{1,0:T(8,128)(2,1)}, u32[]{:S(2)}, u32[]{:S(2)}) collective-permute-start(bf16[192,2176]{1,0:T(8,128)(2,1)S(1)} %get-tuple-element.130.refs_9_), channel_id=1, source_target_pairs={{0,1},{1,0},{2,3},{3,2},{4,5},{5,4},{6,7},{7,6},{8,9},{9,8},{10,11... | collective-permute-start | bytes 2506760 | tf_op jit(solution)/shard_map/ppermute | solution.py:1143
  346.9 18.7 %collective-permute-start.46 = (bf16[192,2176]{1,0:T(8,128)(2,1)S(1)}, bf16[192,2176]{1,0:T(8,128)(2,1)}, u32[]{:S(2)}, u32[]{:S(2)}) collective-permute-start(bf16[192,2176]{1,0:T(8,128)(2,1)S(1)} %get-tuple-element.130.refs_9_), channel_id=1, source_target_pairs={{0,16},{16,0},{1,17},{17,1},{2,18},{18,2},{3,19},{19,3},{4,20},{20... | collective-permute-start | bytes 2506760 | tf_op jit(solution)/shard_map/ppermute | solution.py:1143
  368.8 16.0 %collective-permute-start.55 = (bf16[192,2176]{1,0:T(8,128)(2,1)S(1)}, bf16[192,2176]{1,0:T(8,128)(2,1)S(1)}, u32[]{:S(2)}, u32[]{:S(2)}) collective-permute-start(bf16[192,2176]{1,0:T(8,128)(2,1)S(1)} %copy-done.53), channel_id=1, source_target_pairs={{0,8},{8,0},{1,9},{9,1},{2,10},{10,2},{3,11},{11,3},{4,12},{12,4},... | collective-permute-start | bytes 2506760 | tf_op jit(solution)/shard_map/ppermute | solution.py:1143
  368.9 16.6 %collective-permute-start.57 = (bf16[192,2176]{1,0:T(8,128)(2,1)}, bf16[192,2176]{1,0:T(8,128)(2,1)S(1)}, u32[]{:S(2)}, u32[]{:S(2)}) collective-permute-start(bf16[192,2176]{1,0:T(8,128)(2,1)} %collective-permute-done.47.refs_1_.refs_0_.refs_11_), channel_id=1, source_target_pairs={{0,8},{8,0},{1,9},{9,1},{2,10},{10,2},{3,11},{11,3},{4,12},{12,4},... | collective-permute-start | bytes 2506760 | tf_op jit(solution)/shard_map/ppermute | solution.py:1143
  384.9 31.9 %collective-permute-start.51 = (bf16[192,2048]{1,0:T(8,128)(2,1)}, bf16[192,2048]{1,0:T(8,128)(2,1)S(1)}, u32[]{:S(2)}, u32[]{:S(2)}) collective-permute-start(bf16[192,2048]{1,0:T(8,128)(2,1)} %get-tuple-element.136), channel_id=1, source_target_pairs={{0,1},{1,0},{2,3},{3,2},{4,5},{5,4},{6,7},{7,6},{8,9},{9,8},{10,11... | collective-permute-start | bytes 2359304 | tf_op jit(solution)/shard_map/ppermute | solution.py:1143
  385.4 31.3 %collective-permute-start.52 = (bf16[192,2048]{1,0:T(8,128)(2,1)}, bf16[192,2048]{1,0:T(8,128)(2,1)S(1)}, u32[]{:S(2)}, u32[]{:S(2)}) collective-permute-start(bf16[192,2048]{1,0:T(8,128)(2,1)} %get-tuple-element.137), channel_id=1, source_target_pairs={{0,16},{16,0},{1,17},{17,1},{2,18},{18,2},{3,19},{19,3},{4,20},{20... | collective-permute-start | bytes 2359304 | tf_op jit(solution)/shard_map/ppermute | solution.py:1143
  432.1 20.6 %all-to-all-start.3 = ((bf16[8,64,1152]{2,1,0:T(8,128)(2,1)}), bf16[8,64,1152]{2,1,0:T(8,128)(2,1)}, u32[]{:S(2)}, u32[]{:S(2)}) async-start(bf16[8,64,1152]{2,1,0:T(8,128)(2,1)} %hold.4), calls=%async_computation.6 | async-start | bytes 2359296 | tf_op jit(solution)/shard_map/all_to_all | solution.py:1209
  436.4 89.9 %reduce-scatter.11.cloned.1.call-start = ((), (), s32[]{:S(2)}) async-start(), calls=%async_computation.16 | async-start | bytes 1392640 | tf_op jit(solution)/shard_map/reduce_scatter | solution.py:1226
  443.1 26.5 %collective-permute-start.61 = (bf16[192,2048]{1,0:T(8,128)(2,1)}, bf16[192,2048]{1,0:T(8,128)(2,1)}, u32[]{:S(2)}, u32[]{:S(2)}) collective-permute-start(bf16[192,2048]{1,0:T(8,128)(2,1)} %get-tuple-element.153), channel_id=1, source_target_pairs={{0,1},{1,0},{2,3},{3,2},{4,5},{5,4},{6,7},{7,6},{8,9},{9,8},{10,11... | collective-permute-start | bytes 2359304 | tf_op jit(solution)/shard_map/ppermute | solution.py:1143
  445.0 24.6 %collective-permute-start.62 = (bf16[192,2048]{1,0:T(8,128)(2,1)}, bf16[192,2048]{1,0:T(8,128)(2,1)}, u32[]{:S(2)}, u32[]{:S(2)}) collective-permute-start(bf16[192,2048]{1,0:T(8,128)(2,1)} %get-tuple-element.154), channel_id=1, source_target_pairs={{0,16},{16,0},{1,17},{17,1},{2,18},{18,2},{3,19},{19,3},{4,20},{20... | collective-permute-start | bytes 2359304 | tf_op jit(solution)/shard_map/ppermute | solution.py:1143
  455.0 45.6 %all-to-all-start.4 = ((bf16[8,64,1024]{2,1,0:T(8,128)(2,1)}), bf16[8,64,1024]{2,1,0:T(8,128)(2,1)}, u32[]{:S(2)}, u32[]{:S(2)}) async-start(bf16[8,64,1024]{2,1,0:T(8,128)(2,1)} %hold.5), calls=%async_computation.7 | async-start | bytes 2097152 | tf_op jit(solution)/shard_map/all_to_all | solution.py:1209
  459.5 29.6 %collective-permute-start.53 = (bf16[96,2048]{1,0:T(8,128)(2,1)}, bf16[96,2048]{1,0:T(8,128)(2,1)S(1)}, u32[]{:S(2)}, u32[]{:S(2)}) collective-permute-start(bf16[96,2048]{1,0:T(8,128)(2,1)} %copy-done.55), channel_id=1, source_target_pairs={{0,16},{16,0},{1,17},{17,1},{2,18},{18,2},{3,19},{19,3},{4,20},{20... | collective-permute-start | bytes 1179656 | tf_op jit(solution)/shard_map/ppermute | solution.py:1143
  461.6 27.6 %collective-permute-start.54 = (bf16[96,2048]{1,0:T(8,128)(2,1)S(1)}, bf16[96,2048]{1,0:T(8,128)(2,1)S(1)}, u32[]{:S(2)}, u32[]{:S(2)}) collective-permute-start(bf16[96,2048]{1,0:T(8,128)(2,1)S(1)} %get-tuple-element.140), channel_id=1, source_target_pairs={{0,1},{1,0},{2,3},{3,2},{4,5},{5,4},{6,7},{7,6},{8,9},{9,8},{10,11... | collective-permute-start | bytes 1179656 | tf_op jit(solution)/shard_map/ppermute | solution.py:1143
  472.5 24.6 %collective-permute-start.63 = (bf16[96,2048]{1,0:T(8,128)(2,1)S(1)}, bf16[96,2048]{1,0:T(8,128)(2,1)S(1)}, u32[]{:S(2)}, u32[]{:S(2)}) collective-permute-start(bf16[96,2048]{1,0:T(8,128)(2,1)S(1)} %get-tuple-element.156), channel_id=1, source_target_pairs={{0,16},{16,0},{1,17},{17,1},{2,18},{18,2},{3,19},{19,3},{4,20},{20... | collective-permute-start | bytes 1179656 | tf_op jit(solution)/shard_map/ppermute | solution.py:1143
  474.0 23.2 %collective-permute-start.64 = (bf16[96,2048]{1,0:T(8,128)(2,1)S(1)}, bf16[96,2048]{1,0:T(8,128)(2,1)S(1)}, u32[]{:S(2)}, u32[]{:S(2)}) collective-permute-start(bf16[96,2048]{1,0:T(8,128)(2,1)S(1)} %get-tuple-element.157), channel_id=1, source_target_pairs={{0,1},{1,0},{2,3},{3,2},{4,5},{5,4},{6,7},{7,6},{8,9},{9,8},{10,11... | collective-permute-start | bytes 1179656 | tf_op jit(solution)/shard_map/ppermute | solution.py:1143
  (115 other events, 962.4 us)
Sparse Core Ops, SparseCore 0:
  9.6 29.2 all-gather.3
  84.5 102.4 all-gather.5
  188.6 78.3 all-gather.7
  269.1 85.7 reduce-scatter.8
  357.1 77.2 reduce-scatter.6
  436.7 60.2 reduce-scatter.4
  499.4 26.8 reduce-scatter.10
